TPU v7x, 256 devices: a whole 4x4x8 slice. The times are simulated.
256 devices in a mesh: section: 4 (over x_hi, core), seq: 64 (over y, x_lo, z).
Axes of the slice: x: 4 (x_hi: 2, x_lo: 2; x = x_hi * 2 + x_lo), y: 4, z: 8, core: 2. Of those that a mesh axis runs over, the one named last changes fastest.
Arguments:
- hidden: bfloat16 [32768, 4096], P(('seq', 'section')), may hold values from -6 to 6
- norm_gain: float32 [4096], replicated, may hold values from 0.1 to 1.9
- w_query: bfloat16 [4096, 4096], P('seq', 'section'), may hold values from -0.09375 to 0.09375
- w_keyval: bfloat16 [2, 896, 4096], P(None, None, 'section'), may hold values from -120 to 120
- nbr_states: bfloat16 [512, 256, 896], P('seq'), may hold values from -24 to 24
- nbr_lens: int32 [512, 2], replicated, may hold values from 32 to 128
- segment_ids: int32 [32768], replicated, may hold values from 0 to 63, never falling along the last dimension, each value on 1 to 16384 neighbouring positions
Outputs:
- context: bfloat16 [32768, 4096], P('seq', 'section')
All inputs are finite; a program needn't handle non-finite values.
Results may differ from a plain program's by a relative error of at most 0.017.
The roundings to bfloat16 on the way count: a program that leaves them out, or rounds other values in their place, can miss the bound.
Values may be sent and summed in bfloat16 or wider, within the bound.
No kernel may reach another device: no remote copies, remote signals or barrier semaphores. Data moves between devices by JAX's collectives and lax.ppermute only.
A program may use at most 128 MiB of HBM per device.

v0:
```python
import functools

import jax
import jax.numpy as jnp
from jax import lax
from jax.experimental import pallas as pl
from jax.experimental.pallas import tpu as pltpu
from jax.sharding import Mesh, PartitionSpec as P

HEAD_DIM = 128
SPAN = 64
NBR_LEN = 128
SIZES = {"xh": 2, "core": 2, "y": 4, "xl": 2, "z": 8}
PLANE = ("core", "y", "xl", "z")
VMEM = pl.BlockSpec(memory_space=pltpu.VMEM)
SMEM = pl.BlockSpec(memory_space=pltpu.SMEM)
MIB = 1 << 20


def params(mib):
    return pltpu.CompilerParams(vmem_limit_bytes=mib * MIB)


def cost(flops, moved):
    return pl.CostEstimate(flops=flops // 100, bytes_accessed=moved // 100, transcendentals=0)


def moved(move, y, xl, z):
    by, how = move
    if how == "z":
        return y, xl, (z + by) % 8
    return (y + by) % 4, xl ^ how, z


def send(x, first, second):
    pairs = []
    for core, move in enumerate((first, second)):
        for y in range(4):
            for xl in range(2):
                for z in range(8):
                    y2, xl2, z2 = moved(move, y, xl, z)
                    pairs.append(
                        (((core * 4 + y) * 2 + xl) * 8 + z, ((core * 4 + y2) * 2 + xl2) * 8 + z2)
                    )
    return lax.ppermute(x, PLANE, pairs)


def hop(x, axis):
    return lax.ppermute(x, axis, [(0, 1), (1, 0)])


OUTER_Z = (0, -1, 1, -2, 2, -3, 3, -4)
OUTER_W = ((0, 0), (-1, 0), (1, 0), (0, 1), (2, 0), (-1, 1), (1, 1), (2, 1))


def outer_slots(which):
    y, xl, z = lax.axis_index("y"), lax.axis_index("xl"), lax.axis_index("z")
    out = []
    for i in which:
        dz, (dy, flip) = OUTER_Z[i], OUTER_W[i]
        other = jnp.where(xl == flip, 0, 1)
        along_w = lax.rem(y + dy + 4, 4) * 2 + other
        out.append(jnp.where(lax.axis_index("core") == 1, lax.rem(z + dz + 8, 8), along_w))
    return out


def stack_kernel(orders, *refs):
    out, rows = refs[-1], refs[0].shape[0]
    for core, order in enumerate(orders):

        @pl.when(lax.axis_index("core") == core)
        def _(order=order):
            for i, which in enumerate(order):
                out[i * rows : (i + 1) * rows, :] = refs[which][...]


def stacked(parts, orders):
    rows, columns = parts[0].shape
    return pl.pallas_call(
        functools.partial(stack_kernel, orders),
        out_shape=jax.ShapeDtypeStruct((4 * rows, columns), parts[0].dtype),
        in_specs=[VMEM] * len(parts),
        out_specs=VMEM,
        compiler_params=params(8),
        cost_estimate=cost(0, 16 * rows * columns),
        name="stack",
    )(*parts)


def norm_kernel(hidden_ref, gain_ref, out_ref):
    values = hidden_ref[...].astype(jnp.float32)
    factor = lax.rsqrt(jnp.mean(values * values, axis=-1, keepdims=True) + 1e-06)
    out_ref[...] = (values * factor * gain_ref[...]).astype(jnp.bfloat16)


def normalize(hidden, gain):
    rows, width = hidden.shape
    return pl.pallas_call(
        norm_kernel,
        out_shape=jax.ShapeDtypeStruct((rows, width), jnp.bfloat16),
        in_specs=[VMEM, VMEM],
        out_specs=VMEM,
        compiler_params=params(8),
        cost_estimate=cost(6 * rows * width, 4 * rows * width),
        name="norm",
    )(hidden, gain)


def rows_kernel(own_ref, near_ref, far_ref, far_near_ref, out):
    xh, core = lax.axis_index("xh"), lax.axis_index("core")
    y, xl, z = lax.axis_index("y"), lax.axis_index("xl"), lax.axis_index("z")
    slots = [xh * 2 + core, xh * 2 + 1 - core, 2 - 2 * xh + core, 3 - 2 * xh - core]
    refs = [own_ref, near_ref, far_ref, far_near_ref]
    rows = own_ref.shape[0]
    part = 32
    start = lax.rem(z + 6, 8) // 2

    for slot, ref in zip(slots, refs, strict=True):

        def one(i, _, slot=slot, ref=ref):
            here = pl.ds(pl.multiple_of(i * part, part), part)
            at = pl.ds(pl.multiple_of(slot * rows + i * part, part), part)

            def tile(lane):
                return ref[here, pl.ds(pl.multiple_of(lane, 128), 128)]

            @pl.when((core == 0) & (lax.rem(z, 2) == 0))
            def _():
                for w in range(8):
                    for k in range(4):
                        to = w * 512 + k * 128
                        out[at, to : to + 128] = tile(w * 512 + lax.rem(start + k, 4) * 128)

            @pl.when((core == 0) & (lax.rem(z, 2) == 1))
            def _():
                for w in range(8):
                    for k in range(4):
                        one = tile(w * 512 + lax.rem(start + k, 4) * 128)[:, 64:]
                        two = tile(w * 512 + lax.rem(start + k + 1, 4) * 128)[:, :64]
                        to = w * 512 + k * 128
                        out[at, to : to + 128] = jnp.concatenate([one, two], axis=1)

            @pl.when(core == 1)
            def _():
                for k in range(4):
                    side = xl if k < 2 else 1 - xl
                    base = [(lax.rem(y + 2 * (k % 2) + j, 4) * 2 + side) * 512 for j in range(2)]
                    for z_at in range(8):
                        half = slice(64 * (z_at % 2), 64 * (z_at % 2) + 64)
                        one, two = [tile(b + z_at // 2 * 128)[:, half] for b in base]
                        to = z_at * 512 + k * 128
                        out[at, to : to + 128] = jnp.concatenate([one, two], axis=1)

        lax.fori_loop(0, rows // part, one, None)


def gather_rows(parts):
    rows, width = parts[0].shape
    return pl.pallas_call(
        rows_kernel,
        out_shape=jax.ShapeDtypeStruct((4 * rows, width), parts[0].dtype),
        in_specs=[VMEM] * 4,
        out_specs=VMEM,
        compiler_params=params(16),
        cost_estimate=cost(0, 16 * rows * width),
        name="rows",
    )(*parts)


def project_kernel(states_ref, w_ref, out_ref):
    def one(i, _):
        out_ref[i] = jnp.dot(
            states_ref[i], w_ref[0], preferred_element_type=jnp.float32
        ).astype(jnp.bfloat16)

    lax.fori_loop(0, out_ref.shape[0], one, None)


def project(states, w, which, half):
    spans, keys, depth = states.shape
    columns = w.shape[2] // 2
    whole = lambda i: (0, 0, 0)
    return pl.pallas_call(
        project_kernel,
        grid=(1,),
        out_shape=jax.ShapeDtypeStruct((spans, keys, columns), jnp.bfloat16),
        in_specs=[
            pl.BlockSpec(states.shape, whole, pipeline_mode=pl.Buffered(1)),
            pl.BlockSpec((1, depth, columns), lambda i: (which, 0, half), pipeline_mode=pl.Buffered(1)),
        ],
        out_specs=pl.BlockSpec((spans, keys, columns), whole, pipeline_mode=pl.Buffered(1)),
        compiler_params=params(16),
        cost_estimate=cost(2 * spans * keys * depth * columns, 6 * MIB),
        name="project",
    )(states, w)


def project_prev_kernel(mine_ref, other_ref, w_ref, out_ref):
    core, rows = lax.axis_index("core"), mine_ref.shape[0]
    for which in range(2):
        for slot, ref in ((core, mine_ref), (1 - core, other_ref)):
            out_ref[which, pl.ds(pl.multiple_of(slot * rows, rows), rows), :] = jnp.dot(
                ref[...], w_ref[which], preferred_element_type=jnp.float32
            ).astype(jnp.bfloat16)


def project_prev(mine, other, w):
    rows, depth = mine.shape
    columns = w.shape[2]
    return pl.pallas_call(
        project_prev_kernel,
        out_shape=jax.ShapeDtypeStruct((2, 2 * rows, columns), jnp.bfloat16),
        in_specs=[VMEM] * 3,
        out_specs=VMEM,
        compiler_params=params(12),
        cost_estimate=cost(8 * rows * depth * columns, 6 * MIB),
        name="project_prev",
    )(mine, other, w)


def products(n_ref, refs, places):
    total = None
    for ref, place in zip(refs, places, strict=True):
        lanes = pl.ds(pl.multiple_of(place, 128), ref.shape[0])
        term = jnp.dot(n_ref[:, lanes], ref[...], preferred_element_type=jnp.float32)
        total = term if total is None else total + term
    return total


def partial_product(n, terms, before=None):
    pieces = [piece for _, _, some in terms for piece in some]
    rows, columns = n.shape[0], pieces[0].shape[1]
    depth = sum(p.shape[0] for p in pieces)
    extra = [] if before is None else [before]

    def body(n_ref, *refs):
        places = [slot * 512 + start for start, which, _ in terms for slot in outer_slots(which)]
        total = products(n_ref, refs[: len(pieces)], places)
        if extra:
            total = total + refs[len(pieces)][...]
        refs[-1][...] = total

    return pl.pallas_call(
        body,
        out_shape=jax.ShapeDtypeStruct((rows, columns), jnp.float32),
        in_specs=[VMEM] * (1 + len(pieces) + len(extra)),
        out_specs=VMEM,
        compiler_params=params(20),
        cost_estimate=cost(2 * rows * depth * columns, 2 * depth * (rows + columns)),
        name="partial",
    )(n, *pieces, *extra)


def attend(lens, segments, total, n, pieces, prev, keys, values):
    rows, columns = total.shape
    blocks = keys[0].shape[0] + 1
    heads = columns // HEAD_DIM // 2
    half = columns // 2

    def body(lens_ref, seg_ref, total_ref, n_ref, *refs):
        piece_refs, prev_ref, k_refs, v_refs = refs[:4], refs[4], refs[5:7], refs[7:9]
        out_ref, q_scr, c_scr, s_scr, w_scr = refs[9:]
        seq = (lax.axis_index("y") * 2 + lax.axis_index("xl")) * 8 + lax.axis_index("z")
        (slot,) = outer_slots([7])
        places = [slot * 512 + i * 128 for i in range(4)]
        acc = total_ref[...] + products(n_ref, piece_refs, places)
        acc = acc * HEAD_DIM ** (-0.5)
        acc = jnp.concatenate([acc, jnp.zeros((SPAN, columns), jnp.float32)], axis=0)
        q_scr[...] = pltpu.roll(acc, 1, 0).astype(jnp.bfloat16)
        lane = lax.broadcasted_iota(jnp.int32, (1, 128), 1)
        wide = lax.broadcasted_iota(jnp.int32, (1, 2 * NBR_LEN), 1)
        row = lax.broadcasted_iota(jnp.int32, (SPAN, HEAD_DIM), 0)
        usable, live = [], []
        for b in range(blocks):
            span = jnp.maximum(seq * (blocks - 1) + b - 1, 0)
            usable.append(
                wide < jnp.where(wide < NBR_LEN, lens_ref[0, span], lens_ref[1, span] + NBR_LEN)
            )
            line = seg_ref[pl.ds(span // 2, 1), :]
            if b % 2:
                same = (line == line[:, 63:64]) & (lane >= 63) & (lane < 127)
                count = jnp.sum(same.astype(jnp.int32), axis=1, keepdims=True)
            else:
                after = seg_ref[pl.ds(jnp.minimum(span // 2 + 1, seg_ref.shape[0] - 1), 1), :]
                same = (after == line[:, 127:128]) & (lane < 63)
                count = jnp.sum(same.astype(jnp.int32), axis=1, keepdims=True) + 1
            if b == 0:
                count = jnp.where(seq == 0, 0, count)
            live.append(row < count)
        for part in range(2):
            for h in range(heads):
                at = slice(h * HEAD_DIM, (h + 1) * HEAD_DIM)
                to = slice(part * half + h * HEAD_DIM, part * half + (h + 1) * HEAD_DIM)
                for b in range(blocks):
                    scores = lax.dot_general(
                        q_scr[b * SPAN : (b + 1) * SPAN, to],
                        k_refs[part][b - 1, :, at] if b else prev_ref[0, :, to],
                        (((1,), (1,)), ((), ())),
                        preferred_element_type=jnp.float32,
                    )
                    s_scr[h, b * SPAN : (b + 1) * SPAN, :] = jnp.where(usable[b], scores, jnp.float32(-1e30))
            for h in range(heads):
                for c in range(blocks // 3):
                    r = slice(c * 3 * SPAN, (c + 1) * 3 * SPAN)
                    scores = s_scr[h, r, :]
                    weights = jnp.exp(scores - jnp.max(scores, axis=-1, keepdims=True))
                    scale = 1.0 / jnp.sum(weights, axis=-1, keepdims=True)
                    w_scr[h, r, :] = (weights * scale).astype(jnp.bfloat16)
            for h in range(heads):
                at = slice(h * HEAD_DIM, (h + 1) * HEAD_DIM)
                to = slice(part * half + h * HEAD_DIM, part * half + (h + 1) * HEAD_DIM)
                for b in range(blocks):
                    mixed = jnp.dot(
                        w_scr[h, b * SPAN : (b + 1) * SPAN, :],
                        v_refs[part][b - 1, :, at] if b else prev_ref[1, :, to],
                        preferred_element_type=jnp.float32,
                    )
                    c_scr[b * SPAN : (b + 1) * SPAN, to] = jnp.where(live[b], mixed, 0.0)
        moved = pltpu.roll(c_scr[...], blocks * SPAN - 1, 0)
        out_ref[...] = moved[:rows].astype(jnp.bfloat16)

    return pl.pallas_call(
        body,
        out_shape=jax.ShapeDtypeStruct((rows, columns), jnp.bfloat16),
        in_specs=[SMEM] + [VMEM] * 12,
        out_specs=VMEM,
        scratch_shapes=[
            pltpu.VMEM((blocks * SPAN, columns), jnp.bfloat16),
            pltpu.VMEM((blocks * SPAN, columns), jnp.float32),
            pltpu.VMEM((heads, blocks * SPAN, 2 * NBR_LEN), jnp.float32),
            pltpu.VMEM((heads, blocks * SPAN, 2 * NBR_LEN), jnp.bfloat16),
        ],
        compiler_params=params(28),
        cost_estimate=cost(6 * MIB * 1000, 16 * MIB),
        name="attend",
    )(lens, segments, total, n, *pieces, prev, *keys, *values)


def after(value, *others):
    return lax.optimization_barrier((value, *others))[0]


def local(hidden, norm_gain, w_query, w_keyval, nbr_states, nbr_lens, segment_ids):
    core = lax.axis_index("core")

    def pick(zero, one):
        return jnp.where(core == 0, zero, one)

    def outer_first(column):
        return [send(column, (1, 0), (1, "z")), send(column, (-1, 0), (-1, "z"))]

    def outer_second(column, one, two, *first):
        one, two = after(one, *first), after(two, *first)
        return [send(pick(column, one), (0, 1), (1, "z")), send(two, (-1, 0), (-1, "z"))]

    def outer_third(three, four, *first):
        three, four = after(three, *first), after(four, *first)
        return [send(three, (1, 0), (1, "z")), send(pick(three, four), (-1, 0), (-1, "z"))]

    def outer_last(five, six, *first):
        r = five.shape[0] // 2
        five, six = after(five, *first), after(six, *first)
        return [send(five[:r], (1, 0), (1, "z")), send(six[r:], (-1, 0), (-1, "z"))]

    def projected(which, part, *first):
        return project(after(nbr_states, *first), w_keyval, which, part)

    round_one = [
        send(w_query, (1, "z"), (0, 1)),
        send(w_query, (-1, "z"), (1, 0)),
        send(w_query, (2, "z"), (-1, 0)),
        send(w_query, (-2, "z"), (2, 0)),
    ]
    normed = normalize(hidden, norm_gain[None])
    near = hop(after(normed, *round_one), "core")
    far = hop(normed, "xh")
    column_a = stacked([w_query, *round_one], ((3, 1, 0, 2), (0, 3, 4, 2)))
    head = after(pick(round_one[3], round_one[0]), normed)
    round_two = [
        send(head, (-1, "z"), (-1, 0)),
        send(head, (-2, "z"), (2, 0)),
        send(pick(round_one[2], round_one[0]), (1, "z"), (1, 0)),
    ]
    a = [column_a, *outer_first(column_a)]
    keys_a = projected(0, 0, column_a)
    column_b = stacked([after(head, keys_a), *round_two], ((0, 1, 2, 3), (0, 1, 2, 3)))
    half = nbr_states.shape[1] // 2
    prev = lax.dynamic_slice_in_dim(nbr_states[-1], core * half, half, 0)
    prev = lax.ppermute(after(prev, column_b), ("y", "xl", "z"), [(i, i + 1) for i in range(63)])
    b = [column_b, *outer_first(after(column_b, near))]
    a += outer_second(*a)
    values_a = projected(1, 0, *a[1:3])
    b += outer_second(*b, values_a)
    keys_b = projected(0, 1, *b[1:3])
    far_near = hop(after(far, *a[3:5]), "core")
    a += outer_third(*a[3:5], keys_b)
    values_b = projected(1, 1, *a[3:5])
    prev_near = hop(after(prev, values_b), "core")
    b += outer_third(*b[3:5], values_b, prev)
    whole = gather_rows([after(normed, values_b), near, far, far_near])
    total = partial_product(whole, [(0, [0, 1, 2], a[:3])])
    a += outer_last(*a[5:7])
    prev = project_prev(after(prev, total), prev_near, w_keyval)
    total = partial_product(
        after(whole, *a[5:7]), [(256, [0, 1, 2], b[:3]), (0, [3, 4], a[3:5])], total
    )
    b += outer_last(*b[5:7], total)
    total = partial_product(
        after(whole, *b[5:7]),
        [(256, [3, 4], b[3:5]), (0, [5, 6], a[5:7]), (256, [5, 6], b[5:7])],
        total,
    )
    return attend(
        nbr_lens.T,
        segment_ids.reshape(-1, 128),
        total,
        whole,
        [*a[7:], *b[7:]],
        prev,
        [keys_a, keys_b],
        [values_a, values_b],
    )


def solution(mesh):
    fine = Mesh(mesh.devices.reshape(tuple(SIZES.values())), tuple(SIZES))
    section, seq = ("xh", "core"), ("y", "xl", "z")
    in_specs = (
        P(seq + section, None),
        P(),
        P(seq, section),
        P(None, None, section),
        P(seq, None, None),
        P(),
        P(),
    )
    out_specs = P(seq, section)
    return jax.shard_map(local, mesh=fine, in_specs=in_specs, out_specs=out_specs, check_vma=False)
```

profile of v0, /device:TPU:32, one launch (start us, length us, event | category | flops | bytes accessed | tf_op | source)
XLA Modules:
  0.0 111.4 jit_solution(16508287897007603525)
XLA Ops:
  0.0 1.9 %collective-permute-start = (bf16[64,1024]{1,0:T(8,128)(2,1)}, bf16[64,1024]{1,0:T(8,128)(2,1)S(1)}, u32[]{:S(2)}, u32[]{:S(2)}) collective-permute-start(bf16[64,1024]{1,0:T(8,128)(2,1)} %refs_0_.1), channel_id=1, source_target_pairs={{0,1},{1,2},{2,3},{3,4},{4,5},{5,6},{6,7},{7,0},{8,9},{9,10},{10,1... | collective-permute-start | bytes 393224 | tf_op jit(solution)/shard_map/ppermute | solution.py:45
  1.9 4.5 %collective-permute-start.2 = (bf16[64,1024]{1,0:T(8,128)(2,1)}, bf16[64,1024]{1,0:T(8,128)(2,1)S(1)}, u32[]{:S(2)}, u32[]{:S(2)}) collective-permute-start(bf16[64,1024]{1,0:T(8,128)(2,1)} %refs_0_.1), channel_id=1, source_target_pairs={{0,2},{1,3},{2,4},{3,5},{4,6},{5,7},{6,0},{7,1},{8,10},{9,11},{10,... | collective-permute-start | bytes 393224 | tf_op jit(solution)/shard_map/ppermute | solution.py:45
  16.2 1.9 %collective-permute-start.12 = (bf16[64,1024]{1,0:T(8,128)(2,1)S(1)}, bf16[64,1024]{1,0:T(8,128)(2,1)S(1)}, u32[]{:S(2)}, u32[]{:S(2)}) collective-permute-start(bf16[64,1024]{1,0:T(8,128)(2,1)S(1)} %get-tuple-element.34.refs_0_), channel_id=1, source_target_pairs={{0,6},{1,7},{2,0},{3,1},{4,2},{5,3},{6,4},{7,5},{8,14},{9,15},{10,... | collective-permute-start | bytes 393224 | tf_op jit(solution)/shard_map/ppermute | solution.py:45
  23.8 3.0 %collective-permute-start.9 = (bf16[128,4096]{1,0:T(8,128)(2,1)}, bf16[128,4096]{1,0:T(8,128)(2,1)}, u32[]{:S(2)}, u32[]{:S(2)}) collective-permute-start(bf16[128,4096]{1,0:T(8,128)(2,1)} %norm.1.own_ref), channel_id=1, source_target_pairs={{0,128},{128,0},{1,129},{129,1},{2,130},{130,2},{3,131},{131,3},{4... | collective-permute-start | bytes 3145736 | tf_op jit(solution)/shard_map/ppermute | solution.py:49
  26.8 2.0 %copy-done = bf16[2,896,1024]{2,1,0:T(8,128)(2,1)S(1)} copy-done((bf16[2,896,1024]{2,1,0:T(8,128)(2,1)S(1)}, bf16[2,896,1024]{2,1,0:T(8,128)(2,1)}, u32[]{:S(2)}) %copy-start) | copy-done | bytes 3670040
  28.8 2.0 %copy-done.3 = bf16[8,256,896]{2,1,0:T(8,128)(2,1)S(1)} copy-done((bf16[8,256,896]{2,1,0:T(8,128)(2,1)S(1)}, bf16[8,256,896]{2,1,0:T(8,128)(2,1)}, u32[]{:S(2)}) %copy-start.3) | copy-done | bytes 3670040
  30.9 3.6 %project.5.refs_5_ = bf16[8,256,512]{2,1,0:T(8,128)(2,1)S(1)} custom-call(bf16[8,256,896]{2,1,0:T(8,128)(2,1)S(1)} %copy-done.3, bf16[2,896,1024]{2,1,0:T(8,128)(2,1)S(1)} %copy-done), custom_call_target="tpu_custom_call" | custom-call | flops 18790480 | bytes 62914 | tf_op jit(solution)/shard_map/project/pallas_call | solution.py:183
  34.5 1.7 %collective-permute-start.18 = (bf16[256,1024]{1,0:T(8,128)(2,1)S(1)}, bf16[256,1024]{1,0:T(8,128)(2,1)}, u32[]{:S(2)}, u32[]{:S(2)}) collective-permute-start(bf16[256,1024]{1,0:T(8,128)(2,1)S(1)} %stack.3.refs_0_), channel_id=1, source_target_pairs={{0,48},{1,49},{2,50},{3,51},{4,52},{5,53},{6,54},{7,55},{8,56},{9,... | collective-permute-start | bytes 1572872 | tf_op jit(solution)/shard_map/ppermute | solution.py:45
  38.2 2.9 %collective-permute-start.7 = (bf16[256,1024]{1,0:T(8,128)(2,1)}, bf16[256,1024]{1,0:T(8,128)(2,1)}, u32[]{:S(2)}, u32[]{:S(2)}) collective-permute-start(bf16[256,1024]{1,0:T(8,128)(2,1)} %collective-permute-done.6.refs_2_), channel_id=1, source_target_pairs={{0,48},{1,49},{2,50},{3,51},{4,52},{5,53},{6,54},{7,55},{8,56},{9,... | collective-permute-start | bytes 1572872 | tf_op jit(solution)/shard_map/ppermute | solution.py:45
  41.1 3.6 %project.6.refs_7_ = bf16[8,256,512]{2,1,0:T(8,128)(2,1)S(1)} custom-call(bf16[8,256,896]{2,1,0:T(8,128)(2,1)S(1)} %copy-done.3, bf16[2,896,1024]{2,1,0:T(8,128)(2,1)S(1)} %copy-done), custom_call_target="tpu_custom_call" | custom-call | flops 18790480 | bytes 62914 | tf_op jit(solution)/shard_map/project/pallas_call | solution.py:183
  49.0 8.3 %collective-permute-done.5.refs_3_ = bf16[256,1024]{1,0:T(8,128)(2,1)} collective-permute-done((bf16[256,1024]{1,0:T(8,128)(2,1)}, bf16[256,1024]{1,0:T(8,128)(2,1)}, u32[]{:S(2)}, u32[]{:S(2)}) %collective-permute-start.5) | collective-permute-done | bytes 524320 | tf_op jit(solution)/shard_map/ppermute | solution.py:45
  57.3 5.5 %collective-permute-start.16 = (bf16[128,896]{1,0:T(8,128)(2,1)S(1)}, bf16[128,896]{1,0:T(8,128)(2,1)S(1)}, u32[]{:S(2)}, u32[]{:S(2)}) collective-permute-start(bf16[128,896]{1,0:T(8,128)(2,1)S(1)} %dynamic-slice_bitcast_fusion), channel_id=1, source_target_pairs={{0,1},{1,2},{2,3},{3,4},{4,5},{5,6},{6,7},{7,8},{8,9},{9,10},{10,1... | collective-permute-start | bytes 688136 | tf_op jit(solution)/shard_map/ppermute | solution.py:389
  63.0 2.0 %copy-done.1 = bf16[2,896,1024]{2,1,0:T(8,128)(2,1)S(1)} copy-done((bf16[2,896,1024]{2,1,0:T(8,128)(2,1)S(1)}, bf16[2,896,1024]{2,1,0:T(8,128)(2,1)}, u32[]{:S(2)}) %copy-start.1) | copy-done | bytes 3670040
  65.0 2.0 %copy-done.4 = bf16[8,256,896]{2,1,0:T(8,128)(2,1)S(1)} copy-done((bf16[8,256,896]{2,1,0:T(8,128)(2,1)S(1)}, bf16[8,256,896]{2,1,0:T(8,128)(2,1)}, u32[]{:S(2)}) %copy-start.4) | copy-done | bytes 3670040
  67.1 3.6 %project.4.refs_8_ = bf16[8,256,512]{2,1,0:T(8,128)(2,1)S(1)} custom-call(bf16[8,256,896]{2,1,0:T(8,128)(2,1)S(1)} %copy-done.4, bf16[2,896,1024]{2,1,0:T(8,128)(2,1)S(1)} %copy-done.1), custom_call_target="tpu_custom_call" | custom-call | flops 18790480 | bytes 62914 | tf_op jit(solution)/shard_map/project/pallas_call | solution.py:183
  70.6 3.6 %project.7.refs_6_ = bf16[8,256,512]{2,1,0:T(8,128)(2,1)S(1)} custom-call(bf16[8,256,896]{2,1,0:T(8,128)(2,1)S(1)} %copy-done.4, bf16[2,896,1024]{2,1,0:T(8,128)(2,1)S(1)} %copy-done.1), custom_call_target="tpu_custom_call" | custom-call | flops 18790480 | bytes 62914 | tf_op jit(solution)/shard_map/project/pallas_call | solution.py:183
  75.4 3.3 %collective-permute-start.22 = (bf16[256,1024]{1,0:T(8,128)(2,1)S(1)}, bf16[256,1024]{1,0:T(8,128)(2,1)S(1)}, u32[]{:S(2)}, u32[]{:S(2)}) collective-permute-start(bf16[256,1024]{1,0:T(8,128)(2,1)S(1)} %broadcast_select_fusion), channel_id=1, source_target_pairs={{0,48},{1,49},{2,50},{3,51},{4,52},{5,53},{6,54},{7,55},{8,56},{9,... | collective-permute-start | bytes 1572872 | tf_op jit(solution)/shard_map/ppermute | solution.py:45
  79.9 2.0 %collective-permute-start.17 = (bf16[256,1024]{1,0:T(8,128)(2,1)}, bf16[256,1024]{1,0:T(8,128)(2,1)S(1)}, u32[]{:S(2)}, u32[]{:S(2)}) collective-permute-start(bf16[256,1024]{1,0:T(8,128)(2,1)} %collective-permute-done.15.refs_0_), channel_id=1, source_target_pairs={{0,16},{1,17},{2,18},{3,19},{4,20},{5,21},{6,22},{7,23},{8,24},{9,... | collective-permute-start | bytes 1572872 | tf_op jit(solution)/shard_map/ppermute | solution.py:45
  81.9 5.4 %rows.1.n_ref = bf16[512,4096]{1,0:T(8,128)(2,1)S(1)} custom-call(bf16[128,4096]{1,0:T(8,128)(2,1)} %norm.1.own_ref, bf16[128,4096]{1,0:T(8,128)(2,1)} %collective-permute-done.8.near_ref, bf16[128,4096]{1,0:T(8,128)(2,1)} %collective-permute-done.9.far_ref, bf16[128,4096]{1,0:T(8,128)(2,1)S(1)} %collective-permute-done.10.far_near_ref), custom_call_target="tpu_custom_call" | custom-call | bytes 83886 | tf_op jit(solution)/shard_map/rows/pallas_call | solution.py:159
  87.4 2.1 %partial.3.refs_5_ = f32[512,1024]{1,0:T(8,128)S(1)} custom-call(bf16[512,4096]{1,0:T(8,128)(2,1)S(1)} %rows.1.n_ref, bf16[256,1024]{1,0:T(8,128)(2,1)S(1)} %stack.2.refs_0_, bf16[256,1024]{1,0:T(8,128)(2,1)S(1)} %copy-done.10, bf16[256,1024]{1,0:T(8,128)(2,1)} %collective-permute-done.6.refs_2_), custom_call_target="tpu_custom_call" | custom-call | flops 8053063 | bytes 23592 | tf_op jit(solution)/shard_map/partial/pallas_call | solution.py:243
  91.7 3.0 %partial.4.refs_6_ = f32[512,1024]{1,0:T(8,128)S(1)} custom-call(bf16[512,4096]{1,0:T(8,128)(2,1)S(1)} %rows.1.n_ref, bf16[256,1024]{1,0:T(8,128)(2,1)S(1)} %copy-done.8, bf16[256,1024]{1,0:T(8,128)(2,1)S(1)} %copy-done.12, bf16[256,1024]{1,0:T(8,128)(2,1)} %collective-permute-done.18.refs_2_, bf16[256,1024]{1,0:T(8,128)(2,1)} %collective-permute-done.5.refs_3_, ...), custom_call_target="tpu_custom_call" | custom-call | flops 13421772 | bytes 39321 | tf_op jit(solution)/shard_map/partial/pallas_call | solution.py:243
  94.8 2.6 %collective-permute-start.26 = (bf16[128,1024]{1,0:T(8,128)(2,1)S(1)}, bf16[128,1024]{1,0:T(8,128)(2,1)S(1)}, u32[]{:S(2)}, u32[]{:S(2)}) collective-permute-start(bf16[128,1024]{1,0:T(8,128)(2,1)S(1)} %slice.19), channel_id=1, source_target_pairs={{0,48},{1,49},{2,50},{3,51},{4,52},{5,53},{6,54},{7,55},{8,56},{9,... | collective-permute-start | bytes 786440 | tf_op jit(solution)/shard_map/ppermute | solution.py:45
  100.6 3.1 %partial.5.total_ref = f32[512,1024]{1,0:T(8,128)S(1)} custom-call(bf16[512,4096]{1,0:T(8,128)(2,1)S(1)} %rows.1.n_ref, bf16[256,1024]{1,0:T(8,128)(2,1)} %collective-permute-done.15.refs_0_, bf16[256,1024]{1,0:T(8,128)(2,1)} %collective-permute-done.19.refs_1_, bf16[256,1024]{1,0:T(8,128)(2,1)S(1)} %collective-permute-done.21.refs_2_, ...), custom_call_target="tpu_custom_call" | custom-call | flops 16106127 | bytes 47185 | tf_op jit(solution)/shard_map/partial/pallas_call | solution.py:243
  105.3 6.1 %attend.1 = bf16[512,1024]{1,0:T(8,128)(2,1)} custom-call(s32[2,512]{1,0:T(2,128)S(1)} %bitcast.7, s32[256,128]{1,0:T(8,128)S(1)} %bitcast.5, f32[512,1024]{1,0:T(8,128)S(1)} %partial.5.total_ref, bf16[512,4096]{1,0:T(8,128)(2,1)S(1)} %rows.1.n_ref, bf16[128,1024]{1,0:T(8,128)(2,1)S(1)} %collective-permute-done.23.refs_0_, ...), custom_call_target="tpu_custom_call" | custom-call | flops 62914560 | bytes 167772 | tf_op jit(solution)/shard_map/attend/pallas_call | solution.py:322
  (93 shorter events, 31.2 us)
Async XLA Ops:
  0.0 10.9 %collective-permute-start = (bf16[64,1024]{1,0:T(8,128)(2,1)}, bf16[64,1024]{1,0:T(8,128)(2,1)S(1)}, u32[]{:S(2)}, u32[]{:S(2)}) collective-permute-start(bf16[64,1024]{1,0:T(8,128)(2,1)} %refs_0_.1), channel_id=1, source_target_pairs={{0,1},{1,2},{2,3},{3,4},{4,5},{5,6},{6,7},{7,0},{8,9},{9,10},{10,1... | collective-permute-start | bytes 393224 | tf_op jit(solution)/shard_map/ppermute | solution.py:45
  1.9 9.0 %collective-permute-start.2 = (bf16[64,1024]{1,0:T(8,128)(2,1)}, bf16[64,1024]{1,0:T(8,128)(2,1)S(1)}, u32[]{:S(2)}, u32[]{:S(2)}) collective-permute-start(bf16[64,1024]{1,0:T(8,128)(2,1)} %refs_0_.1), channel_id=1, source_target_pairs={{0,2},{1,3},{2,4},{3,5},{4,6},{5,7},{6,0},{7,1},{8,10},{9,11},{10,... | collective-permute-start | bytes 393224 | tf_op jit(solution)/shard_map/ppermute | solution.py:45
  13.5 21.1 %collective-permute-start.8 = (bf16[128,4096]{1,0:T(8,128)(2,1)}, bf16[128,4096]{1,0:T(8,128)(2,1)}, u32[]{:S(2)}, u32[]{:S(2)}) collective-permute-start(bf16[128,4096]{1,0:T(8,128)(2,1)} %norm.1.own_ref), channel_id=1, source_target_pairs={{0,64},{64,0},{1,65},{65,1},{2,66},{66,2},{3,67},{67,3},{4,68},{68... | collective-permute-start | bytes 3145736 | tf_op jit(solution)/shard_map/ppermute | solution.py:49
  13.5 23.1 %collective-permute-start.4 = (bf16[256,1024]{1,0:T(8,128)(2,1)S(1)}, bf16[256,1024]{1,0:T(8,128)(2,1)S(1)}, u32[]{:S(2)}, u32[]{:S(2)}) collective-permute-start(bf16[256,1024]{1,0:T(8,128)(2,1)S(1)} %stack.2.refs_0_), channel_id=1, source_target_pairs={{0,16},{1,17},{2,18},{3,19},{4,20},{5,21},{6,22},{7,23},{8,24},{9,... | collective-permute-start | bytes 1572872 | tf_op jit(solution)/shard_map/ppermute | solution.py:45
  16.2 7.5 %collective-permute-start.12 = (bf16[64,1024]{1,0:T(8,128)(2,1)S(1)}, bf16[64,1024]{1,0:T(8,128)(2,1)S(1)}, u32[]{:S(2)}, u32[]{:S(2)}) collective-permute-start(bf16[64,1024]{1,0:T(8,128)(2,1)S(1)} %get-tuple-element.34.refs_0_), channel_id=1, source_target_pairs={{0,6},{1,7},{2,0},{3,1},{4,2},{5,3},{6,4},{7,5},{8,14},{9,15},{10,... | collective-permute-start | bytes 393224 | tf_op jit(solution)/shard_map/ppermute | solution.py:45
  18.2 16.3 %collective-permute-start.13 = (bf16[64,1024]{1,0:T(8,128)(2,1)S(1)}, bf16[64,1024]{1,0:T(8,128)(2,1)S(1)}, u32[]{:S(2)}, u32[]{:S(2)}) collective-permute-start(bf16[64,1024]{1,0:T(8,128)(2,1)S(1)} %get-tuple-element.51), channel_id=1, source_target_pairs={{0,1},{1,2},{2,3},{3,4},{4,5},{5,6},{6,7},{7,0},{8,9},{9,10},{10,1... | collective-permute-start | bytes 393224 | tf_op jit(solution)/shard_map/ppermute | solution.py:45
  20.7 17.5 %collective-permute-start.6 = (bf16[256,1024]{1,0:T(8,128)(2,1)S(1)}, bf16[256,1024]{1,0:T(8,128)(2,1)}, u32[]{:S(2)}, u32[]{:S(2)}) collective-permute-start(bf16[256,1024]{1,0:T(8,128)(2,1)S(1)} %stack.2.refs_0_), channel_id=1, source_target_pairs={{0,48},{1,49},{2,50},{3,51},{4,52},{5,53},{6,54},{7,55},{8,56},{9,... | collective-permute-start | bytes 1572872 | tf_op jit(solution)/shard_map/ppermute | solution.py:45
  23.8 39.1 %collective-permute-start.9 = (bf16[128,4096]{1,0:T(8,128)(2,1)}, bf16[128,4096]{1,0:T(8,128)(2,1)}, u32[]{:S(2)}, u32[]{:S(2)}) collective-permute-start(bf16[128,4096]{1,0:T(8,128)(2,1)} %norm.1.own_ref), channel_id=1, source_target_pairs={{0,128},{128,0},{1,129},{129,1},{2,130},{130,2},{3,131},{131,3},{4... | collective-permute-start | bytes 3145736 | tf_op jit(solution)/shard_map/ppermute | solution.py:49
  34.5 11.5 %collective-permute-start.18 = (bf16[256,1024]{1,0:T(8,128)(2,1)S(1)}, bf16[256,1024]{1,0:T(8,128)(2,1)}, u32[]{:S(2)}, u32[]{:S(2)}) collective-permute-start(bf16[256,1024]{1,0:T(8,128)(2,1)S(1)} %stack.3.refs_0_), channel_id=1, source_target_pairs={{0,48},{1,49},{2,50},{3,51},{4,52},{5,53},{6,54},{7,55},{8,56},{9,... | collective-permute-start | bytes 1572872 | tf_op jit(solution)/shard_map/ppermute | solution.py:45
  36.3 10.5 %collective-permute-start.14 = (bf16[256,1024]{1,0:T(8,128)(2,1)S(1)}, bf16[256,1024]{1,0:T(8,128)(2,1)S(1)}, u32[]{:S(2)}, u32[]{:S(2)}) collective-permute-start(bf16[256,1024]{1,0:T(8,128)(2,1)S(1)} %stack.3.refs_0_), channel_id=1, source_target_pairs={{0,16},{1,17},{2,18},{3,19},{4,20},{5,21},{6,22},{7,23},{8,24},{9,... | collective-permute-start | bytes 1572872 | tf_op jit(solution)/shard_map/ppermute | solution.py:45
  37.6 19.7 %collective-permute-start.5 = (bf16[256,1024]{1,0:T(8,128)(2,1)}, bf16[256,1024]{1,0:T(8,128)(2,1)}, u32[]{:S(2)}, u32[]{:S(2)}) collective-permute-start(bf16[256,1024]{1,0:T(8,128)(2,1)} %broadcast_select_fusion.3), channel_id=1, source_target_pairs={{0,8},{1,9},{2,10},{3,11},{4,12},{5,13},{6,14},{7,15},{8,0},{9,1},... | collective-permute-start | bytes 1572872 | tf_op jit(solution)/shard_map/ppermute | solution.py:45
  38.2 24.7 %collective-permute-start.7 = (bf16[256,1024]{1,0:T(8,128)(2,1)}, bf16[256,1024]{1,0:T(8,128)(2,1)}, u32[]{:S(2)}, u32[]{:S(2)}) collective-permute-start(bf16[256,1024]{1,0:T(8,128)(2,1)} %collective-permute-done.6.refs_2_), channel_id=1, source_target_pairs={{0,48},{1,49},{2,50},{3,51},{4,52},{5,53},{6,54},{7,55},{8,56},{9,... | collective-permute-start | bytes 1572872 | tf_op jit(solution)/shard_map/ppermute | solution.py:45
  46.0 32.7 %collective-permute-start.19 = (bf16[256,1024]{1,0:T(8,128)(2,1)}, bf16[256,1024]{1,0:T(8,128)(2,1)}, u32[]{:S(2)}, u32[]{:S(2)}) collective-permute-start(bf16[256,1024]{1,0:T(8,128)(2,1)} %collective-permute-done.18.refs_2_), channel_id=1, source_target_pairs={{0,48},{1,49},{2,50},{3,51},{4,52},{5,53},{6,54},{7,55},{8,56},{9,... | collective-permute-start | bytes 1572872 | tf_op jit(solution)/shard_map/ppermute | solution.py:45
  47.8 30.9 %collective-permute-start.15 = (bf16[256,1024]{1,0:T(8,128)(2,1)}, bf16[256,1024]{1,0:T(8,128)(2,1)}, u32[]{:S(2)}, u32[]{:S(2)}) collective-permute-start(bf16[256,1024]{1,0:T(8,128)(2,1)} %broadcast_select_fusion.2), channel_id=1, source_target_pairs={{0,8},{1,9},{2,10},{3,11},{4,12},{5,13},{6,14},{7,15},{8,0},{9,1},... | collective-permute-start | bytes 1572872 | tf_op jit(solution)/shard_map/ppermute | solution.py:45
  57.3 18.1 %collective-permute-start.16 = (bf16[128,896]{1,0:T(8,128)(2,1)S(1)}, bf16[128,896]{1,0:T(8,128)(2,1)S(1)}, u32[]{:S(2)}, u32[]{:S(2)}) collective-permute-start(bf16[128,896]{1,0:T(8,128)(2,1)S(1)} %dynamic-slice_bitcast_fusion), channel_id=1, source_target_pairs={{0,1},{1,2},{2,3},{3,4},{4,5},{5,6},{6,7},{7,8},{8,9},{9,10},{10,1... | collective-permute-start | bytes 688136 | tf_op jit(solution)/shard_map/ppermute | solution.py:389
  62.9 19.1 %collective-permute-start.10 = (bf16[128,4096]{1,0:T(8,128)(2,1)}, bf16[128,4096]{1,0:T(8,128)(2,1)S(1)}, u32[]{:S(2)}, u32[]{:S(2)}) collective-permute-start(bf16[128,4096]{1,0:T(8,128)(2,1)} %collective-permute-done.9.far_ref), channel_id=1, source_target_pairs={{0,64},{64,0},{1,65},{65,1},{2,66},{66,2},{3,67},{67,3},{4,68},{68... | collective-permute-start | bytes 3145736 | tf_op jit(solution)/shard_map/ppermute | solution.py:49
  74.2 15.3 %collective-permute-start.21 = (bf16[256,1024]{1,0:T(8,128)(2,1)}, bf16[256,1024]{1,0:T(8,128)(2,1)S(1)}, u32[]{:S(2)}, u32[]{:S(2)}) collective-permute-start(bf16[256,1024]{1,0:T(8,128)(2,1)} %collective-permute-done.5.refs_3_), channel_id=1, source_target_pairs={{0,16},{1,17},{2,18},{3,19},{4,20},{5,21},{6,22},{7,23},{8,24},{9,... | collective-permute-start | bytes 1572872 | tf_op jit(solution)/shard_map/ppermute | solution.py:45
  75.4 14.1 %collective-permute-start.22 = (bf16[256,1024]{1,0:T(8,128)(2,1)S(1)}, bf16[256,1024]{1,0:T(8,128)(2,1)S(1)}, u32[]{:S(2)}, u32[]{:S(2)}) collective-permute-start(bf16[256,1024]{1,0:T(8,128)(2,1)S(1)} %broadcast_select_fusion), channel_id=1, source_target_pairs={{0,48},{1,49},{2,50},{3,51},{4,52},{5,53},{6,54},{7,55},{8,56},{9,... | collective-permute-start | bytes 1572872 | tf_op jit(solution)/shard_map/ppermute | solution.py:45
  79.8 14.9 %collective-permute-start.20 = (bf16[256,1024]{1,0:T(8,128)(2,1)S(1)}, bf16[256,1024]{1,0:T(8,128)(2,1)S(1)}, u32[]{:S(2)}, u32[]{:S(2)}) collective-permute-start(bf16[256,1024]{1,0:T(8,128)(2,1)S(1)} %broadcast_select_fusion.1), channel_id=1, source_target_pairs={{0,48},{1,49},{2,50},{3,51},{4,52},{5,53},{6,54},{7,55},{8,56},{9,... | collective-permute-start | bytes 1572872 | tf_op jit(solution)/shard_map/ppermute | solution.py:45
  79.9 17.5 %collective-permute-start.17 = (bf16[256,1024]{1,0:T(8,128)(2,1)}, bf16[256,1024]{1,0:T(8,128)(2,1)S(1)}, u32[]{:S(2)}, u32[]{:S(2)}) collective-permute-start(bf16[256,1024]{1,0:T(8,128)(2,1)} %collective-permute-done.15.refs_0_), channel_id=1, source_target_pairs={{0,16},{1,17},{2,18},{3,19},{4,20},{5,21},{6,22},{7,23},{8,24},{9,... | collective-permute-start | bytes 1572872 | tf_op jit(solution)/shard_map/ppermute | solution.py:45
  89.5 14.3 %collective-permute-start.24 = (bf16[128,1024]{1,0:T(8,128)(2,1)S(1)}, bf16[128,1024]{1,0:T(8,128)(2,1)S(1)}, u32[]{:S(2)}, u32[]{:S(2)}) collective-permute-start(bf16[128,1024]{1,0:T(8,128)(2,1)S(1)} %slice.21), channel_id=1, source_target_pairs={{0,48},{1,49},{2,50},{3,51},{4,52},{5,53},{6,54},{7,55},{8,56},{9,... | collective-permute-start | bytes 786440 | tf_op jit(solution)/shard_map/ppermute | solution.py:45
  90.9 12.9 %collective-permute-start.23 = (bf16[128,1024]{1,0:T(8,128)(2,1)S(1)}, bf16[128,1024]{1,0:T(8,128)(2,1)S(1)}, u32[]{:S(2)}, u32[]{:S(2)}) collective-permute-start(bf16[128,1024]{1,0:T(8,128)(2,1)S(1)} %slice.20), channel_id=1, source_target_pairs={{0,16},{1,17},{2,18},{3,19},{4,20},{5,21},{6,22},{7,23},{8,24},{9,... | collective-permute-start | bytes 786440 | tf_op jit(solution)/shard_map/ppermute | solution.py:45
  94.8 9.0 %collective-permute-start.26 = (bf16[128,1024]{1,0:T(8,128)(2,1)S(1)}, bf16[128,1024]{1,0:T(8,128)(2,1)S(1)}, u32[]{:S(2)}, u32[]{:S(2)}) collective-permute-start(bf16[128,1024]{1,0:T(8,128)(2,1)S(1)} %slice.19), channel_id=1, source_target_pairs={{0,48},{1,49},{2,50},{3,51},{4,52},{5,53},{6,54},{7,55},{8,56},{9,... | collective-permute-start | bytes 786440 | tf_op jit(solution)/shard_map/ppermute | solution.py:45
  97.4 7.9 %collective-permute-start.25 = (bf16[128,1024]{1,0:T(8,128)(2,1)S(1)}, bf16[128,1024]{1,0:T(8,128)(2,1)S(1)}, u32[]{:S(2)}, u32[]{:S(2)}) collective-permute-start(bf16[128,1024]{1,0:T(8,128)(2,1)S(1)} %slice.18), channel_id=1, source_target_pairs={{0,16},{1,17},{2,18},{3,19},{4,20},{5,21},{6,22},{7,23},{8,24},{9,... | collective-permute-start | bytes 786440 | tf_op jit(solution)/shard_map/ppermute | solution.py:45
  (23 other events, 91.6 us)
where the time goes:
time: 112 us; the launch traced here: 111 us
  starting transfers between devices  42.3 us (38%)
  Pallas kernels  36.9 us (33%)
  waiting for transfers between devices  16.1 us (14%)
  local copies, waits for them, and re-layouts  11.6 us (10%)
  other arithmetic  4.14 us (4%)
    ppermute x23, starting transfers between devices, send(): return lax.ppermute(x, PLANE, pairs)  33.6 us
    ppermute x23, waiting for transfers between devices, send(): return lax.ppermute(x, PLANE, pairs)  14.6 us
    pallas_call x4, Pallas kernels, project(): pl.pallas_call(project_kernel, grid=(1,), out_shape=jax.ShapeDtypeStruct(...  14.2 us
    unnamed x36, local copies, waits for them, and re-layouts  11.5 us
    pallas_call x3, Pallas kernels, partial_product(): pl.pallas_call(body, out_shape=jax.ShapeDtypeStruct((rows, columns), jnp....  8.28 us
    pallas_call x1, Pallas kernels, attend(): pl.pallas_call(body, out_shape=jax.ShapeDtypeStruct((rows, columns), jnp....  6.1 us
    ppermute x1, starting transfers between devices, local(): lax.ppermute(after(prev, column_b), ('y', 'xl', 'z'), [(i, i + 1) for i i...  5.5 us
    pallas_call x1, Pallas kernels, gather_rows(): pl.pallas_call(rows_kernel, out_shape=jax.ShapeDtypeStruct((4 * rows, wid...  5.39 us
  transfers between devices with their start and end apart: 28, of which 7 were waited for; matrix products, arithmetic and copies ran while one was open for 4% of the time, Pallas kernels for 28%

commit v1 on v0

--- a/solution.py
+++ b/solution.py
@@ -21,8 +21,8 @@
     return pltpu.CompilerParams(vmem_limit_bytes=mib * MIB)
 
 
-def cost(flops, moved):
-    return pl.CostEstimate(flops=flops // 100, bytes_accessed=moved // 100, transcendentals=0)
+def cost(flops, moved, exps=0):
+    return pl.CostEstimate(flops=flops, bytes_accessed=moved, transcendentals=exps)
 
 
 def moved(move, y, xl, z):
@@ -382,14 +382,14 @@
         send(pick(round_one[2], round_one[0]), (1, "z"), (1, 0)),
     ]
     a = [column_a, *outer_first(column_a)]
-    keys_a = projected(0, 0, column_a)
-    column_b = stacked([after(head, keys_a), *round_two], ((0, 1, 2, 3), (0, 1, 2, 3)))
+    column_b = stacked([head, *round_two], ((0, 1, 2, 3), (0, 1, 2, 3)))
     half = nbr_states.shape[1] // 2
     prev = lax.dynamic_slice_in_dim(nbr_states[-1], core * half, half, 0)
     prev = lax.ppermute(after(prev, column_b), ("y", "xl", "z"), [(i, i + 1) for i in range(63)])
     b = [column_b, *outer_first(after(column_b, near))]
-    a += outer_second(*a)
-    values_a = projected(1, 0, *a[1:3])
+    a += outer_second(*a, *round_two)
+    keys_a = projected(0, 0, column_b)
+    values_a = projected(1, 0, keys_a, *a[1:3])
     b += outer_second(*b, values_a)
     keys_b = projected(0, 1, *b[1:3])
     far_near = hop(after(far, *a[3:5]), "core")

time: 112 us -> 106 us (0.946)
  the two profiles are of different devices: /device:TPU:32 before, /device:TPU:1 now
where the time goes in v1:
time: 106 us
  starting transfers between devices  48.6 us (46%)
  Pallas kernels  33.3 us (31%)
  waiting for transfers between devices  14.5 us (14%)
  local copies, waits for them, and re-layouts  6.14 us (6%)
  other arithmetic  3.13 us (3%)
    ppermute x23, starting transfers between devices, send(): return lax.ppermute(x, PLANE, pairs)  29.2 us
    ppermute x4, starting transfers between devices, hop(): return lax.ppermute(x, axis, [(0, 1), (1, 0)])  15.9 us
    ppermute x23, waiting for transfers between devices, send(): return lax.ppermute(x, PLANE, pairs)  14.5 us
    pallas_call x4, Pallas kernels, project(): pl.pallas_call(project_kernel, grid=(1,), out_shape=jax.ShapeDtypeStruct(...  14.2 us
    pallas_call x3, Pallas kernels, partial_product(): pl.pallas_call(body, out_shape=jax.ShapeDtypeStruct((rows, columns), jnp....  7.01 us
    pallas_call x1, Pallas kernels, attend(): pl.pallas_call(body, out_shape=jax.ShapeDtypeStruct((rows, columns), jnp....  6.09 us
    unnamed x16, local copies, waits for them, and re-layouts  6.04 us
    pallas_call x1, Pallas kernels, gather_rows(): pl.pallas_call(rows_kernel, out_shape=jax.ShapeDtypeStruct((4 * rows, wid...  4.07 us
  transfers between devices with their start and end apart: 28, of which 8 were waited for; matrix products, arithmetic and copies ran while one was open for 3% of the time, Pallas kernels for 26%

profile of v1, /device:TPU:1, one launch (start us, length us, event | category | flops | bytes accessed | tf_op | source)
XLA Modules:
  0.0 106.0 jit_solution(14555537237834642869)
XLA Ops:
  0.0 2.0 %collective-permute-start = (bf16[64,1024]{1,0:T(8,128)(2,1)}, bf16[64,1024]{1,0:T(8,128)(2,1)S(1)}, u32[]{:S(2)}, u32[]{:S(2)}) collective-permute-start(bf16[64,1024]{1,0:T(8,128)(2,1)} %refs_0_.1), channel_id=1, source_target_pairs={{0,1},{1,2},{2,3},{3,4},{4,5},{5,6},{6,7},{7,0},{8,9},{9,10},{10,1... | collective-permute-start | bytes 393224 | tf_op jit(solution)/shard_map/ppermute | solution.py:45
  2.0 2.7 %collective-permute-start.2 = (bf16[64,1024]{1,0:T(8,128)(2,1)}, bf16[64,1024]{1,0:T(8,128)(2,1)S(1)}, u32[]{:S(2)}, u32[]{:S(2)}) collective-permute-start(bf16[64,1024]{1,0:T(8,128)(2,1)} %refs_0_.1), channel_id=1, source_target_pairs={{0,2},{1,3},{2,4},{3,5},{4,6},{5,7},{6,0},{7,1},{8,10},{9,11},{10,... | collective-permute-start | bytes 393224 | tf_op jit(solution)/shard_map/ppermute | solution.py:45
  12.0 3.8 %collective-permute-start.11 = (bf16[128,4096]{1,0:T(8,128)(2,1)S(1)}, bf16[128,4096]{1,0:T(8,128)(2,1)}, u32[]{:S(2)}, u32[]{:S(2)}) collective-permute-start(bf16[128,4096]{1,0:T(8,128)(2,1)S(1)} %norm.1.own_ref), channel_id=1, source_target_pairs={{0,64},{64,0},{1,65},{65,1},{2,66},{66,2},{3,67},{67,3},{4,68},{68... | collective-permute-start | bytes 3145736 | tf_op jit(solution)/shard_map/ppermute | solution.py:49
  16.8 2.8 %collective-permute-start.5 = (bf16[64,1024]{1,0:T(8,128)(2,1)S(1)}, bf16[64,1024]{1,0:T(8,128)(2,1)S(1)}, u32[]{:S(2)}, u32[]{:S(2)}) collective-permute-start(bf16[64,1024]{1,0:T(8,128)(2,1)S(1)} %get-tuple-element.29.refs_0_), channel_id=1, source_target_pairs={{0,7},{1,0},{2,1},{3,2},{4,3},{5,4},{6,5},{7,6},{8,15},{9,8},{10,9... | collective-permute-start | bytes 393224 | tf_op jit(solution)/shard_map/ppermute | solution.py:45
  22.9 2.7 %collective-permute-start.12 = (bf16[128,4096]{1,0:T(8,128)(2,1)S(1)}, bf16[128,4096]{1,0:T(8,128)(2,1)}, u32[]{:S(2)}, u32[]{:S(2)}) collective-permute-start(bf16[128,4096]{1,0:T(8,128)(2,1)S(1)} %norm.1.own_ref), channel_id=1, source_target_pairs={{0,128},{128,0},{1,129},{129,1},{2,130},{130,2},{3,131},{131,3},{4... | collective-permute-start | bytes 3145736 | tf_op jit(solution)/shard_map/ppermute | solution.py:49
  26.4 5.4 %collective-permute-done.7.refs_3_ = bf16[64,1024]{1,0:T(8,128)(2,1)S(1)} collective-permute-done((bf16[64,1024]{1,0:T(8,128)(2,1)S(1)}, bf16[64,1024]{1,0:T(8,128)(2,1)S(1)}, u32[]{:S(2)}, u32[]{:S(2)}) %collective-permute-start.7) | collective-permute-done | bytes 131104 | tf_op jit(solution)/shard_map/ppermute | solution.py:45
  32.7 2.6 %collective-permute-start.8 = (bf16[256,1024]{1,0:T(8,128)(2,1)}, bf16[256,1024]{1,0:T(8,128)(2,1)}, u32[]{:S(2)}, u32[]{:S(2)}) collective-permute-start(bf16[256,1024]{1,0:T(8,128)(2,1)} %broadcast_select_fusion.3), channel_id=1, source_target_pairs={{0,8},{1,9},{2,10},{3,11},{4,12},{5,13},{6,14},{7,15},{8,0},{9,1},... | collective-permute-start | bytes 1572872 | tf_op jit(solution)/shard_map/ppermute | solution.py:45
  37.6 2.0 %copy-done = bf16[2,896,1024]{2,1,0:T(8,128)(2,1)S(1)} copy-done((bf16[2,896,1024]{2,1,0:T(8,128)(2,1)S(1)}, bf16[2,896,1024]{2,1,0:T(8,128)(2,1)}, u32[]{:S(2)}) %copy-start) | copy-done | bytes 3670040
  39.6 2.0 %copy-done.2 = bf16[8,256,896]{2,1,0:T(8,128)(2,1)S(1)} copy-done((bf16[8,256,896]{2,1,0:T(8,128)(2,1)S(1)}, bf16[8,256,896]{2,1,0:T(8,128)(2,1)}, u32[]{:S(2)}) %copy-start.2) | copy-done | bytes 3670040
  41.6 3.6 %project.5.refs_5_ = bf16[8,256,512]{2,1,0:T(8,128)(2,1)S(1)} custom-call(bf16[8,256,896]{2,1,0:T(8,128)(2,1)S(1)} %copy-done.2, bf16[2,896,1024]{2,1,0:T(8,128)(2,1)S(1)} %copy-done), custom_call_target="tpu_custom_call" | custom-call | flops 1879048192 | bytes 6291456 | tf_op jit(solution)/shard_map/project/pallas_call | solution.py:183
  45.2 3.6 %project.6.refs_7_ = bf16[8,256,512]{2,1,0:T(8,128)(2,1)S(1)} custom-call(bf16[8,256,896]{2,1,0:T(8,128)(2,1)S(1)} %copy-done.2, bf16[2,896,1024]{2,1,0:T(8,128)(2,1)S(1)} %copy-done), custom_call_target="tpu_custom_call" | custom-call | flops 1879048192 | bytes 6291456 | tf_op jit(solution)/shard_map/project/pallas_call | solution.py:183
  48.8 3.6 %collective-permute-start.16 = (bf16[128,896]{1,0:T(8,128)(2,1)S(1)}, bf16[128,896]{1,0:T(8,128)(2,1)S(1)}, u32[]{:S(2)}, u32[]{:S(2)}) collective-permute-start(bf16[128,896]{1,0:T(8,128)(2,1)S(1)} %dynamic-slice_bitcast_fusion), channel_id=1, source_target_pairs={{0,1},{1,2},{2,3},{3,4},{4,5},{5,6},{6,7},{7,8},{8,9},{9,10},{10,1... | collective-permute-start | bytes 688136 | tf_op jit(solution)/shard_map/ppermute | solution.py:388
  52.4 7.3 %collective-permute-start.13 = (bf16[128,4096]{1,0:T(8,128)(2,1)}, bf16[128,4096]{1,0:T(8,128)(2,1)S(1)}, u32[]{:S(2)}, u32[]{:S(2)}) collective-permute-start(bf16[128,4096]{1,0:T(8,128)(2,1)} %collective-permute-done.12.far_ref), channel_id=1, source_target_pairs={{0,64},{64,0},{1,65},{65,1},{2,66},{66,2},{3,67},{67,3},{4,68},{68... | collective-permute-start | bytes 3145736 | tf_op jit(solution)/shard_map/ppermute | solution.py:49
  59.6 2.5 %collective-permute-start.19 = (bf16[256,1024]{1,0:T(8,128)(2,1)}, bf16[256,1024]{1,0:T(8,128)(2,1)S(1)}, u32[]{:S(2)}, u32[]{:S(2)}) collective-permute-start(bf16[256,1024]{1,0:T(8,128)(2,1)} %collective-permute-done.18.refs_2_), channel_id=1, source_target_pairs={{0,48},{1,49},{2,50},{3,51},{4,52},{5,53},{6,54},{7,55},{8,56},{9,... | collective-permute-start | bytes 1572872 | tf_op jit(solution)/shard_map/ppermute | solution.py:45
  63.4 3.6 %project.4.refs_8_ = bf16[8,256,512]{2,1,0:T(8,128)(2,1)S(1)} custom-call(bf16[8,256,896]{2,1,0:T(8,128)(2,1)S(1)} %copy-done.2, bf16[2,896,1024]{2,1,0:T(8,128)(2,1)S(1)} %copy-done), custom_call_target="tpu_custom_call" | custom-call | flops 1879048192 | bytes 6291456 | tf_op jit(solution)/shard_map/project/pallas_call | solution.py:183
  67.0 3.6 %project.7.refs_6_ = bf16[8,256,512]{2,1,0:T(8,128)(2,1)S(1)} custom-call(bf16[8,256,896]{2,1,0:T(8,128)(2,1)S(1)} %copy-done.2, bf16[2,896,1024]{2,1,0:T(8,128)(2,1)S(1)} %copy-done), custom_call_target="tpu_custom_call" | custom-call | flops 1879048192 | bytes 6291456 | tf_op jit(solution)/shard_map/project/pallas_call | solution.py:183
  76.1 2.1 %collective-permute-start.27 = (bf16[128,896]{1,0:T(8,128)(2,1)S(1)}, bf16[128,896]{1,0:T(8,128)(2,1)S(1)}, u32[]{:S(2)}, u32[]{:S(2)}) collective-permute-start(bf16[128,896]{1,0:T(8,128)(2,1)S(1)} %collective-permute-done.16.mine_ref), channel_id=1, source_target_pairs={{0,64},{64,0},{1,65},{65,1},{2,66},{66,2},{3,67},{67,3},{4,68},{68... | collective-permute-start | bytes 688136 | tf_op jit(solution)/shard_map/ppermute | solution.py:49
  78.2 4.1 %rows.1.n_ref = bf16[512,4096]{1,0:T(8,128)(2,1)S(1)} custom-call(bf16[128,4096]{1,0:T(8,128)(2,1)S(1)} %norm.1.own_ref, bf16[128,4096]{1,0:T(8,128)(2,1)} %collective-permute-done.11.near_ref, bf16[128,4096]{1,0:T(8,128)(2,1)} %collective-permute-done.12.far_ref, bf16[128,4096]{1,0:T(8,128)(2,1)S(1)} %collective-permute-done.13.far_near_ref), custom_call_target="tpu_custom_call" | custom-call | bytes 8388608 | tf_op jit(solution)/shard_map/rows/pallas_call | solution.py:159
  82.3 2.0 %partial.3.refs_5_ = f32[512,1024]{1,0:T(8,128)S(1)} custom-call(bf16[512,4096]{1,0:T(8,128)(2,1)S(1)} %rows.1.n_ref, bf16[256,1024]{1,0:T(8,128)(2,1)S(1)} %stack.2.refs_0_, bf16[256,1024]{1,0:T(8,128)(2,1)S(1)} %collective-permute-done.4.refs_1_, bf16[256,1024]{1,0:T(8,128)(2,1)} %collective-permute-done.9.refs_2_), custom_call_target="tpu_custom_call" | custom-call | flops 805306368 | bytes 2359296 | tf_op jit(solution)/shard_map/partial/pallas_call | solution.py:243
  84.3 2.5 %collective-permute-start.24 = (bf16[128,1024]{1,0:T(8,128)(2,1)S(1)}, bf16[128,1024]{1,0:T(8,128)(2,1)S(1)}, u32[]{:S(2)}, u32[]{:S(2)}) collective-permute-start(bf16[128,1024]{1,0:T(8,128)(2,1)S(1)} %slice.21), channel_id=1, source_target_pairs={{0,48},{1,49},{2,50},{3,51},{4,52},{5,53},{6,54},{7,55},{8,56},{9,... | collective-permute-start | bytes 786440 | tf_op jit(solution)/shard_map/ppermute | solution.py:45
  86.9 3.2 %partial.4.refs_6_ = f32[512,1024]{1,0:T(8,128)S(1)} custom-call(bf16[512,4096]{1,0:T(8,128)(2,1)S(1)} %rows.1.n_ref, bf16[256,1024]{1,0:T(8,128)(2,1)S(1)} %stack.3.refs_0_, bf16[256,1024]{1,0:T(8,128)(2,1)} %collective-permute-done.14.refs_1_, bf16[256,1024]{1,0:T(8,128)(2,1)} %collective-permute-done.18.refs_2_, ...), custom_call_target="tpu_custom_call" | custom-call | flops 1342177280 | bytes 3932160 | tf_op jit(solution)/shard_map/partial/pallas_call | solution.py:243
  90.2 3.0 %collective-permute-start.26 = (bf16[128,1024]{1,0:T(8,128)(2,1)S(1)}, bf16[128,1024]{1,0:T(8,128)(2,1)S(1)}, u32[]{:S(2)}, u32[]{:S(2)}) collective-permute-start(bf16[128,1024]{1,0:T(8,128)(2,1)S(1)} %slice.19), channel_id=1, source_target_pairs={{0,48},{1,49},{2,50},{3,51},{4,52},{5,53},{6,54},{7,55},{8,56},{9,... | collective-permute-start | bytes 786440 | tf_op jit(solution)/shard_map/ppermute | solution.py:45
  96.4 3.5 %collective-permute-done.25.refs_2_ = bf16[128,1024]{1,0:T(8,128)(2,1)S(1)} collective-permute-done((bf16[128,1024]{1,0:T(8,128)(2,1)S(1)}, bf16[128,1024]{1,0:T(8,128)(2,1)S(1)}, u32[]{:S(2)}, u32[]{:S(2)}) %collective-permute-start.25) | collective-permute-done | bytes 262176 | tf_op jit(solution)/shard_map/ppermute | solution.py:45
  100.0 6.1 %attend.1 = bf16[512,1024]{1,0:T(8,128)(2,1)} custom-call(s32[2,512]{1,0:T(2,128)S(1)} %bitcast.7, s32[256,128]{1,0:T(8,128)S(1)} %bitcast.6, f32[512,1024]{1,0:T(8,128)S(1)} %partial.5.total_ref, bf16[512,4096]{1,0:T(8,128)(2,1)S(1)} %rows.1.n_ref, bf16[128,1024]{1,0:T(8,128)(2,1)S(1)} %collective-permute-done.23.refs_0_, ...), custom_call_target="tpu_custom_call" | custom-call | flops 6291456000 | bytes 16777216 | tf_op jit(solution)/shard_map/attend/pallas_call | solution.py:322
  (73 shorter events, 25.5 us)
Async XLA Ops:
  0.0 8.4 %collective-permute-start = (bf16[64,1024]{1,0:T(8,128)(2,1)}, bf16[64,1024]{1,0:T(8,128)(2,1)S(1)}, u32[]{:S(2)}, u32[]{:S(2)}) collective-permute-start(bf16[64,1024]{1,0:T(8,128)(2,1)} %refs_0_.1), channel_id=1, source_target_pairs={{0,1},{1,2},{2,3},{3,4},{4,5},{5,6},{6,7},{7,0},{8,9},{9,10},{10,1... | collective-permute-start | bytes 393224 | tf_op jit(solution)/shard_map/ppermute | solution.py:45
  2.0 6.4 %collective-permute-start.2 = (bf16[64,1024]{1,0:T(8,128)(2,1)}, bf16[64,1024]{1,0:T(8,128)(2,1)S(1)}, u32[]{:S(2)}, u32[]{:S(2)}) collective-permute-start(bf16[64,1024]{1,0:T(8,128)(2,1)} %refs_0_.1), channel_id=1, source_target_pairs={{0,2},{1,3},{2,4},{3,5},{4,6},{5,7},{6,0},{7,1},{8,10},{9,11},{10,... | collective-permute-start | bytes 393224 | tf_op jit(solution)/shard_map/ppermute | solution.py:45
  5.1 6.9 %collective-permute-start.1 = (bf16[64,1024]{1,0:T(8,128)(2,1)}, bf16[64,1024]{1,0:T(8,128)(2,1)S(1)}, u32[]{:S(2)}, u32[]{:S(2)}) collective-permute-start(bf16[64,1024]{1,0:T(8,128)(2,1)} %refs_0_.1), channel_id=1, source_target_pairs={{0,7},{1,0},{2,1},{3,2},{4,3},{5,4},{6,5},{7,6},{8,15},{9,8},{10,9... | collective-permute-start | bytes 393224 | tf_op jit(solution)/shard_map/ppermute | solution.py:45
  12.0 23.4 %collective-permute-start.11 = (bf16[128,4096]{1,0:T(8,128)(2,1)S(1)}, bf16[128,4096]{1,0:T(8,128)(2,1)}, u32[]{:S(2)}, u32[]{:S(2)}) collective-permute-start(bf16[128,4096]{1,0:T(8,128)(2,1)S(1)} %norm.1.own_ref), channel_id=1, source_target_pairs={{0,64},{64,0},{1,65},{65,1},{2,66},{66,2},{3,67},{67,3},{4,68},{68... | collective-permute-start | bytes 3145736 | tf_op jit(solution)/shard_map/ppermute | solution.py:49
  15.9 15.9 %collective-permute-start.4 = (bf16[256,1024]{1,0:T(8,128)(2,1)S(1)}, bf16[256,1024]{1,0:T(8,128)(2,1)S(1)}, u32[]{:S(2)}, u32[]{:S(2)}) collective-permute-start(bf16[256,1024]{1,0:T(8,128)(2,1)S(1)} %stack.2.refs_0_), channel_id=1, source_target_pairs={{0,16},{1,17},{2,18},{3,19},{4,20},{5,21},{6,22},{7,23},{8,24},{9,... | collective-permute-start | bytes 1572872 | tf_op jit(solution)/shard_map/ppermute | solution.py:45
  19.6 6.8 %collective-permute-start.6 = (bf16[64,1024]{1,0:T(8,128)(2,1)S(1)}, bf16[64,1024]{1,0:T(8,128)(2,1)S(1)}, u32[]{:S(2)}, u32[]{:S(2)}) collective-permute-start(bf16[64,1024]{1,0:T(8,128)(2,1)S(1)} %get-tuple-element.29.refs_0_), channel_id=1, source_target_pairs={{0,6},{1,7},{2,0},{3,1},{4,2},{5,3},{6,4},{7,5},{8,14},{9,15},{10,... | collective-permute-start | bytes 393224 | tf_op jit(solution)/shard_map/ppermute | solution.py:45
  19.9 15.3 %collective-permute-start.9 = (bf16[256,1024]{1,0:T(8,128)(2,1)S(1)}, bf16[256,1024]{1,0:T(8,128)(2,1)}, u32[]{:S(2)}, u32[]{:S(2)}) collective-permute-start(bf16[256,1024]{1,0:T(8,128)(2,1)S(1)} %stack.2.refs_0_), channel_id=1, source_target_pairs={{0,48},{1,49},{2,50},{3,51},{4,52},{5,53},{6,54},{7,55},{8,56},{9,... | collective-permute-start | bytes 1572872 | tf_op jit(solution)/shard_map/ppermute | solution.py:45
  22.9 29.5 %collective-permute-start.12 = (bf16[128,4096]{1,0:T(8,128)(2,1)S(1)}, bf16[128,4096]{1,0:T(8,128)(2,1)}, u32[]{:S(2)}, u32[]{:S(2)}) collective-permute-start(bf16[128,4096]{1,0:T(8,128)(2,1)S(1)} %norm.1.own_ref), channel_id=1, source_target_pairs={{0,128},{128,0},{1,129},{129,1},{2,130},{130,2},{3,131},{131,3},{4... | collective-permute-start | bytes 3145736 | tf_op jit(solution)/shard_map/ppermute | solution.py:49
  32.7 16.1 %collective-permute-start.8 = (bf16[256,1024]{1,0:T(8,128)(2,1)}, bf16[256,1024]{1,0:T(8,128)(2,1)}, u32[]{:S(2)}, u32[]{:S(2)}) collective-permute-start(bf16[256,1024]{1,0:T(8,128)(2,1)} %broadcast_select_fusion.3), channel_id=1, source_target_pairs={{0,8},{1,9},{2,10},{3,11},{4,12},{5,13},{6,14},{7,15},{8,0},{9,1},... | collective-permute-start | bytes 1572872 | tf_op jit(solution)/shard_map/ppermute | solution.py:45
  35.2 17.1 %collective-permute-start.10 = (bf16[256,1024]{1,0:T(8,128)(2,1)}, bf16[256,1024]{1,0:T(8,128)(2,1)}, u32[]{:S(2)}, u32[]{:S(2)}) collective-permute-start(bf16[256,1024]{1,0:T(8,128)(2,1)} %collective-permute-done.9.refs_2_), channel_id=1, source_target_pairs={{0,48},{1,49},{2,50},{3,51},{4,52},{5,53},{6,54},{7,55},{8,56},{9,... | collective-permute-start | bytes 1572872 | tf_op jit(solution)/shard_map/ppermute | solution.py:45
  35.4 24.3 %collective-permute-start.18 = (bf16[256,1024]{1,0:T(8,128)(2,1)S(1)}, bf16[256,1024]{1,0:T(8,128)(2,1)}, u32[]{:S(2)}, u32[]{:S(2)}) collective-permute-start(bf16[256,1024]{1,0:T(8,128)(2,1)S(1)} %stack.3.refs_0_), channel_id=1, source_target_pairs={{0,48},{1,49},{2,50},{3,51},{4,52},{5,53},{6,54},{7,55},{8,56},{9,... | collective-permute-start | bytes 1572872 | tf_op jit(solution)/shard_map/ppermute | solution.py:45
  36.3 25.9 %collective-permute-start.14 = (bf16[256,1024]{1,0:T(8,128)(2,1)S(1)}, bf16[256,1024]{1,0:T(8,128)(2,1)}, u32[]{:S(2)}, u32[]{:S(2)}) collective-permute-start(bf16[256,1024]{1,0:T(8,128)(2,1)S(1)} %stack.3.refs_0_), channel_id=1, source_target_pairs={{0,16},{1,17},{2,18},{3,19},{4,20},{5,21},{6,22},{7,23},{8,24},{9,... | collective-permute-start | bytes 1572872 | tf_op jit(solution)/shard_map/ppermute | solution.py:45
  48.8 24.7 %collective-permute-start.16 = (bf16[128,896]{1,0:T(8,128)(2,1)S(1)}, bf16[128,896]{1,0:T(8,128)(2,1)S(1)}, u32[]{:S(2)}, u32[]{:S(2)}) collective-permute-start(bf16[128,896]{1,0:T(8,128)(2,1)S(1)} %dynamic-slice_bitcast_fusion), channel_id=1, source_target_pairs={{0,1},{1,2},{2,3},{3,4},{4,5},{5,6},{6,7},{7,8},{8,9},{9,10},{10,1... | collective-permute-start | bytes 688136 | tf_op jit(solution)/shard_map/ppermute | solution.py:388
  52.4 23.7 %collective-permute-start.13 = (bf16[128,4096]{1,0:T(8,128)(2,1)}, bf16[128,4096]{1,0:T(8,128)(2,1)S(1)}, u32[]{:S(2)}, u32[]{:S(2)}) collective-permute-start(bf16[128,4096]{1,0:T(8,128)(2,1)} %collective-permute-done.12.far_ref), channel_id=1, source_target_pairs={{0,64},{64,0},{1,65},{65,1},{2,66},{66,2},{3,67},{67,3},{4,68},{68... | collective-permute-start | bytes 3145736 | tf_op jit(solution)/shard_map/ppermute | solution.py:49
  59.6 14.8 %collective-permute-start.19 = (bf16[256,1024]{1,0:T(8,128)(2,1)}, bf16[256,1024]{1,0:T(8,128)(2,1)S(1)}, u32[]{:S(2)}, u32[]{:S(2)}) collective-permute-start(bf16[256,1024]{1,0:T(8,128)(2,1)} %collective-permute-done.18.refs_2_), channel_id=1, source_target_pairs={{0,48},{1,49},{2,50},{3,51},{4,52},{5,53},{6,54},{7,55},{8,56},{9,... | collective-permute-start | bytes 1572872 | tf_op jit(solution)/shard_map/ppermute | solution.py:45
  63.3 11.2 %collective-permute-start.15 = (bf16[256,1024]{1,0:T(8,128)(2,1)S(1)}, bf16[256,1024]{1,0:T(8,128)(2,1)S(1)}, u32[]{:S(2)}, u32[]{:S(2)}) collective-permute-start(bf16[256,1024]{1,0:T(8,128)(2,1)S(1)} %broadcast_select_fusion.2), channel_id=1, source_target_pairs={{0,8},{1,9},{2,10},{3,11},{4,12},{5,13},{6,14},{7,15},{8,0},{9,1},... | collective-permute-start | bytes 1572872 | tf_op jit(solution)/shard_map/ppermute | solution.py:45
  70.5 13.8 %collective-permute-start.21 = (bf16[256,1024]{1,0:T(8,128)(2,1)}, bf16[256,1024]{1,0:T(8,128)(2,1)S(1)}, u32[]{:S(2)}, u32[]{:S(2)}) collective-permute-start(bf16[256,1024]{1,0:T(8,128)(2,1)} %collective-permute-done.8.refs_3_), channel_id=1, source_target_pairs={{0,16},{1,17},{2,18},{3,19},{4,20},{5,21},{6,22},{7,23},{8,24},{9,... | collective-permute-start | bytes 1572872 | tf_op jit(solution)/shard_map/ppermute | solution.py:45
  73.5 10.8 %collective-permute-start.22 = (bf16[256,1024]{1,0:T(8,128)(2,1)S(1)}, bf16[256,1024]{1,0:T(8,128)(2,1)S(1)}, u32[]{:S(2)}, u32[]{:S(2)}) collective-permute-start(bf16[256,1024]{1,0:T(8,128)(2,1)S(1)} %broadcast_select_fusion), channel_id=1, source_target_pairs={{0,48},{1,49},{2,50},{3,51},{4,52},{5,53},{6,54},{7,55},{8,56},{9,... | collective-permute-start | bytes 1572872 | tf_op jit(solution)/shard_map/ppermute | solution.py:45
  74.5 15.6 %collective-permute-start.20 = (bf16[256,1024]{1,0:T(8,128)(2,1)S(1)}, bf16[256,1024]{1,0:T(8,128)(2,1)S(1)}, u32[]{:S(2)}, u32[]{:S(2)}) collective-permute-start(bf16[256,1024]{1,0:T(8,128)(2,1)S(1)} %broadcast_select_fusion.1), channel_id=1, source_target_pairs={{0,48},{1,49},{2,50},{3,51},{4,52},{5,53},{6,54},{7,55},{8,56},{9,... | collective-permute-start | bytes 1572872 | tf_op jit(solution)/shard_map/ppermute | solution.py:45
  76.1 17.1 %collective-permute-start.17 = (bf16[256,1024]{1,0:T(8,128)(2,1)S(1)}, bf16[256,1024]{1,0:T(8,128)(2,1)S(1)}, u32[]{:S(2)}, u32[]{:S(2)}) collective-permute-start(bf16[256,1024]{1,0:T(8,128)(2,1)S(1)} %collective-permute-done.15.refs_0_), channel_id=1, source_target_pairs={{0,16},{1,17},{2,18},{3,19},{4,20},{5,21},{6,22},{7,23},{8,24},{9,... | collective-permute-start | bytes 1572872 | tf_op jit(solution)/shard_map/ppermute | solution.py:45
  76.1 17.2 %collective-permute-start.27 = (bf16[128,896]{1,0:T(8,128)(2,1)S(1)}, bf16[128,896]{1,0:T(8,128)(2,1)S(1)}, u32[]{:S(2)}, u32[]{:S(2)}) collective-permute-start(bf16[128,896]{1,0:T(8,128)(2,1)S(1)} %collective-permute-done.16.mine_ref), channel_id=1, source_target_pairs={{0,64},{64,0},{1,65},{65,1},{2,66},{66,2},{3,67},{67,3},{4,68},{68... | collective-permute-start | bytes 688136 | tf_op jit(solution)/shard_map/ppermute | solution.py:49
  84.3 12.0 %collective-permute-start.24 = (bf16[128,1024]{1,0:T(8,128)(2,1)S(1)}, bf16[128,1024]{1,0:T(8,128)(2,1)S(1)}, u32[]{:S(2)}, u32[]{:S(2)}) collective-permute-start(bf16[128,1024]{1,0:T(8,128)(2,1)S(1)} %slice.21), channel_id=1, source_target_pairs={{0,48},{1,49},{2,50},{3,51},{4,52},{5,53},{6,54},{7,55},{8,56},{9,... | collective-permute-start | bytes 786440 | tf_op jit(solution)/shard_map/ppermute | solution.py:45
  86.8 9.5 %collective-permute-start.23 = (bf16[128,1024]{1,0:T(8,128)(2,1)S(1)}, bf16[128,1024]{1,0:T(8,128)(2,1)S(1)}, u32[]{:S(2)}, u32[]{:S(2)}) collective-permute-start(bf16[128,1024]{1,0:T(8,128)(2,1)S(1)} %slice.20), channel_id=1, source_target_pairs={{0,16},{1,17},{2,18},{3,19},{4,20},{5,21},{6,22},{7,23},{8,24},{9,... | collective-permute-start | bytes 786440 | tf_op jit(solution)/shard_map/ppermute | solution.py:45
  93.1 6.8 %collective-permute-start.25 = (bf16[128,1024]{1,0:T(8,128)(2,1)S(1)}, bf16[128,1024]{1,0:T(8,128)(2,1)S(1)}, u32[]{:S(2)}, u32[]{:S(2)}) collective-permute-start(bf16[128,1024]{1,0:T(8,128)(2,1)S(1)} %slice.18), channel_id=1, source_target_pairs={{0,16},{1,17},{2,18},{3,19},{4,20},{5,21},{6,22},{7,23},{8,24},{9,... | collective-permute-start | bytes 786440 | tf_op jit(solution)/shard_map/ppermute | solution.py:45
  (13 other events, 76.4 us)

commit v2 on v1

--- a/solution.py
+++ b/solution.py
@@ -81,7 +81,7 @@
         out_shape=jax.ShapeDtypeStruct((4 * rows, columns), parts[0].dtype),
         in_specs=[VMEM] * len(parts),
         out_specs=VMEM,
-        compiler_params=params(8),
+        compiler_params=params(4),
         cost_estimate=cost(0, 16 * rows * columns),
         name="stack",
     )(*parts)
@@ -161,19 +161,17 @@
         out_shape=jax.ShapeDtypeStruct((4 * rows, width), parts[0].dtype),
         in_specs=[VMEM] * 4,
         out_specs=VMEM,
-        compiler_params=params(16),
+        compiler_params=params(10),
         cost_estimate=cost(0, 16 * rows * width),
         name="rows",
     )(*parts)
 
 
 def project_kernel(states_ref, w_ref, out_ref):
-    def one(i, _):
+    for i in range(out_ref.shape[0]):
         out_ref[i] = jnp.dot(
             states_ref[i], w_ref[0], preferred_element_type=jnp.float32
         ).astype(jnp.bfloat16)
-
-    lax.fori_loop(0, out_ref.shape[0], one, None)
 
 
 def project(states, w, which, half):
@@ -189,7 +187,7 @@
             pl.BlockSpec((1, depth, columns), lambda i: (which, 0, half), pipeline_mode=pl.Buffered(1)),
         ],
         out_specs=pl.BlockSpec((spans, keys, columns), whole, pipeline_mode=pl.Buffered(1)),
-        compiler_params=params(16),
+        compiler_params=params(10),
         cost_estimate=cost(2 * spans * keys * depth * columns, 6 * MIB),
         name="project",
     )(states, w)
@@ -212,7 +210,7 @@
         out_shape=jax.ShapeDtypeStruct((2, 2 * rows, columns), jnp.bfloat16),
         in_specs=[VMEM] * 3,
         out_specs=VMEM,
-        compiler_params=params(12),
+        compiler_params=params(8),
         cost_estimate=cost(8 * rows * depth * columns, 6 * MIB),
         name="project_prev",
     )(mine, other, w)
@@ -235,17 +233,23 @@
 
     def body(n_ref, *refs):
         places = [slot * 512 + start for start, which, _ in terms for slot in outer_slots(which)]
-        total = products(n_ref, refs[: len(pieces)], places)
-        if extra:
-            total = total + refs[len(pieces)][...]
-        refs[-1][...] = total
+        tile = columns // 2
+
+        def one(i, _):
+            at = pl.ds(pl.multiple_of(i * tile, tile), tile)
+            total = products(n_ref, [ref.at[:, at] for ref in refs[: len(pieces)]], places)
+            if extra:
+                total = total + refs[len(pieces)][:, at]
+            refs[-1][:, at] = total
+
+        lax.fori_loop(0, columns // tile, one, None)
 
     return pl.pallas_call(
         body,
         out_shape=jax.ShapeDtypeStruct((rows, columns), jnp.float32),
         in_specs=[VMEM] * (1 + len(pieces) + len(extra)),
         out_specs=VMEM,
-        compiler_params=params(20),
+        compiler_params=params(14),
         cost_estimate=cost(2 * rows * depth * columns, 2 * depth * (rows + columns)),
         name="partial",
     )(n, *pieces, *extra)
@@ -299,13 +303,16 @@
                         preferred_element_type=jnp.float32,
                     )
                     s_scr[h, b * SPAN : (b + 1) * SPAN, :] = jnp.where(usable[b], scores, jnp.float32(-1e30))
-            for h in range(heads):
+
+            def soften(h, _):
                 for c in range(blocks // 3):
                     r = slice(c * 3 * SPAN, (c + 1) * 3 * SPAN)
                     scores = s_scr[h, r, :]
                     weights = jnp.exp(scores - jnp.max(scores, axis=-1, keepdims=True))
                     scale = 1.0 / jnp.sum(weights, axis=-1, keepdims=True)
                     w_scr[h, r, :] = (weights * scale).astype(jnp.bfloat16)
+
+            lax.fori_loop(0, heads, soften, None)
             for h in range(heads):
                 at = slice(h * HEAD_DIM, (h + 1) * HEAD_DIM)
                 to = slice(part * half + h * HEAD_DIM, part * half + (h + 1) * HEAD_DIM)
@@ -330,7 +337,7 @@
             pltpu.VMEM((heads, blocks * SPAN, 2 * NBR_LEN), jnp.float32),
             pltpu.VMEM((heads, blocks * SPAN, 2 * NBR_LEN), jnp.bfloat16),
         ],
-        compiler_params=params(28),
+        compiler_params=params(27),
         cost_estimate=cost(6 * MIB * 1000, 16 * MIB),
         name="attend",
     )(lens, segments, total, n, *pieces, prev, *keys, *values)

time: 106 us -> 106 us (level)
  the two profiles are of different devices: /device:TPU:1 before, /device:TPU:2 now
where the time goes in v2:
time: 106 us; the launch traced here: 104 us
  starting transfers between devices  38.6 us (36%)
  Pallas kernels  29.6 us (28%)
  waiting for transfers between devices  27.2 us (26%)
  local copies, waits for them, and re-layouts  6.14 us (6%)
  other arithmetic  2.11 us (2%)
    ppermute x23, starting transfers between devices, send(): return lax.ppermute(x, PLANE, pairs)  34.5 us
    ppermute x23, waiting for transfers between devices, send(): return lax.ppermute(x, PLANE, pairs)  27.2 us
    pallas_call x4, Pallas kernels, project(): pl.pallas_call(project_kernel, grid=(1,), out_shape=jax.ShapeDtypeStruct(...  9.33 us
    pallas_call x1, Pallas kernels, attend(): pl.pallas_call(body, out_shape=jax.ShapeDtypeStruct((rows, columns), jnp....  7.87 us
    pallas_call x3, Pallas kernels, partial_product(): pl.pallas_call(body, out_shape=jax.ShapeDtypeStruct((rows, columns), jnp....  7.43 us
    unnamed x18, local copies, waits for them, and re-layouts  6.04 us
    pallas_call x1, Pallas kernels, gather_rows(): pl.pallas_call(rows_kernel, out_shape=jax.ShapeDtypeStruct((4 * rows, wid...  3.01 us
    ppermute x4, starting transfers between devices, hop(): return lax.ppermute(x, axis, [(0, 1), (1, 0)])  2.24 us
  transfers between devices with their start and end apart: 28, of which 8 were waited for; matrix products, arithmetic and copies ran while one was open for 2% of the time, Pallas kernels for 21%

profile of v2, /device:TPU:2, one launch (start us, length us, event | category | flops | bytes accessed | tf_op | source)
XLA Modules:
  0.0 104.0 jit_solution(1355315446042379685)
XLA Ops:
  1.9 3.3 %collective-permute-start.2 = (bf16[64,1024]{1,0:T(8,128)(2,1)}, bf16[64,1024]{1,0:T(8,128)(2,1)S(1)}, u32[]{:S(2)}, u32[]{:S(2)}) collective-permute-start(bf16[64,1024]{1,0:T(8,128)(2,1)} %refs_0_.1), channel_id=1, source_target_pairs={{0,2},{1,3},{2,4},{3,5},{4,6},{5,7},{6,0},{7,1},{8,10},{9,11},{10,... | collective-permute-start | bytes 393224 | tf_op jit(solution)/shard_map/ppermute | solution.py:45
  5.2 2.1 %collective-permute-start.3 = (bf16[64,1024]{1,0:T(8,128)(2,1)}, bf16[64,1024]{1,0:T(8,128)(2,1)S(1)}, u32[]{:S(2)}, u32[]{:S(2)}) collective-permute-start(bf16[64,1024]{1,0:T(8,128)(2,1)} %refs_0_.1), channel_id=1, source_target_pairs={{0,6},{1,7},{2,0},{3,1},{4,2},{5,3},{6,4},{7,5},{8,14},{9,15},{10,... | collective-permute-start | bytes 393224 | tf_op jit(solution)/shard_map/ppermute | solution.py:45
  16.1 2.3 %collective-permute-start.5 = (bf16[64,1024]{1,0:T(8,128)(2,1)S(1)}, bf16[64,1024]{1,0:T(8,128)(2,1)S(1)}, u32[]{:S(2)}, u32[]{:S(2)}) collective-permute-start(bf16[64,1024]{1,0:T(8,128)(2,1)S(1)} %get-tuple-element.29.refs_0_), channel_id=1, source_target_pairs={{0,7},{1,0},{2,1},{3,2},{4,3},{5,4},{6,5},{7,6},{8,15},{9,8},{10,9... | collective-permute-start | bytes 393224 | tf_op jit(solution)/shard_map/ppermute | solution.py:45
  21.5 2.1 %collective-permute-start.12 = (bf16[128,4096]{1,0:T(8,128)(2,1)S(1)}, bf16[128,4096]{1,0:T(8,128)(2,1)}, u32[]{:S(2)}, u32[]{:S(2)}) collective-permute-start(bf16[128,4096]{1,0:T(8,128)(2,1)S(1)} %norm.1.own_ref), channel_id=1, source_target_pairs={{0,128},{128,0},{1,129},{129,1},{2,130},{130,2},{3,131},{131,3},{4... | collective-permute-start | bytes 3145736 | tf_op jit(solution)/shard_map/ppermute | solution.py:49
  23.7 2.4 %collective-permute-done.6.refs_2_ = bf16[64,1024]{1,0:T(8,128)(2,1)S(1)} collective-permute-done((bf16[64,1024]{1,0:T(8,128)(2,1)S(1)}, bf16[64,1024]{1,0:T(8,128)(2,1)S(1)}, u32[]{:S(2)}, u32[]{:S(2)}) %collective-permute-start.6) | collective-permute-done | bytes 131104 | tf_op jit(solution)/shard_map/ppermute | solution.py:45
  26.1 6.2 %collective-permute-done.7.refs_3_ = bf16[64,1024]{1,0:T(8,128)(2,1)S(1)} collective-permute-done((bf16[64,1024]{1,0:T(8,128)(2,1)S(1)}, bf16[64,1024]{1,0:T(8,128)(2,1)S(1)}, u32[]{:S(2)}, u32[]{:S(2)}) %collective-permute-start.7) | collective-permute-done | bytes 131104 | tf_op jit(solution)/shard_map/ppermute | solution.py:45
  33.7 2.4 %collective-permute-start.10 = (bf16[256,1024]{1,0:T(8,128)(2,1)}, bf16[256,1024]{1,0:T(8,128)(2,1)}, u32[]{:S(2)}, u32[]{:S(2)}) collective-permute-start(bf16[256,1024]{1,0:T(8,128)(2,1)} %collective-permute-done.9.refs_2_), channel_id=1, source_target_pairs={{0,48},{1,49},{2,50},{3,51},{4,52},{5,53},{6,54},{7,55},{8,56},{9,... | collective-permute-start | bytes 1572872 | tf_op jit(solution)/shard_map/ppermute | solution.py:45
  38.2 2.0 %copy-done = bf16[2,896,1024]{2,1,0:T(8,128)(2,1)S(1)} copy-done((bf16[2,896,1024]{2,1,0:T(8,128)(2,1)S(1)}, bf16[2,896,1024]{2,1,0:T(8,128)(2,1)}, u32[]{:S(2)}) %copy-start) | copy-done | bytes 3670040
  40.3 2.0 %copy-done.2 = bf16[8,256,896]{2,1,0:T(8,128)(2,1)S(1)} copy-done((bf16[8,256,896]{2,1,0:T(8,128)(2,1)S(1)}, bf16[8,256,896]{2,1,0:T(8,128)(2,1)}, u32[]{:S(2)}) %copy-start.2) | copy-done | bytes 3670040
  42.3 2.3 %project.5.refs_5_ = bf16[8,256,512]{2,1,0:T(8,128)(2,1)S(1)} custom-call(bf16[8,256,896]{2,1,0:T(8,128)(2,1)S(1)} %copy-done.2, bf16[2,896,1024]{2,1,0:T(8,128)(2,1)S(1)} %copy-done), custom_call_target="tpu_custom_call" | custom-call | flops 1879048192 | bytes 6291456 | tf_op jit(solution)/shard_map/project/pallas_call | solution.py:181
  44.7 2.3 %project.6.refs_7_ = bf16[8,256,512]{2,1,0:T(8,128)(2,1)S(1)} custom-call(bf16[8,256,896]{2,1,0:T(8,128)(2,1)S(1)} %copy-done.2, bf16[2,896,1024]{2,1,0:T(8,128)(2,1)S(1)} %copy-done), custom_call_target="tpu_custom_call" | custom-call | flops 1879048192 | bytes 6291456 | tf_op jit(solution)/shard_map/project/pallas_call | solution.py:181
  47.0 9.7 %collective-permute-done.8.refs_3_ = bf16[256,1024]{1,0:T(8,128)(2,1)} collective-permute-done((bf16[256,1024]{1,0:T(8,128)(2,1)}, bf16[256,1024]{1,0:T(8,128)(2,1)}, u32[]{:S(2)}, u32[]{:S(2)}) %collective-permute-start.8) | collective-permute-done | bytes 524320 | tf_op jit(solution)/shard_map/ppermute | solution.py:45
  58.7 2.5 %collective-permute-start.19 = (bf16[256,1024]{1,0:T(8,128)(2,1)}, bf16[256,1024]{1,0:T(8,128)(2,1)S(1)}, u32[]{:S(2)}, u32[]{:S(2)}) collective-permute-start(bf16[256,1024]{1,0:T(8,128)(2,1)} %collective-permute-done.18.refs_2_), channel_id=1, source_target_pairs={{0,48},{1,49},{2,50},{3,51},{4,52},{5,53},{6,54},{7,55},{8,56},{9,... | collective-permute-start | bytes 1572872 | tf_op jit(solution)/shard_map/ppermute | solution.py:45
  61.4 2.3 %project.4.refs_8_ = bf16[8,256,512]{2,1,0:T(8,128)(2,1)S(1)} custom-call(bf16[8,256,896]{2,1,0:T(8,128)(2,1)S(1)} %copy-done.3, bf16[2,896,1024]{2,1,0:T(8,128)(2,1)S(1)} %copy-done.1), custom_call_target="tpu_custom_call" | custom-call | flops 1879048192 | bytes 6291456 | tf_op jit(solution)/shard_map/project/pallas_call | solution.py:181
  63.7 2.3 %project.7.refs_6_ = bf16[8,256,512]{2,1,0:T(8,128)(2,1)S(1)} custom-call(bf16[8,256,896]{2,1,0:T(8,128)(2,1)S(1)} %copy-done.3, bf16[2,896,1024]{2,1,0:T(8,128)(2,1)S(1)} %copy-done.1), custom_call_target="tpu_custom_call" | custom-call | flops 1879048192 | bytes 6291456 | tf_op jit(solution)/shard_map/project/pallas_call | solution.py:181
  67.3 3.3 %collective-permute-start.22 = (bf16[256,1024]{1,0:T(8,128)(2,1)S(1)}, bf16[256,1024]{1,0:T(8,128)(2,1)S(1)}, u32[]{:S(2)}, u32[]{:S(2)}) collective-permute-start(bf16[256,1024]{1,0:T(8,128)(2,1)S(1)} %broadcast_select_fusion), channel_id=1, source_target_pairs={{0,48},{1,49},{2,50},{3,51},{4,52},{5,53},{6,54},{7,55},{8,56},{9,... | collective-permute-start | bytes 1572872 | tf_op jit(solution)/shard_map/ppermute | solution.py:45
  74.5 3.0 %rows.1.n_ref = bf16[512,4096]{1,0:T(8,128)(2,1)S(1)} custom-call(bf16[128,4096]{1,0:T(8,128)(2,1)S(1)} %norm.1.own_ref, bf16[128,4096]{1,0:T(8,128)(2,1)} %collective-permute-done.11.near_ref, bf16[128,4096]{1,0:T(8,128)(2,1)} %collective-permute-done.12.far_ref, bf16[128,4096]{1,0:T(8,128)(2,1)S(1)} %collective-permute-done.13.far_near_ref), custom_call_target="tpu_custom_call" | custom-call | bytes 8388608 | tf_op jit(solution)/shard_map/rows/pallas_call | solution.py:159
  77.5 2.2 %partial.3.refs_5_ = f32[512,1024]{1,0:T(8,128)S(1)} custom-call(bf16[512,4096]{1,0:T(8,128)(2,1)S(1)} %rows.1.n_ref, bf16[256,1024]{1,0:T(8,128)(2,1)S(1)} %stack.2.refs_0_, bf16[256,1024]{1,0:T(8,128)(2,1)S(1)} %collective-permute-done.4.refs_1_, bf16[256,1024]{1,0:T(8,128)(2,1)} %collective-permute-done.9.refs_2_), custom_call_target="tpu_custom_call" | custom-call | flops 805306368 | bytes 2359296 | tf_op jit(solution)/shard_map/partial/pallas_call | solution.py:247
  79.8 2.0 %collective-permute-start.24 = (bf16[128,1024]{1,0:T(8,128)(2,1)S(1)}, bf16[128,1024]{1,0:T(8,128)(2,1)S(1)}, u32[]{:S(2)}, u32[]{:S(2)}) collective-permute-start(bf16[128,1024]{1,0:T(8,128)(2,1)S(1)} %slice.21), channel_id=1, source_target_pairs={{0,48},{1,49},{2,50},{3,51},{4,52},{5,53},{6,54},{7,55},{8,56},{9,... | collective-permute-start | bytes 786440 | tf_op jit(solution)/shard_map/ppermute | solution.py:45
  82.0 3.2 %partial.4.refs_6_ = f32[512,1024]{1,0:T(8,128)S(1)} custom-call(bf16[512,4096]{1,0:T(8,128)(2,1)S(1)} %rows.1.n_ref, bf16[256,1024]{1,0:T(8,128)(2,1)S(1)} %stack.3.refs_0_, bf16[256,1024]{1,0:T(8,128)(2,1)} %collective-permute-done.14.refs_1_, bf16[256,1024]{1,0:T(8,128)(2,1)} %collective-permute-done.18.refs_2_, ...), custom_call_target="tpu_custom_call" | custom-call | flops 1342177280 | bytes 3932160 | tf_op jit(solution)/shard_map/partial/pallas_call | solution.py:247
  85.2 3.2 %collective-permute-start.26 = (bf16[128,1024]{1,0:T(8,128)(2,1)S(1)}, bf16[128,1024]{1,0:T(8,128)(2,1)S(1)}, u32[]{:S(2)}, u32[]{:S(2)}) collective-permute-start(bf16[128,1024]{1,0:T(8,128)(2,1)S(1)} %slice.19), channel_id=1, source_target_pairs={{0,48},{1,49},{2,50},{3,51},{4,52},{5,53},{6,54},{7,55},{8,56},{9,... | collective-permute-start | bytes 786440 | tf_op jit(solution)/shard_map/ppermute | solution.py:45
  89.9 2.0 %partial.5.total_ref = f32[512,1024]{1,0:T(8,128)S(1)} custom-call(bf16[512,4096]{1,0:T(8,128)(2,1)S(1)} %rows.1.n_ref, bf16[256,1024]{1,0:T(8,128)(2,1)S(1)} %collective-permute-done.15.refs_0_, bf16[256,1024]{1,0:T(8,128)(2,1)S(1)} %collective-permute-done.19.refs_1_, bf16[256,1024]{1,0:T(8,128)(2,1)S(1)} %collective-permute-done.21.refs_2_, ...), custom_call_target="tpu_custom_call" | custom-call | flops 1610612736 | bytes 4718592 | tf_op jit(solution)/shard_map/partial/pallas_call | solution.py:247
  92.3 3.8 %collective-permute-done.25.refs_2_ = bf16[128,1024]{1,0:T(8,128)(2,1)S(1)} collective-permute-done((bf16[128,1024]{1,0:T(8,128)(2,1)S(1)}, bf16[128,1024]{1,0:T(8,128)(2,1)S(1)}, u32[]{:S(2)}, u32[]{:S(2)}) %collective-permute-start.25) | collective-permute-done | bytes 262176 | tf_op jit(solution)/shard_map/ppermute | solution.py:45
  96.1 7.9 %attend.1 = bf16[512,1024]{1,0:T(8,128)(2,1)} custom-call(s32[2,512]{1,0:T(2,128)S(1)} %bitcast.7, s32[256,128]{1,0:T(8,128)S(1)} %bitcast.6, f32[512,1024]{1,0:T(8,128)S(1)} %partial.5.total_ref, bf16[512,4096]{1,0:T(8,128)(2,1)S(1)} %rows.1.n_ref, bf16[128,1024]{1,0:T(8,128)(2,1)S(1)} %collective-permute-done.23.refs_0_, ...), custom_call_target="tpu_custom_call" | custom-call | flops 6291456000 | bytes 16777216 | tf_op jit(solution)/shard_map/attend/pallas_call | solution.py:329
  (75 shorter events, 26.7 us)
Async XLA Ops:
  0.0 11.3 %collective-permute-start = (bf16[64,1024]{1,0:T(8,128)(2,1)}, bf16[64,1024]{1,0:T(8,128)(2,1)S(1)}, u32[]{:S(2)}, u32[]{:S(2)}) collective-permute-start(bf16[64,1024]{1,0:T(8,128)(2,1)} %refs_0_.1), channel_id=1, source_target_pairs={{0,1},{1,2},{2,3},{3,4},{4,5},{5,6},{6,7},{7,0},{8,9},{9,10},{10,1... | collective-permute-start | bytes 393224 | tf_op jit(solution)/shard_map/ppermute | solution.py:45
  1.9 10.6 %collective-permute-start.2 = (bf16[64,1024]{1,0:T(8,128)(2,1)}, bf16[64,1024]{1,0:T(8,128)(2,1)S(1)}, u32[]{:S(2)}, u32[]{:S(2)}) collective-permute-start(bf16[64,1024]{1,0:T(8,128)(2,1)} %refs_0_.1), channel_id=1, source_target_pairs={{0,2},{1,3},{2,4},{3,5},{4,6},{5,7},{6,0},{7,1},{8,10},{9,11},{10,... | collective-permute-start | bytes 393224 | tf_op jit(solution)/shard_map/ppermute | solution.py:45
  5.2 7.3 %collective-permute-start.3 = (bf16[64,1024]{1,0:T(8,128)(2,1)}, bf16[64,1024]{1,0:T(8,128)(2,1)S(1)}, u32[]{:S(2)}, u32[]{:S(2)}) collective-permute-start(bf16[64,1024]{1,0:T(8,128)(2,1)} %refs_0_.1), channel_id=1, source_target_pairs={{0,6},{1,7},{2,0},{3,1},{4,2},{5,3},{6,4},{7,5},{8,14},{9,15},{10,... | collective-permute-start | bytes 393224 | tf_op jit(solution)/shard_map/ppermute | solution.py:45
  14.3 21.8 %collective-permute-start.11 = (bf16[128,4096]{1,0:T(8,128)(2,1)S(1)}, bf16[128,4096]{1,0:T(8,128)(2,1)}, u32[]{:S(2)}, u32[]{:S(2)}) collective-permute-start(bf16[128,4096]{1,0:T(8,128)(2,1)S(1)} %norm.1.own_ref), channel_id=1, source_target_pairs={{0,64},{64,0},{1,65},{65,1},{2,66},{66,2},{3,67},{67,3},{4,68},{68... | collective-permute-start | bytes 3145736 | tf_op jit(solution)/shard_map/ppermute | solution.py:49
  14.4 17.9 %collective-permute-start.4 = (bf16[256,1024]{1,0:T(8,128)(2,1)S(1)}, bf16[256,1024]{1,0:T(8,128)(2,1)S(1)}, u32[]{:S(2)}, u32[]{:S(2)}) collective-permute-start(bf16[256,1024]{1,0:T(8,128)(2,1)S(1)} %stack.2.refs_0_), channel_id=1, source_target_pairs={{0,16},{1,17},{2,18},{3,19},{4,20},{5,21},{6,22},{7,23},{8,24},{9,... | collective-permute-start | bytes 1572872 | tf_op jit(solution)/shard_map/ppermute | solution.py:45
  18.3 7.7 %collective-permute-start.6 = (bf16[64,1024]{1,0:T(8,128)(2,1)S(1)}, bf16[64,1024]{1,0:T(8,128)(2,1)S(1)}, u32[]{:S(2)}, u32[]{:S(2)}) collective-permute-start(bf16[64,1024]{1,0:T(8,128)(2,1)S(1)} %get-tuple-element.29.refs_0_), channel_id=1, source_target_pairs={{0,6},{1,7},{2,0},{3,1},{4,2},{5,3},{6,4},{7,5},{8,14},{9,15},{10,... | collective-permute-start | bytes 393224 | tf_op jit(solution)/shard_map/ppermute | solution.py:45
  19.9 13.8 %collective-permute-start.9 = (bf16[256,1024]{1,0:T(8,128)(2,1)S(1)}, bf16[256,1024]{1,0:T(8,128)(2,1)}, u32[]{:S(2)}, u32[]{:S(2)}) collective-permute-start(bf16[256,1024]{1,0:T(8,128)(2,1)S(1)} %stack.2.refs_0_), channel_id=1, source_target_pairs={{0,48},{1,49},{2,50},{3,51},{4,52},{5,53},{6,54},{7,55},{8,56},{9,... | collective-permute-start | bytes 1572872 | tf_op jit(solution)/shard_map/ppermute | solution.py:45
  21.5 37.1 %collective-permute-start.12 = (bf16[128,4096]{1,0:T(8,128)(2,1)S(1)}, bf16[128,4096]{1,0:T(8,128)(2,1)}, u32[]{:S(2)}, u32[]{:S(2)}) collective-permute-start(bf16[128,4096]{1,0:T(8,128)(2,1)S(1)} %norm.1.own_ref), channel_id=1, source_target_pairs={{0,128},{128,0},{1,129},{129,1},{2,130},{130,2},{3,131},{131,3},{4... | collective-permute-start | bytes 3145736 | tf_op jit(solution)/shard_map/ppermute | solution.py:49
  33.1 23.6 %collective-permute-start.8 = (bf16[256,1024]{1,0:T(8,128)(2,1)}, bf16[256,1024]{1,0:T(8,128)(2,1)}, u32[]{:S(2)}, u32[]{:S(2)}) collective-permute-start(bf16[256,1024]{1,0:T(8,128)(2,1)} %broadcast_select_fusion.3), channel_id=1, source_target_pairs={{0,8},{1,9},{2,10},{3,11},{4,12},{5,13},{6,14},{7,15},{8,0},{9,1},... | collective-permute-start | bytes 1572872 | tf_op jit(solution)/shard_map/ppermute | solution.py:45
  33.7 24.9 %collective-permute-start.10 = (bf16[256,1024]{1,0:T(8,128)(2,1)}, bf16[256,1024]{1,0:T(8,128)(2,1)}, u32[]{:S(2)}, u32[]{:S(2)}) collective-permute-start(bf16[256,1024]{1,0:T(8,128)(2,1)} %collective-permute-done.9.refs_2_), channel_id=1, source_target_pairs={{0,48},{1,49},{2,50},{3,51},{4,52},{5,53},{6,54},{7,55},{8,56},{9,... | collective-permute-start | bytes 1572872 | tf_op jit(solution)/shard_map/ppermute | solution.py:45
  36.1 22.6 %collective-permute-start.18 = (bf16[256,1024]{1,0:T(8,128)(2,1)S(1)}, bf16[256,1024]{1,0:T(8,128)(2,1)}, u32[]{:S(2)}, u32[]{:S(2)}) collective-permute-start(bf16[256,1024]{1,0:T(8,128)(2,1)S(1)} %stack.3.refs_0_), channel_id=1, source_target_pairs={{0,48},{1,49},{2,50},{3,51},{4,52},{5,53},{6,54},{7,55},{8,56},{9,... | collective-permute-start | bytes 1572872 | tf_op jit(solution)/shard_map/ppermute | solution.py:45
  37.3 24.0 %collective-permute-start.14 = (bf16[256,1024]{1,0:T(8,128)(2,1)S(1)}, bf16[256,1024]{1,0:T(8,128)(2,1)}, u32[]{:S(2)}, u32[]{:S(2)}) collective-permute-start(bf16[256,1024]{1,0:T(8,128)(2,1)S(1)} %stack.3.refs_0_), channel_id=1, source_target_pairs={{0,16},{1,17},{2,18},{3,19},{4,20},{5,21},{6,22},{7,23},{8,24},{9,... | collective-permute-start | bytes 1572872 | tf_op jit(solution)/shard_map/ppermute | solution.py:45
  56.7 10.6 %collective-permute-start.16 = (bf16[128,896]{1,0:T(8,128)(2,1)S(1)}, bf16[128,896]{1,0:T(8,128)(2,1)S(1)}, u32[]{:S(2)}, u32[]{:S(2)}) collective-permute-start(bf16[128,896]{1,0:T(8,128)(2,1)S(1)} %dynamic-slice_bitcast_fusion), channel_id=1, source_target_pairs={{0,1},{1,2},{2,3},{3,4},{4,5},{5,6},{6,7},{7,8},{8,9},{9,10},{10,1... | collective-permute-start | bytes 688136 | tf_op jit(solution)/shard_map/ppermute | solution.py:395
  58.6 15.9 %collective-permute-start.13 = (bf16[128,4096]{1,0:T(8,128)(2,1)}, bf16[128,4096]{1,0:T(8,128)(2,1)S(1)}, u32[]{:S(2)}, u32[]{:S(2)}) collective-permute-start(bf16[128,4096]{1,0:T(8,128)(2,1)} %collective-permute-done.12.far_ref), channel_id=1, source_target_pairs={{0,64},{64,0},{1,65},{65,1},{2,66},{66,2},{3,67},{67,3},{4,68},{68... | collective-permute-start | bytes 3145736 | tf_op jit(solution)/shard_map/ppermute | solution.py:49
  58.7 11.9 %collective-permute-start.19 = (bf16[256,1024]{1,0:T(8,128)(2,1)}, bf16[256,1024]{1,0:T(8,128)(2,1)S(1)}, u32[]{:S(2)}, u32[]{:S(2)}) collective-permute-start(bf16[256,1024]{1,0:T(8,128)(2,1)} %collective-permute-done.18.refs_2_), channel_id=1, source_target_pairs={{0,48},{1,49},{2,50},{3,51},{4,52},{5,53},{6,54},{7,55},{8,56},{9,... | collective-permute-start | bytes 1572872 | tf_op jit(solution)/shard_map/ppermute | solution.py:45
  61.3 11.0 %collective-permute-start.15 = (bf16[256,1024]{1,0:T(8,128)(2,1)S(1)}, bf16[256,1024]{1,0:T(8,128)(2,1)S(1)}, u32[]{:S(2)}, u32[]{:S(2)}) collective-permute-start(bf16[256,1024]{1,0:T(8,128)(2,1)S(1)} %broadcast_select_fusion.2), channel_id=1, source_target_pairs={{0,8},{1,9},{2,10},{3,11},{4,12},{5,13},{6,14},{7,15},{8,0},{9,1},... | collective-permute-start | bytes 1572872 | tf_op jit(solution)/shard_map/ppermute | solution.py:45
  66.1 13.6 %collective-permute-start.21 = (bf16[256,1024]{1,0:T(8,128)(2,1)}, bf16[256,1024]{1,0:T(8,128)(2,1)S(1)}, u32[]{:S(2)}, u32[]{:S(2)}) collective-permute-start(bf16[256,1024]{1,0:T(8,128)(2,1)} %collective-permute-done.8.refs_3_), channel_id=1, source_target_pairs={{0,16},{1,17},{2,18},{3,19},{4,20},{5,21},{6,22},{7,23},{8,24},{9,... | collective-permute-start | bytes 1572872 | tf_op jit(solution)/shard_map/ppermute | solution.py:45
  67.3 12.4 %collective-permute-start.22 = (bf16[256,1024]{1,0:T(8,128)(2,1)S(1)}, bf16[256,1024]{1,0:T(8,128)(2,1)S(1)}, u32[]{:S(2)}, u32[]{:S(2)}) collective-permute-start(bf16[256,1024]{1,0:T(8,128)(2,1)S(1)} %broadcast_select_fusion), channel_id=1, source_target_pairs={{0,48},{1,49},{2,50},{3,51},{4,52},{5,53},{6,54},{7,55},{8,56},{9,... | collective-permute-start | bytes 1572872 | tf_op jit(solution)/shard_map/ppermute | solution.py:45
  72.4 12.8 %collective-permute-start.20 = (bf16[256,1024]{1,0:T(8,128)(2,1)S(1)}, bf16[256,1024]{1,0:T(8,128)(2,1)S(1)}, u32[]{:S(2)}, u32[]{:S(2)}) collective-permute-start(bf16[256,1024]{1,0:T(8,128)(2,1)S(1)} %broadcast_select_fusion.1), channel_id=1, source_target_pairs={{0,48},{1,49},{2,50},{3,51},{4,52},{5,53},{6,54},{7,55},{8,56},{9,... | collective-permute-start | bytes 1572872 | tf_op jit(solution)/shard_map/ppermute | solution.py:45
  73.2 15.3 %collective-permute-start.17 = (bf16[256,1024]{1,0:T(8,128)(2,1)S(1)}, bf16[256,1024]{1,0:T(8,128)(2,1)S(1)}, u32[]{:S(2)}, u32[]{:S(2)}) collective-permute-start(bf16[256,1024]{1,0:T(8,128)(2,1)S(1)} %collective-permute-done.15.refs_0_), channel_id=1, source_target_pairs={{0,16},{1,17},{2,18},{3,19},{4,20},{5,21},{6,22},{7,23},{8,24},{9,... | collective-permute-start | bytes 1572872 | tf_op jit(solution)/shard_map/ppermute | solution.py:45
  74.5 14.1 %collective-permute-start.27 = (bf16[128,896]{1,0:T(8,128)(2,1)S(1)}, bf16[128,896]{1,0:T(8,128)(2,1)S(1)}, u32[]{:S(2)}, u32[]{:S(2)}) collective-permute-start(bf16[128,896]{1,0:T(8,128)(2,1)S(1)} %collective-permute-done.16.mine_ref), channel_id=1, source_target_pairs={{0,64},{64,0},{1,65},{65,1},{2,66},{66,2},{3,67},{67,3},{4,68},{68... | collective-permute-start | bytes 688136 | tf_op jit(solution)/shard_map/ppermute | solution.py:49
  79.8 12.1 %collective-permute-start.24 = (bf16[128,1024]{1,0:T(8,128)(2,1)S(1)}, bf16[128,1024]{1,0:T(8,128)(2,1)S(1)}, u32[]{:S(2)}, u32[]{:S(2)}) collective-permute-start(bf16[128,1024]{1,0:T(8,128)(2,1)S(1)} %slice.21), channel_id=1, source_target_pairs={{0,48},{1,49},{2,50},{3,51},{4,52},{5,53},{6,54},{7,55},{8,56},{9,... | collective-permute-start | bytes 786440 | tf_op jit(solution)/shard_map/ppermute | solution.py:45
  81.8 10.1 %collective-permute-start.23 = (bf16[128,1024]{1,0:T(8,128)(2,1)S(1)}, bf16[128,1024]{1,0:T(8,128)(2,1)S(1)}, u32[]{:S(2)}, u32[]{:S(2)}) collective-permute-start(bf16[128,1024]{1,0:T(8,128)(2,1)S(1)} %slice.20), channel_id=1, source_target_pairs={{0,16},{1,17},{2,18},{3,19},{4,20},{5,21},{6,22},{7,23},{8,24},{9,... | collective-permute-start | bytes 786440 | tf_op jit(solution)/shard_map/ppermute | solution.py:45
  88.4 7.7 %collective-permute-start.25 = (bf16[128,1024]{1,0:T(8,128)(2,1)S(1)}, bf16[128,1024]{1,0:T(8,128)(2,1)S(1)}, u32[]{:S(2)}, u32[]{:S(2)}) collective-permute-start(bf16[128,1024]{1,0:T(8,128)(2,1)S(1)} %slice.18), channel_id=1, source_target_pairs={{0,16},{1,17},{2,18},{3,19},{4,20},{5,21},{6,22},{7,23},{8,24},{9,... | collective-permute-start | bytes 786440 | tf_op jit(solution)/shard_map/ppermute | solution.py:45
  (14 other events, 105.2 us)

commit v3 on v2

--- a/solution.py
+++ b/solution.py
@@ -303,16 +303,13 @@
                         preferred_element_type=jnp.float32,
                     )
                     s_scr[h, b * SPAN : (b + 1) * SPAN, :] = jnp.where(usable[b], scores, jnp.float32(-1e30))
-
-            def soften(h, _):
+            for h in range(heads):
                 for c in range(blocks // 3):
                     r = slice(c * 3 * SPAN, (c + 1) * 3 * SPAN)
                     scores = s_scr[h, r, :]
                     weights = jnp.exp(scores - jnp.max(scores, axis=-1, keepdims=True))
                     scale = 1.0 / jnp.sum(weights, axis=-1, keepdims=True)
                     w_scr[h, r, :] = (weights * scale).astype(jnp.bfloat16)
-
-            lax.fori_loop(0, heads, soften, None)
             for h in range(heads):
                 at = slice(h * HEAD_DIM, (h + 1) * HEAD_DIM)
                 to = slice(part * half + h * HEAD_DIM, part * half + (h + 1) * HEAD_DIM)
@@ -395,27 +392,25 @@
     prev = lax.ppermute(after(prev, column_b), ("y", "xl", "z"), [(i, i + 1) for i in range(63)])
     b = [column_b, *outer_first(after(column_b, near))]
     a += outer_second(*a, *round_two)
-    keys_a = projected(0, 0, column_b)
-    values_a = projected(1, 0, keys_a, *a[1:3])
+    far_near = hop(after(far, column_b), "core")
+    keys_a = projected(0, 0, column_b, far)
+    values_a = projected(1, 0, keys_a)
     b += outer_second(*b, values_a)
-    keys_b = projected(0, 1, *b[1:3])
-    far_near = hop(after(far, *a[3:5]), "core")
-    a += outer_third(*a[3:5], keys_b)
-    values_b = projected(1, 1, *a[3:5])
-    prev_near = hop(after(prev, values_b), "core")
-    b += outer_third(*b[3:5], values_b, prev)
-    whole = gather_rows([after(normed, values_b), near, far, far_near])
-    total = partial_product(whole, [(0, [0, 1, 2], a[:3])])
-    a += outer_last(*a[5:7])
+    a += outer_third(*a[3:5], values_a)
+    whole = gather_rows([after(normed, values_a), near, far, far_near])
+    total = partial_product(whole, [(0, [0, 1, 2], a[:3]), (256, [0, 1, 2], b[:3])])
+    b += outer_third(*b[3:5], total)
+    keys_b = projected(0, 1, total)
+    prev_near = hop(after(prev, keys_b), "core")
+    a += outer_last(*a[5:7], keys_b)
+    values_b = projected(1, 1, keys_b, *b[3:5])
+    total = partial_product(
+        after(whole, values_b), [(0, [3, 4], a[3:5]), (256, [3, 4], b[3:5])], total
+    )
+    b += outer_last(*b[5:7], total)
     prev = project_prev(after(prev, total), prev_near, w_keyval)
     total = partial_product(
-        after(whole, *a[5:7]), [(256, [0, 1, 2], b[:3]), (0, [3, 4], a[3:5])], total
-    )
-    b += outer_last(*b[5:7], total)
-    total = partial_product(
-        after(whole, *b[5:7]),
-        [(256, [3, 4], b[3:5]), (0, [5, 6], a[5:7]), (256, [5, 6], b[5:7])],
-        total,
+        after(whole, prev), [(0, [5, 6], a[5:7]), (256, [5, 6], b[5:7])], total
     )
     return attend(
         nbr_lens.T,

time: 106 us -> 105 us (level); the launches traced: 104 us -> 104 us
  waiting for transfers between devices: 27.2 us -> 24.4 us
  starting transfers between devices: 38.6 us -> 40.8 us
  local copies, waits for them, and re-layouts: 6.14 us -> 7.58 us
  Pallas kernels: 29.6 us -> 28.2 us
    ppermute x23, waiting for transfers between devices: 27.2 us -> 17.5 us  [send(): return lax.ppermute(x, PLANE, pairs)]
    ppermute x1, waiting for transfers between devices: 0.01 us -> 5.75 us  [local(): lax.ppermute(after(prev, column_b), ('y', 'xl', 'z'), [(i, i + 1) for i i...]
    ppermute x1, starting transfers between devices: 1.91 us -> 5.29 us  [local(): lax.ppermute(after(prev, column_b), ('y', 'xl', 'z'), [(i, i + 1) for i i...]
    pallas_call x1, Pallas kernels: 7.87 us -> 6.1 us  [attend(): pl.pallas_call(body, out_shape=jax.ShapeDtypeStruct((rows, columns), jnp....]
    unnamed x18 -> x30, local copies, waits for them, and re-layouts: 6.04 us -> 7.48 us
    ppermute x23, starting transfers between devices: 34.5 us -> 33.3 us  [send(): return lax.ppermute(x, PLANE, pairs)]
    ppermute x4, waiting for transfers between devices: 0.01 us -> 1.18 us  [hop(): return lax.ppermute(x, axis, [(0, 1), (1, 0)])]
  transfers between devices with their start and end apart: 28 -> 28, of which waited for: 8 -> 8; matrix products, arithmetic and copies ran while one was open for 2% -> 3% of each run, Pallas kernels for 21% -> 21%
where the time goes in v3:
time: 105 us; the launch traced here: 104 us
  starting transfers between devices  40.8 us (39%)
  Pallas kernels  28.2 us (27%)
  waiting for transfers between devices  24.4 us (23%)
  local copies, waits for them, and re-layouts  7.58 us (7%)
  other arithmetic  2.93 us (3%)
    ppermute x23, starting transfers between devices, send(): return lax.ppermute(x, PLANE, pairs)  33.3 us
    ppermute x23, waiting for transfers between devices, send(): return lax.ppermute(x, PLANE, pairs)  17.5 us
    pallas_call x4, Pallas kernels, project(): pl.pallas_call(project_kernel, grid=(1,), out_shape=jax.ShapeDtypeStruct(...  9.32 us
    pallas_call x3, Pallas kernels, partial_product(): pl.pallas_call(body, out_shape=jax.ShapeDtypeStruct((rows, columns), jnp....  7.57 us
    unnamed x30, local copies, waits for them, and re-layouts  7.48 us
    pallas_call x1, Pallas kernels, attend(): pl.pallas_call(body, out_shape=jax.ShapeDtypeStruct((rows, columns), jnp....  6.1 us
    ppermute x1, waiting for transfers between devices, local(): lax.ppermute(after(prev, column_b), ('y', 'xl', 'z'), [(i, i + 1) for i i...  5.75 us
    ppermute x1, starting transfers between devices, local(): lax.ppermute(after(prev, column_b), ('y', 'xl', 'z'), [(i, i + 1) for i i...  5.29 us
  transfers between devices with their start and end apart: 28, of which 8 were waited for; matrix products, arithmetic and copies ran while one was open for 3% of the time, Pallas kernels for 21%

profile of v3, /device:TPU:2, one launch (start us, length us, event | category | flops | bytes accessed | tf_op | source)
XLA Modules:
  0.0 104.3 jit_solution(7141095028107494542)
XLA Ops:
  0.0 6.3 %collective-permute-start = (bf16[64,1024]{1,0:T(8,128)(2,1)}, bf16[64,1024]{1,0:T(8,128)(2,1)S(1)}, u32[]{:S(2)}, u32[]{:S(2)}) collective-permute-start(bf16[64,1024]{1,0:T(8,128)(2,1)} %refs_0_.1), channel_id=1, source_target_pairs={{0,6},{1,7},{2,0},{3,1},{4,2},{5,3},{6,4},{7,5},{8,14},{9,15},{10,... | collective-permute-start | bytes 393224 | tf_op jit(solution)/shard_map/ppermute | solution.py:45
  7.3 2.7 %collective-permute-start.7 = (bf16[64,1024]{1,0:T(8,128)(2,1)}, bf16[64,1024]{1,0:T(8,128)(2,1)S(1)}, u32[]{:S(2)}, u32[]{:S(2)}) collective-permute-start(bf16[64,1024]{1,0:T(8,128)(2,1)} %refs_0_.1), channel_id=1, source_target_pairs={{0,7},{1,0},{2,1},{3,2},{4,3},{5,4},{6,5},{7,6},{8,15},{9,8},{10,9... | collective-permute-start | bytes 393224 | tf_op jit(solution)/shard_map/ppermute | solution.py:45
  12.5 2.2 %collective-permute-start.6 = (bf16[128,4096]{1,0:T(8,128)(2,1)S(1)}, bf16[128,4096]{1,0:T(8,128)(2,1)}, u32[]{:S(2)}, u32[]{:S(2)}) collective-permute-start(bf16[128,4096]{1,0:T(8,128)(2,1)S(1)} %norm.1.own_ref), channel_id=1, source_target_pairs={{0,128},{128,0},{1,129},{129,1},{2,130},{130,2},{3,131},{131,3},{4... | collective-permute-start | bytes 3145736 | tf_op jit(solution)/shard_map/ppermute | solution.py:49
  19.5 3.4 %collective-permute-done.2.refs_1_ = bf16[64,1024]{1,0:T(8,128)(2,1)S(1)} collective-permute-done((bf16[64,1024]{1,0:T(8,128)(2,1)S(1)}, bf16[64,1024]{1,0:T(8,128)(2,1)S(1)}, u32[]{:S(2)}, u32[]{:S(2)}) %collective-permute-start.2) | collective-permute-done | bytes 131104 | tf_op jit(solution)/shard_map/ppermute | solution.py:45
  22.8 1.7 %collective-permute-start.12 = (bf16[256,1024]{1,0:T(8,128)(2,1)S(1)}, bf16[256,1024]{1,0:T(8,128)(2,1)}, u32[]{:S(2)}, u32[]{:S(2)}) collective-permute-start(bf16[256,1024]{1,0:T(8,128)(2,1)S(1)} %stack.3.refs_0_), channel_id=1, source_target_pairs={{0,48},{1,49},{2,50},{3,51},{4,52},{5,53},{6,54},{7,55},{8,56},{9,... | collective-permute-start | bytes 1572872 | tf_op jit(solution)/shard_map/ppermute | solution.py:45
  24.5 1.9 %collective-permute-done.3.refs_2_ = bf16[64,1024]{1,0:T(8,128)(2,1)S(1)} collective-permute-done((bf16[64,1024]{1,0:T(8,128)(2,1)S(1)}, bf16[64,1024]{1,0:T(8,128)(2,1)S(1)}, u32[]{:S(2)}, u32[]{:S(2)}) %collective-permute-start.3) | collective-permute-done | bytes 131104 | tf_op jit(solution)/shard_map/ppermute | solution.py:45
  26.4 6.2 %collective-permute-done.5.refs_3_ = bf16[64,1024]{1,0:T(8,128)(2,1)S(1)} collective-permute-done((bf16[64,1024]{1,0:T(8,128)(2,1)S(1)}, bf16[64,1024]{1,0:T(8,128)(2,1)S(1)}, u32[]{:S(2)}, u32[]{:S(2)}) %collective-permute-start.5) | collective-permute-done | bytes 131104 | tf_op jit(solution)/shard_map/ppermute | solution.py:45
  34.9 2.1 %collective-permute-start.14 = (bf16[256,1024]{1,0:T(8,128)(2,1)S(1)}, bf16[256,1024]{1,0:T(8,128)(2,1)}, u32[]{:S(2)}, u32[]{:S(2)}) collective-permute-start(bf16[256,1024]{1,0:T(8,128)(2,1)S(1)} %stack.2.refs_3_), channel_id=1, source_target_pairs={{0,48},{1,49},{2,50},{3,51},{4,52},{5,53},{6,54},{7,55},{8,56},{9,... | collective-permute-start | bytes 1572872 | tf_op jit(solution)/shard_map/ppermute | solution.py:45
  40.4 2.0 %copy-done.2 = bf16[8,256,896]{2,1,0:T(8,128)(2,1)S(1)} copy-done((bf16[8,256,896]{2,1,0:T(8,128)(2,1)S(1)}, bf16[8,256,896]{2,1,0:T(8,128)(2,1)}, u32[]{:S(2)}) %copy-start.2) | copy-done | bytes 3670040
  42.5 2.3 %project.4.refs_5_ = bf16[8,256,512]{2,1,0:T(8,128)(2,1)S(1)} custom-call(bf16[8,256,896]{2,1,0:T(8,128)(2,1)S(1)} %copy-done.2, bf16[2,896,1024]{2,1,0:T(8,128)(2,1)S(1)} %copy-done), custom_call_target="tpu_custom_call" | custom-call | flops 1879048192 | bytes 6291456 | tf_op jit(solution)/shard_map/project/pallas_call | solution.py:181
  46.1 2.3 %project.5.refs_7_ = bf16[8,256,512]{2,1,0:T(8,128)(2,1)S(1)} custom-call(bf16[8,256,896]{2,1,0:T(8,128)(2,1)S(1)} %copy-done.2, bf16[2,896,1024]{2,1,0:T(8,128)(2,1)S(1)} %copy-done), custom_call_target="tpu_custom_call" | custom-call | flops 1879048192 | bytes 6291456 | tf_op jit(solution)/shard_map/project/pallas_call | solution.py:181
  54.1 1.9 %collective-permute-start.21 = (bf16[256,1024]{1,0:T(8,128)(2,1)S(1)}, bf16[256,1024]{1,0:T(8,128)(2,1)S(1)}, u32[]{:S(2)}, u32[]{:S(2)}) collective-permute-start(bf16[256,1024]{1,0:T(8,128)(2,1)S(1)} %broadcast_select_fusion.1), channel_id=1, source_target_pairs={{0,48},{1,49},{2,50},{3,51},{4,52},{5,53},{6,54},{7,55},{8,56},{9,... | collective-permute-start | bytes 1572872 | tf_op jit(solution)/shard_map/ppermute | solution.py:45
  56.0 3.3 %rows.1.n_ref = bf16[512,4096]{1,0:T(8,128)(2,1)S(1)} custom-call(bf16[128,4096]{1,0:T(8,128)(2,1)S(1)} %norm.1.own_ref, bf16[128,4096]{1,0:T(8,128)(2,1)} %collective-permute-done.8.near_ref, bf16[128,4096]{1,0:T(8,128)(2,1)} %collective-permute-done.6.far_ref, bf16[128,4096]{1,0:T(8,128)(2,1)} %collective-permute-done.9.far_near_ref), custom_call_target="tpu_custom_call" | custom-call | bytes 8388608 | tf_op jit(solution)/shard_map/rows/pallas_call | solution.py:159
  59.4 3.3 %partial.3.refs_4_ = f32[512,1024]{1,0:T(8,128)S(1)} custom-call(bf16[512,4096]{1,0:T(8,128)(2,1)S(1)} %rows.1.n_ref, bf16[256,1024]{1,0:T(8,128)(2,1)S(1)} %stack.3.refs_0_, bf16[256,1024]{1,0:T(8,128)(2,1)S(1)} %collective-permute-done.11.refs_1_, bf16[256,1024]{1,0:T(8,128)(2,1)} %collective-permute-done.12.refs_2_, bf16[256,1024]{1,0:T(8,128)(2,1)S(1)} %stack.2.refs_3_, ...), custom_call_target="tpu_custom_call" | custom-call | flops 1610612736 | bytes 4718592 | tf_op jit(solution)/shard_map/partial/pallas_call | solution.py:247
  64.2 3.1 %collective-permute-start.23 = (bf16[256,1024]{1,0:T(8,128)(2,1)S(1)}, bf16[256,1024]{1,0:T(8,128)(2,1)S(1)}, u32[]{:S(2)}, u32[]{:S(2)}) collective-permute-start(bf16[256,1024]{1,0:T(8,128)(2,1)S(1)} %broadcast_select_fusion), channel_id=1, source_target_pairs={{0,48},{1,49},{2,50},{3,51},{4,52},{5,53},{6,54},{7,55},{8,56},{9,... | collective-permute-start | bytes 1572872 | tf_op jit(solution)/shard_map/ppermute | solution.py:45
  67.3 5.3 %collective-permute-start.10 = (bf16[128,896]{1,0:T(8,128)(2,1)S(1)}, bf16[128,896]{1,0:T(8,128)(2,1)S(1)}, u32[]{:S(2)}, u32[]{:S(2)}) collective-permute-start(bf16[128,896]{1,0:T(8,128)(2,1)S(1)} %dynamic-slice_bitcast_fusion), channel_id=1, source_target_pairs={{0,1},{1,2},{2,3},{3,4},{4,5},{5,6},{6,7},{7,8},{8,9},{9,10},{10,1... | collective-permute-start | bytes 688136 | tf_op jit(solution)/shard_map/ppermute | solution.py:392
  72.6 2.3 %project.6.refs_6_ = bf16[8,256,512]{2,1,0:T(8,128)(2,1)S(1)} custom-call(bf16[8,256,896]{2,1,0:T(8,128)(2,1)S(1)} %copy-done.3, bf16[2,896,1024]{2,1,0:T(8,128)(2,1)S(1)} %copy-done.1), custom_call_target="tpu_custom_call" | custom-call | flops 1879048192 | bytes 6291456 | tf_op jit(solution)/shard_map/project/pallas_call | solution.py:181
  75.4 2.1 %collective-permute-start.24 = (bf16[128,1024]{1,0:T(8,128)(2,1)S(1)}, bf16[128,1024]{1,0:T(8,128)(2,1)S(1)}, u32[]{:S(2)}, u32[]{:S(2)}) collective-permute-start(bf16[128,1024]{1,0:T(8,128)(2,1)S(1)} %slice.16), channel_id=1, source_target_pairs={{0,16},{1,17},{2,18},{3,19},{4,20},{5,21},{6,22},{7,23},{8,24},{9,... | collective-permute-start | bytes 786440 | tf_op jit(solution)/shard_map/ppermute | solution.py:45
  77.4 5.7 %collective-permute-done.10.mine_ref = bf16[128,896]{1,0:T(8,128)(2,1)S(1)} collective-permute-done((bf16[128,896]{1,0:T(8,128)(2,1)S(1)}, bf16[128,896]{1,0:T(8,128)(2,1)S(1)}, u32[]{:S(2)}, u32[]{:S(2)}) %collective-permute-start.10) | collective-permute-done | bytes 229408 | tf_op jit(solution)/shard_map/ppermute | solution.py:392
  83.2 2.3 %project.7.refs_8_ = bf16[8,256,512]{2,1,0:T(8,128)(2,1)S(1)} custom-call(bf16[8,256,896]{2,1,0:T(8,128)(2,1)S(1)} %copy-done.3, bf16[2,896,1024]{2,1,0:T(8,128)(2,1)S(1)} %copy-done.1), custom_call_target="tpu_custom_call" | custom-call | flops 1879048192 | bytes 6291456 | tf_op jit(solution)/shard_map/project/pallas_call | solution.py:181
  85.5 2.8 %partial.4.refs_4_ = f32[512,1024]{1,0:T(8,128)S(1)} custom-call(bf16[512,4096]{1,0:T(8,128)(2,1)S(1)} %rows.1.n_ref, bf16[256,1024]{1,0:T(8,128)(2,1)S(1)} %collective-permute-done.17.refs_0_, bf16[256,1024]{1,0:T(8,128)(2,1)} %collective-permute-done.18.refs_1_, bf16[256,1024]{1,0:T(8,128)(2,1)} %collective-permute-done.15.refs_2_, ...), custom_call_target="tpu_custom_call" | custom-call | flops 1073741824 | bytes 3145728 | tf_op jit(solution)/shard_map/partial/pallas_call | solution.py:247
  88.3 2.2 %collective-permute-start.27 = (bf16[128,1024]{1,0:T(8,128)(2,1)S(1)}, bf16[128,1024]{1,0:T(8,128)(2,1)S(1)}, u32[]{:S(2)}, u32[]{:S(2)}) collective-permute-start(bf16[128,1024]{1,0:T(8,128)(2,1)S(1)} %slice.19), channel_id=1, source_target_pairs={{0,48},{1,49},{2,50},{3,51},{4,52},{5,53},{6,54},{7,55},{8,56},{9,... | collective-permute-start | bytes 786440 | tf_op jit(solution)/shard_map/ppermute | solution.py:45
  94.8 3.4 %collective-permute-done.26.refs_2_ = bf16[128,1024]{1,0:T(8,128)(2,1)S(1)} collective-permute-done((bf16[128,1024]{1,0:T(8,128)(2,1)S(1)}, bf16[128,1024]{1,0:T(8,128)(2,1)S(1)}, u32[]{:S(2)}, u32[]{:S(2)}) %collective-permute-start.26) | collective-permute-done | bytes 262176 | tf_op jit(solution)/shard_map/ppermute | solution.py:45
  98.2 6.1 %attend.1 = bf16[512,1024]{1,0:T(8,128)(2,1)} custom-call(s32[2,512]{1,0:T(2,128)S(1)} %bitcast.7, s32[256,128]{1,0:T(8,128)S(1)} %bitcast.6, f32[512,1024]{1,0:T(8,128)S(1)} %partial.5.total_ref, bf16[512,4096]{1,0:T(8,128)(2,1)S(1)} %rows.1.n_ref, bf16[128,1024]{1,0:T(8,128)(2,1)S(1)} %collective-permute-done.24.refs_0_, ...), custom_call_target="tpu_custom_call" | custom-call | flops 6291456000 | bytes 16777216 | tf_op jit(solution)/shard_map/attend/pallas_call | solution.py:326
  (87 shorter events, 27.0 us)
Async XLA Ops:
  0.0 14.7 %collective-permute-start = (bf16[64,1024]{1,0:T(8,128)(2,1)}, bf16[64,1024]{1,0:T(8,128)(2,1)S(1)}, u32[]{:S(2)}, u32[]{:S(2)}) collective-permute-start(bf16[64,1024]{1,0:T(8,128)(2,1)} %refs_0_.1), channel_id=1, source_target_pairs={{0,6},{1,7},{2,0},{3,1},{4,2},{5,3},{6,4},{7,5},{8,14},{9,15},{10,... | collective-permute-start | bytes 393224 | tf_op jit(solution)/shard_map/ppermute | solution.py:45
  6.3 8.4 %collective-permute-start.1 = (bf16[64,1024]{1,0:T(8,128)(2,1)}, bf16[64,1024]{1,0:T(8,128)(2,1)S(1)}, u32[]{:S(2)}, u32[]{:S(2)}) collective-permute-start(bf16[64,1024]{1,0:T(8,128)(2,1)} %refs_0_.1), channel_id=1, source_target_pairs={{0,1},{1,2},{2,3},{3,4},{4,5},{5,6},{6,7},{7,0},{8,9},{9,10},{10,1... | collective-permute-start | bytes 393224 | tf_op jit(solution)/shard_map/ppermute | solution.py:45
  7.3 8.7 %collective-permute-start.4 = (bf16[64,1024]{1,0:T(8,128)(2,1)}, bf16[64,1024]{1,0:T(8,128)(2,1)S(1)}, u32[]{:S(2)}, u32[]{:S(2)}) collective-permute-start(bf16[64,1024]{1,0:T(8,128)(2,1)} %refs_0_.1), channel_id=1, source_target_pairs={{0,2},{1,3},{2,4},{3,5},{4,6},{5,7},{6,0},{7,1},{8,10},{9,11},{10,... | collective-permute-start | bytes 393224 | tf_op jit(solution)/shard_map/ppermute | solution.py:45
  7.3 8.7 %collective-permute-start.7 = (bf16[64,1024]{1,0:T(8,128)(2,1)}, bf16[64,1024]{1,0:T(8,128)(2,1)S(1)}, u32[]{:S(2)}, u32[]{:S(2)}) collective-permute-start(bf16[64,1024]{1,0:T(8,128)(2,1)} %refs_0_.1), channel_id=1, source_target_pairs={{0,7},{1,0},{2,1},{3,2},{4,3},{5,4},{6,5},{7,6},{8,15},{9,8},{10,9... | collective-permute-start | bytes 393224 | tf_op jit(solution)/shard_map/ppermute | solution.py:45
  12.5 21.2 %collective-permute-start.6 = (bf16[128,4096]{1,0:T(8,128)(2,1)S(1)}, bf16[128,4096]{1,0:T(8,128)(2,1)}, u32[]{:S(2)}, u32[]{:S(2)}) collective-permute-start(bf16[128,4096]{1,0:T(8,128)(2,1)S(1)} %norm.1.own_ref), channel_id=1, source_target_pairs={{0,128},{128,0},{1,129},{129,1},{2,130},{130,2},{3,131},{131,3},{4... | collective-permute-start | bytes 3145736 | tf_op jit(solution)/shard_map/ppermute | solution.py:49
  16.0 17.8 %collective-permute-start.8 = (bf16[128,4096]{1,0:T(8,128)(2,1)S(1)}, bf16[128,4096]{1,0:T(8,128)(2,1)}, u32[]{:S(2)}, u32[]{:S(2)}) collective-permute-start(bf16[128,4096]{1,0:T(8,128)(2,1)S(1)} %norm.1.own_ref), channel_id=1, source_target_pairs={{0,64},{64,0},{1,65},{65,1},{2,66},{66,2},{3,67},{67,3},{4,68},{68... | collective-permute-start | bytes 3145736 | tf_op jit(solution)/shard_map/ppermute | solution.py:49
  16.1 16.5 %collective-permute-start.11 = (bf16[256,1024]{1,0:T(8,128)(2,1)S(1)}, bf16[256,1024]{1,0:T(8,128)(2,1)S(1)}, u32[]{:S(2)}, u32[]{:S(2)}) collective-permute-start(bf16[256,1024]{1,0:T(8,128)(2,1)S(1)} %stack.3.refs_0_), channel_id=1, source_target_pairs={{0,16},{1,17},{2,18},{3,19},{4,20},{5,21},{6,22},{7,23},{8,24},{9,... | collective-permute-start | bytes 1572872 | tf_op jit(solution)/shard_map/ppermute | solution.py:45
  18.7 7.6 %collective-permute-start.3 = (bf16[64,1024]{1,0:T(8,128)(2,1)S(1)}, bf16[64,1024]{1,0:T(8,128)(2,1)S(1)}, u32[]{:S(2)}, u32[]{:S(2)}) collective-permute-start(bf16[64,1024]{1,0:T(8,128)(2,1)S(1)} %get-tuple-element.31.refs_0_), channel_id=1, source_target_pairs={{0,6},{1,7},{2,0},{3,1},{4,2},{5,3},{6,4},{7,5},{8,14},{9,15},{10,... | collective-permute-start | bytes 393224 | tf_op jit(solution)/shard_map/ppermute | solution.py:45
  22.8 16.5 %collective-permute-start.12 = (bf16[256,1024]{1,0:T(8,128)(2,1)S(1)}, bf16[256,1024]{1,0:T(8,128)(2,1)}, u32[]{:S(2)}, u32[]{:S(2)}) collective-permute-start(bf16[256,1024]{1,0:T(8,128)(2,1)S(1)} %stack.3.refs_0_), channel_id=1, source_target_pairs={{0,48},{1,49},{2,50},{3,51},{4,52},{5,53},{6,54},{7,55},{8,56},{9,... | collective-permute-start | bytes 1572872 | tf_op jit(solution)/shard_map/ppermute | solution.py:45
  33.8 22.2 %collective-permute-start.9 = (bf16[128,4096]{1,0:T(8,128)(2,1)}, bf16[128,4096]{1,0:T(8,128)(2,1)}, u32[]{:S(2)}, u32[]{:S(2)}) collective-permute-start(bf16[128,4096]{1,0:T(8,128)(2,1)} %collective-permute-done.6.far_ref), channel_id=1, source_target_pairs={{0,64},{64,0},{1,65},{65,1},{2,66},{66,2},{3,67},{67,3},{4,68},{68... | collective-permute-start | bytes 3145736 | tf_op jit(solution)/shard_map/ppermute | solution.py:49
  33.8 16.9 %collective-permute-start.13 = (bf16[256,1024]{1,0:T(8,128)(2,1)S(1)}, bf16[256,1024]{1,0:T(8,128)(2,1)S(1)}, u32[]{:S(2)}, u32[]{:S(2)}) collective-permute-start(bf16[256,1024]{1,0:T(8,128)(2,1)S(1)} %stack.2.refs_3_), channel_id=1, source_target_pairs={{0,16},{1,17},{2,18},{3,19},{4,20},{5,21},{6,22},{7,23},{8,24},{9,... | collective-permute-start | bytes 1572872 | tf_op jit(solution)/shard_map/ppermute | solution.py:45
  34.9 14.9 %collective-permute-start.14 = (bf16[256,1024]{1,0:T(8,128)(2,1)S(1)}, bf16[256,1024]{1,0:T(8,128)(2,1)}, u32[]{:S(2)}, u32[]{:S(2)}) collective-permute-start(bf16[256,1024]{1,0:T(8,128)(2,1)S(1)} %stack.2.refs_3_), channel_id=1, source_target_pairs={{0,48},{1,49},{2,50},{3,51},{4,52},{5,53},{6,54},{7,55},{8,56},{9,... | collective-permute-start | bytes 1572872 | tf_op jit(solution)/shard_map/ppermute | solution.py:45
  37.9 14.8 %collective-permute-start.17 = (bf16[256,1024]{1,0:T(8,128)(2,1)}, bf16[256,1024]{1,0:T(8,128)(2,1)S(1)}, u32[]{:S(2)}, u32[]{:S(2)}) collective-permute-start(bf16[256,1024]{1,0:T(8,128)(2,1)} %broadcast_select_fusion.2), channel_id=1, source_target_pairs={{0,8},{1,9},{2,10},{3,11},{4,12},{5,13},{6,14},{7,15},{8,0},{9,1},... | collective-permute-start | bytes 1572872 | tf_op jit(solution)/shard_map/ppermute | solution.py:45
  39.4 13.3 %collective-permute-start.18 = (bf16[256,1024]{1,0:T(8,128)(2,1)}, bf16[256,1024]{1,0:T(8,128)(2,1)}, u32[]{:S(2)}, u32[]{:S(2)}) collective-permute-start(bf16[256,1024]{1,0:T(8,128)(2,1)} %collective-permute-done.12.refs_2_), channel_id=1, source_target_pairs={{0,48},{1,49},{2,50},{3,51},{4,52},{5,53},{6,54},{7,55},{8,56},{9,... | collective-permute-start | bytes 1572872 | tf_op jit(solution)/shard_map/ppermute | solution.py:45
  49.8 12.9 %collective-permute-start.16 = (bf16[256,1024]{1,0:T(8,128)(2,1)}, bf16[256,1024]{1,0:T(8,128)(2,1)}, u32[]{:S(2)}, u32[]{:S(2)}) collective-permute-start(bf16[256,1024]{1,0:T(8,128)(2,1)} %collective-permute-done.14.refs_5_), channel_id=1, source_target_pairs={{0,48},{1,49},{2,50},{3,51},{4,52},{5,53},{6,54},{7,55},{8,56},{9,... | collective-permute-start | bytes 1572872 | tf_op jit(solution)/shard_map/ppermute | solution.py:45
  52.4 10.4 %collective-permute-start.15 = (bf16[256,1024]{1,0:T(8,128)(2,1)}, bf16[256,1024]{1,0:T(8,128)(2,1)}, u32[]{:S(2)}, u32[]{:S(2)}) collective-permute-start(bf16[256,1024]{1,0:T(8,128)(2,1)} %broadcast_select_fusion.3), channel_id=1, source_target_pairs={{0,8},{1,9},{2,10},{3,11},{4,12},{5,13},{6,14},{7,15},{8,0},{9,1},... | collective-permute-start | bytes 1572872 | tf_op jit(solution)/shard_map/ppermute | solution.py:45
  52.6 22.7 %collective-permute-start.20 = (bf16[256,1024]{1,0:T(8,128)(2,1)S(1)}, bf16[256,1024]{1,0:T(8,128)(2,1)S(1)}, u32[]{:S(2)}, u32[]{:S(2)}) collective-permute-start(bf16[256,1024]{1,0:T(8,128)(2,1)S(1)} %collective-permute-done.17.refs_0_), channel_id=1, source_target_pairs={{0,16},{1,17},{2,18},{3,19},{4,20},{5,21},{6,22},{7,23},{8,24},{9,... | collective-permute-start | bytes 1572872 | tf_op jit(solution)/shard_map/ppermute | solution.py:45
  54.1 20.8 %collective-permute-start.21 = (bf16[256,1024]{1,0:T(8,128)(2,1)S(1)}, bf16[256,1024]{1,0:T(8,128)(2,1)S(1)}, u32[]{:S(2)}, u32[]{:S(2)}) collective-permute-start(bf16[256,1024]{1,0:T(8,128)(2,1)S(1)} %broadcast_select_fusion.1), channel_id=1, source_target_pairs={{0,48},{1,49},{2,50},{3,51},{4,52},{5,53},{6,54},{7,55},{8,56},{9,... | collective-permute-start | bytes 1572872 | tf_op jit(solution)/shard_map/ppermute | solution.py:45
  62.7 27.8 %collective-permute-start.22 = (bf16[256,1024]{1,0:T(8,128)(2,1)}, bf16[256,1024]{1,0:T(8,128)(2,1)S(1)}, u32[]{:S(2)}, u32[]{:S(2)}) collective-permute-start(bf16[256,1024]{1,0:T(8,128)(2,1)} %collective-permute-done.15.refs_2_), channel_id=1, source_target_pairs={{0,16},{1,17},{2,18},{3,19},{4,20},{5,21},{6,22},{7,23},{8,24},{9,... | collective-permute-start | bytes 1572872 | tf_op jit(solution)/shard_map/ppermute | solution.py:45
  64.2 24.1 %collective-permute-start.23 = (bf16[256,1024]{1,0:T(8,128)(2,1)S(1)}, bf16[256,1024]{1,0:T(8,128)(2,1)S(1)}, u32[]{:S(2)}, u32[]{:S(2)}) collective-permute-start(bf16[256,1024]{1,0:T(8,128)(2,1)S(1)} %broadcast_select_fusion), channel_id=1, source_target_pairs={{0,48},{1,49},{2,50},{3,51},{4,52},{5,53},{6,54},{7,55},{8,56},{9,... | collective-permute-start | bytes 1572872 | tf_op jit(solution)/shard_map/ppermute | solution.py:45
  67.3 15.9 %collective-permute-start.10 = (bf16[128,896]{1,0:T(8,128)(2,1)S(1)}, bf16[128,896]{1,0:T(8,128)(2,1)S(1)}, u32[]{:S(2)}, u32[]{:S(2)}) collective-permute-start(bf16[128,896]{1,0:T(8,128)(2,1)S(1)} %dynamic-slice_bitcast_fusion), channel_id=1, source_target_pairs={{0,1},{1,2},{2,3},{3,4},{4,5},{5,6},{6,7},{7,8},{8,9},{9,10},{10,1... | collective-permute-start | bytes 688136 | tf_op jit(solution)/shard_map/ppermute | solution.py:392
  75.0 18.4 %collective-permute-start.25 = (bf16[128,1024]{1,0:T(8,128)(2,1)S(1)}, bf16[128,1024]{1,0:T(8,128)(2,1)S(1)}, u32[]{:S(2)}, u32[]{:S(2)}) collective-permute-start(bf16[128,1024]{1,0:T(8,128)(2,1)S(1)} %slice.17), channel_id=1, source_target_pairs={{0,48},{1,49},{2,50},{3,51},{4,52},{5,53},{6,54},{7,55},{8,56},{9,... | collective-permute-start | bytes 786440 | tf_op jit(solution)/shard_map/ppermute | solution.py:45
  75.4 18.1 %collective-permute-start.24 = (bf16[128,1024]{1,0:T(8,128)(2,1)S(1)}, bf16[128,1024]{1,0:T(8,128)(2,1)S(1)}, u32[]{:S(2)}, u32[]{:S(2)}) collective-permute-start(bf16[128,1024]{1,0:T(8,128)(2,1)S(1)} %slice.16), channel_id=1, source_target_pairs={{0,16},{1,17},{2,18},{3,19},{4,20},{5,21},{6,22},{7,23},{8,24},{9,... | collective-permute-start | bytes 786440 | tf_op jit(solution)/shard_map/ppermute | solution.py:45
  90.5 7.7 %collective-permute-start.26 = (bf16[128,1024]{1,0:T(8,128)(2,1)S(1)}, bf16[128,1024]{1,0:T(8,128)(2,1)S(1)}, u32[]{:S(2)}, u32[]{:S(2)}) collective-permute-start(bf16[128,1024]{1,0:T(8,128)(2,1)S(1)} %slice.18), channel_id=1, source_target_pairs={{0,16},{1,17},{2,18},{3,19},{4,20},{5,21},{6,22},{7,23},{8,24},{9,... | collective-permute-start | bytes 786440 | tf_op jit(solution)/shard_map/ppermute | solution.py:45
  (20 other events, 125.8 us)

commit v4 on v1

--- a/solution.py
+++ b/solution.py
@@ -168,12 +168,10 @@
 
 
 def project_kernel(states_ref, w_ref, out_ref):
-    def one(i, _):
+    for i in range(out_ref.shape[0]):
         out_ref[i] = jnp.dot(
             states_ref[i], w_ref[0], preferred_element_type=jnp.float32
         ).astype(jnp.bfloat16)
-
-    lax.fori_loop(0, out_ref.shape[0], one, None)
 
 
 def project(states, w, which, half):
@@ -372,7 +370,7 @@
         send(w_query, (-2, "z"), (2, 0)),
     ]
     normed = normalize(hidden, norm_gain[None])
-    near = hop(after(normed, *round_one), "core")
+    near = hop(normed, "core")
     far = hop(normed, "xh")
     column_a = stacked([w_query, *round_one], ((3, 1, 0, 2), (0, 3, 4, 2)))
     head = after(pick(round_one[3], round_one[0]), normed)
@@ -381,26 +379,27 @@
         send(head, (-2, "z"), (2, 0)),
         send(pick(round_one[2], round_one[0]), (1, "z"), (1, 0)),
     ]
+    column_b = stacked([head, *round_two], ((0, 1, 2, 3), (0, 1, 2, 3)))
+
     a = [column_a, *outer_first(column_a)]
-    column_b = stacked([head, *round_two], ((0, 1, 2, 3), (0, 1, 2, 3)))
     half = nbr_states.shape[1] // 2
     prev = lax.dynamic_slice_in_dim(nbr_states[-1], core * half, half, 0)
-    prev = lax.ppermute(after(prev, column_b), ("y", "xl", "z"), [(i, i + 1) for i in range(63)])
-    b = [column_b, *outer_first(after(column_b, near))]
-    a += outer_second(*a, *round_two)
-    keys_a = projected(0, 0, column_b)
-    values_a = projected(1, 0, keys_a, *a[1:3])
-    b += outer_second(*b, values_a)
+    prev = lax.ppermute(after(prev, column_a), ("y", "xl", "z"), [(i, i + 1) for i in range(63)])
+    keys_a = projected(0, 0, column_a)
+    b = [column_b, *outer_first(column_b)]
+    a += outer_second(*a, keys_a)
+    values_a = projected(1, 0, *a[1:3])
+    b += outer_second(*b, values_a, prev)
+    prev_near = hop(prev, "core")
     keys_b = projected(0, 1, *b[1:3])
-    far_near = hop(after(far, *a[3:5]), "core")
+    far_near = hop(after(far, keys_b), "core")
     a += outer_third(*a[3:5], keys_b)
     values_b = projected(1, 1, *a[3:5])
-    prev_near = hop(after(prev, values_b), "core")
-    b += outer_third(*b[3:5], values_b, prev)
-    whole = gather_rows([after(normed, values_b), near, far, far_near])
-    total = partial_product(whole, [(0, [0, 1, 2], a[:3])])
-    a += outer_last(*a[5:7])
-    prev = project_prev(after(prev, total), prev_near, w_keyval)
+    prev = project_prev(after(prev, values_b), prev_near, w_keyval)
+    whole = gather_rows([after(normed, prev), near, far, far_near])
+    b += outer_third(*b[3:5], whole)
+    total = partial_product(after(whole, *b[3:5]), [(0, [0, 1, 2], a[:3])])
+    a += outer_last(*a[5:7], total)
     total = partial_product(
         after(whole, *a[5:7]), [(256, [0, 1, 2], b[:3]), (0, [3, 4], a[3:5])], total
     )

time: 106 us -> 97 us (0.915)
  the two profiles are of different devices: /device:TPU:1 before, /device:TPU:2 now
where the time goes in v4:
time: 97 us; the launch traced here: 95.4 us
  starting transfers between devices  42.5 us (44%)
  Pallas kernels  25.3 us (26%)
  waiting for transfers between devices  20.3 us (21%)
  local copies, waits for them, and re-layouts  6.13 us (6%)
    ppermute x23, starting transfers between devices, send(): return lax.ppermute(x, PLANE, pairs)  37 us
    ppermute x23, waiting for transfers between devices, send(): return lax.ppermute(x, PLANE, pairs)  15.7 us
    pallas_call x4, Pallas kernels, project(): pl.pallas_call(project_kernel, grid=(1,), out_shape=jax.ShapeDtypeStruct(...  9.32 us
    pallas_call x1, Pallas kernels, attend(): pl.pallas_call(body, out_shape=jax.ShapeDtypeStruct((rows, columns), jnp....  6.1 us
    unnamed x16, local copies, waits for them, and re-layouts  6.04 us
    ppermute x1, waiting for transfers between devices, local(): lax.ppermute(after(prev, column_a), ('y', 'xl', 'z'), [(i, i + 1) for i i...  4.6 us
    pallas_call x3, Pallas kernels, partial_product(): pl.pallas_call(body, out_shape=jax.ShapeDtypeStruct((rows, columns), jnp....  4.31 us
    ppermute x4, starting transfers between devices, hop(): return lax.ppermute(x, axis, [(0, 1), (1, 0)])  3.52 us
  transfers between devices with their start and end apart: 28, of which 9 were waited for; matrix products, arithmetic and copies ran while one was open for 1% of the time, Pallas kernels for 20%

profile of v4, /device:TPU:2, one launch (start us, length us, event | category | flops | bytes accessed | tf_op | source)
XLA Modules:
  0.0 95.4 jit_solution(2243131017440016232)
XLA Ops:
  0.0 1.9 %collective-permute-start = (bf16[64,1024]{1,0:T(8,128)(2,1)}, bf16[64,1024]{1,0:T(8,128)(2,1)S(1)}, u32[]{:S(2)}, u32[]{:S(2)}) collective-permute-start(bf16[64,1024]{1,0:T(8,128)(2,1)} %refs_0_.1), channel_id=1, source_target_pairs={{0,1},{1,2},{2,3},{3,4},{4,5},{5,6},{6,7},{7,0},{8,9},{9,10},{10,1... | collective-permute-start | bytes 393224 | tf_op jit(solution)/shard_map/ppermute | solution.py:45
  1.9 3.3 %collective-permute-start.2 = (bf16[64,1024]{1,0:T(8,128)(2,1)}, bf16[64,1024]{1,0:T(8,128)(2,1)S(1)}, u32[]{:S(2)}, u32[]{:S(2)}) collective-permute-start(bf16[64,1024]{1,0:T(8,128)(2,1)} %refs_0_.1), channel_id=1, source_target_pairs={{0,2},{1,3},{2,4},{3,5},{4,6},{5,7},{6,0},{7,1},{8,10},{9,11},{10,... | collective-permute-start | bytes 393224 | tf_op jit(solution)/shard_map/ppermute | solution.py:45
  5.2 2.1 %collective-permute-start.3 = (bf16[64,1024]{1,0:T(8,128)(2,1)}, bf16[64,1024]{1,0:T(8,128)(2,1)S(1)}, u32[]{:S(2)}, u32[]{:S(2)}) collective-permute-start(bf16[64,1024]{1,0:T(8,128)(2,1)} %refs_0_.1), channel_id=1, source_target_pairs={{0,6},{1,7},{2,0},{3,1},{4,2},{5,3},{6,4},{7,5},{8,14},{9,15},{10,... | collective-permute-start | bytes 393224 | tf_op jit(solution)/shard_map/ppermute | solution.py:45
  11.3 2.2 %collective-permute-start.11 = (bf16[128,4096]{1,0:T(8,128)(2,1)S(1)}, bf16[128,4096]{1,0:T(8,128)(2,1)}, u32[]{:S(2)}, u32[]{:S(2)}) collective-permute-start(bf16[128,4096]{1,0:T(8,128)(2,1)S(1)} %norm.1.own_ref), channel_id=1, source_target_pairs={{0,128},{128,0},{1,129},{129,1},{2,130},{130,2},{3,131},{131,3},{4... | collective-permute-start | bytes 3145736 | tf_op jit(solution)/shard_map/ppermute | solution.py:49
  14.2 2.1 %collective-permute-start.12 = (bf16[64,1024]{1,0:T(8,128)(2,1)S(1)}, bf16[64,1024]{1,0:T(8,128)(2,1)S(1)}, u32[]{:S(2)}, u32[]{:S(2)}) collective-permute-start(bf16[64,1024]{1,0:T(8,128)(2,1)S(1)} %get-tuple-element.36.refs_0_), channel_id=1, source_target_pairs={{0,7},{1,0},{2,1},{3,2},{4,3},{5,4},{6,5},{7,6},{8,15},{9,8},{10,9... | collective-permute-start | bytes 393224 | tf_op jit(solution)/shard_map/ppermute | solution.py:45
  19.7 2.6 %collective-permute-start.13 = (bf16[64,1024]{1,0:T(8,128)(2,1)S(1)}, bf16[64,1024]{1,0:T(8,128)(2,1)S(1)}, u32[]{:S(2)}, u32[]{:S(2)}) collective-permute-start(bf16[64,1024]{1,0:T(8,128)(2,1)S(1)} %get-tuple-element.36.refs_0_), channel_id=1, source_target_pairs={{0,6},{1,7},{2,0},{3,1},{4,2},{5,3},{6,4},{7,5},{8,14},{9,15},{10,... | collective-permute-start | bytes 393224 | tf_op jit(solution)/shard_map/ppermute | solution.py:45
  23.3 4.0 %collective-permute-done.13.refs_2_ = bf16[64,1024]{1,0:T(8,128)(2,1)S(1)} collective-permute-done((bf16[64,1024]{1,0:T(8,128)(2,1)S(1)}, bf16[64,1024]{1,0:T(8,128)(2,1)S(1)}, u32[]{:S(2)}, u32[]{:S(2)}) %collective-permute-start.13) | collective-permute-done | bytes 131104 | tf_op jit(solution)/shard_map/ppermute | solution.py:45
  30.2 2.9 %collective-permute-start.16 = (bf16[256,1024]{1,0:T(8,128)(2,1)S(1)}, bf16[256,1024]{1,0:T(8,128)(2,1)S(1)}, u32[]{:S(2)}, u32[]{:S(2)}) collective-permute-start(bf16[256,1024]{1,0:T(8,128)(2,1)S(1)} %stack.3.refs_0_), channel_id=1, source_target_pairs={{0,48},{1,49},{2,50},{3,51},{4,52},{5,53},{6,54},{7,55},{8,56},{9,... | collective-permute-start | bytes 1572872 | tf_op jit(solution)/shard_map/ppermute | solution.py:45
  33.1 2.0 %copy-done = bf16[2,896,1024]{2,1,0:T(8,128)(2,1)S(1)} copy-done((bf16[2,896,1024]{2,1,0:T(8,128)(2,1)S(1)}, bf16[2,896,1024]{2,1,0:T(8,128)(2,1)}, u32[]{:S(2)}) %copy-start) | copy-done | bytes 3670040
  35.1 2.0 %copy-done.2 = bf16[8,256,896]{2,1,0:T(8,128)(2,1)S(1)} copy-done((bf16[8,256,896]{2,1,0:T(8,128)(2,1)S(1)}, bf16[8,256,896]{2,1,0:T(8,128)(2,1)}, u32[]{:S(2)}) %copy-start.2) | copy-done | bytes 3670040
  37.2 2.3 %project.4.refs_5_ = bf16[8,256,512]{2,1,0:T(8,128)(2,1)S(1)} custom-call(bf16[8,256,896]{2,1,0:T(8,128)(2,1)S(1)} %copy-done.2, bf16[2,896,1024]{2,1,0:T(8,128)(2,1)S(1)} %copy-done), custom_call_target="tpu_custom_call" | custom-call | flops 1879048192 | bytes 6291456 | tf_op jit(solution)/shard_map/project/pallas_call | solution.py:181
  39.6 1.9 %collective-permute-start.4 = (bf16[128,896]{1,0:T(8,128)(2,1)S(1)}, bf16[128,896]{1,0:T(8,128)(2,1)S(1)}, u32[]{:S(2)}, u32[]{:S(2)}) collective-permute-start(bf16[128,896]{1,0:T(8,128)(2,1)S(1)} %dynamic-slice_bitcast_fusion), channel_id=1, source_target_pairs={{0,1},{1,2},{2,3},{3,4},{4,5},{5,6},{6,7},{7,8},{8,9},{9,10},{10,1... | collective-permute-start | bytes 688136 | tf_op jit(solution)/shard_map/ppermute | solution.py:387
  43.9 2.3 %project.6.refs_6_ = bf16[8,256,512]{2,1,0:T(8,128)(2,1)S(1)} custom-call(bf16[8,256,896]{2,1,0:T(8,128)(2,1)S(1)} %copy-done.2, bf16[2,896,1024]{2,1,0:T(8,128)(2,1)S(1)} %copy-done), custom_call_target="tpu_custom_call" | custom-call | flops 1879048192 | bytes 6291456 | tf_op jit(solution)/shard_map/project/pallas_call | solution.py:181
  47.5 4.6 %collective-permute-done.4.mine_ref = bf16[128,896]{1,0:T(8,128)(2,1)S(1)} collective-permute-done((bf16[128,896]{1,0:T(8,128)(2,1)S(1)}, bf16[128,896]{1,0:T(8,128)(2,1)S(1)}, u32[]{:S(2)}, u32[]{:S(2)}) %collective-permute-start.4) | collective-permute-done | bytes 229408 | tf_op jit(solution)/shard_map/ppermute | solution.py:387
  52.1 2.3 %project.7.refs_7_ = bf16[8,256,512]{2,1,0:T(8,128)(2,1)S(1)} custom-call(bf16[8,256,896]{2,1,0:T(8,128)(2,1)S(1)} %copy-done.2, bf16[2,896,1024]{2,1,0:T(8,128)(2,1)S(1)} %copy-done), custom_call_target="tpu_custom_call" | custom-call | flops 1879048192 | bytes 6291456 | tf_op jit(solution)/shard_map/project/pallas_call | solution.py:181
  57.5 2.3 %project.5.refs_8_ = bf16[8,256,512]{2,1,0:T(8,128)(2,1)S(1)} custom-call(bf16[8,256,896]{2,1,0:T(8,128)(2,1)S(1)} %copy-done.2, bf16[2,896,1024]{2,1,0:T(8,128)(2,1)S(1)} %copy-done), custom_call_target="tpu_custom_call" | custom-call | flops 1879048192 | bytes 6291456 | tf_op jit(solution)/shard_map/project/pallas_call | solution.py:181
  61.1 1.8 %collective-permute-start.22 = (bf16[256,1024]{1,0:T(8,128)(2,1)S(1)}, bf16[256,1024]{1,0:T(8,128)(2,1)S(1)}, u32[]{:S(2)}, u32[]{:S(2)}) collective-permute-start(bf16[256,1024]{1,0:T(8,128)(2,1)S(1)} %collective-permute-done.6.refs_3_), channel_id=1, source_target_pairs={{0,16},{1,17},{2,18},{3,19},{4,20},{5,21},{6,22},{7,23},{8,24},{9,... | collective-permute-start | bytes 1572872 | tf_op jit(solution)/shard_map/ppermute | solution.py:45
  63.0 1.8 %collective-permute-start.23 = (bf16[256,1024]{1,0:T(8,128)(2,1)S(1)}, bf16[256,1024]{1,0:T(8,128)(2,1)S(1)}, u32[]{:S(2)}, u32[]{:S(2)}) collective-permute-start(bf16[256,1024]{1,0:T(8,128)(2,1)S(1)} %broadcast_select_fusion), channel_id=1, source_target_pairs={{0,48},{1,49},{2,50},{3,51},{4,52},{5,53},{6,54},{7,55},{8,56},{9,... | collective-permute-start | bytes 1572872 | tf_op jit(solution)/shard_map/ppermute | solution.py:45
  64.8 2.7 %rows.1.n_ref = bf16[512,4096]{1,0:T(8,128)(2,1)S(1)} custom-call(bf16[128,4096]{1,0:T(8,128)(2,1)S(1)} %norm.1.own_ref, bf16[128,4096]{1,0:T(8,128)(2,1)S(1)} %collective-permute-done.10.near_ref, bf16[128,4096]{1,0:T(8,128)(2,1)} %collective-permute-done.11.far_ref, bf16[128,4096]{1,0:T(8,128)(2,1)S(1)} %collective-permute-done.17.far_near_ref), custom_call_target="tpu_custom_call" | custom-call | bytes 8388608 | tf_op jit(solution)/shard_map/rows/pallas_call | solution.py:159
  69.7 2.8 %collective-permute-done.23.refs_3_ = bf16[256,1024]{1,0:T(8,128)(2,1)S(1)} collective-permute-done((bf16[256,1024]{1,0:T(8,128)(2,1)S(1)}, bf16[256,1024]{1,0:T(8,128)(2,1)S(1)}, u32[]{:S(2)}, u32[]{:S(2)}) %collective-permute-start.23) | collective-permute-done | bytes 524320 | tf_op jit(solution)/shard_map/ppermute | solution.py:45
  73.5 2.8 %collective-permute-start.25 = (bf16[128,1024]{1,0:T(8,128)(2,1)S(1)}, bf16[128,1024]{1,0:T(8,128)(2,1)S(1)}, u32[]{:S(2)}, u32[]{:S(2)}) collective-permute-start(bf16[128,1024]{1,0:T(8,128)(2,1)S(1)} %slice.17), channel_id=1, source_target_pairs={{0,48},{1,49},{2,50},{3,51},{4,52},{5,53},{6,54},{7,55},{8,56},{9,... | collective-permute-start | bytes 786440 | tf_op jit(solution)/shard_map/ppermute | solution.py:45
  78.1 3.2 %collective-permute-start.27 = (bf16[128,1024]{1,0:T(8,128)(2,1)S(1)}, bf16[128,1024]{1,0:T(8,128)(2,1)S(1)}, u32[]{:S(2)}, u32[]{:S(2)}) collective-permute-start(bf16[128,1024]{1,0:T(8,128)(2,1)S(1)} %slice.19), channel_id=1, source_target_pairs={{0,48},{1,49},{2,50},{3,51},{4,52},{5,53},{6,54},{7,55},{8,56},{9,... | collective-permute-start | bytes 786440 | tf_op jit(solution)/shard_map/ppermute | solution.py:45
  85.2 4.1 %collective-permute-done.26.refs_2_ = bf16[128,1024]{1,0:T(8,128)(2,1)S(1)} collective-permute-done((bf16[128,1024]{1,0:T(8,128)(2,1)S(1)}, bf16[128,1024]{1,0:T(8,128)(2,1)S(1)}, u32[]{:S(2)}, u32[]{:S(2)}) %collective-permute-start.26) | collective-permute-done | bytes 262176 | tf_op jit(solution)/shard_map/ppermute | solution.py:45
  89.3 6.1 %attend.1 = bf16[512,1024]{1,0:T(8,128)(2,1)} custom-call(s32[2,512]{1,0:T(2,128)S(1)} %bitcast.7, s32[256,128]{1,0:T(8,128)S(1)} %bitcast.6, f32[512,1024]{1,0:T(8,128)S(1)} %partial.5.total_ref, bf16[512,4096]{1,0:T(8,128)(2,1)S(1)} %rows.1.n_ref, bf16[128,1024]{1,0:T(8,128)(2,1)S(1)} %collective-permute-done.24.refs_0_, ...), custom_call_target="tpu_custom_call" | custom-call | flops 6291456000 | bytes 16777216 | tf_op jit(solution)/shard_map/attend/pallas_call | solution.py:320
  (73 shorter events, 28.8 us)
Async XLA Ops:
  0.0 13.5 %collective-permute-start = (bf16[64,1024]{1,0:T(8,128)(2,1)}, bf16[64,1024]{1,0:T(8,128)(2,1)S(1)}, u32[]{:S(2)}, u32[]{:S(2)}) collective-permute-start(bf16[64,1024]{1,0:T(8,128)(2,1)} %refs_0_.1), channel_id=1, source_target_pairs={{0,1},{1,2},{2,3},{3,4},{4,5},{5,6},{6,7},{7,0},{8,9},{9,10},{10,1... | collective-permute-start | bytes 393224 | tf_op jit(solution)/shard_map/ppermute | solution.py:45
  1.9 11.6 %collective-permute-start.2 = (bf16[64,1024]{1,0:T(8,128)(2,1)}, bf16[64,1024]{1,0:T(8,128)(2,1)S(1)}, u32[]{:S(2)}, u32[]{:S(2)}) collective-permute-start(bf16[64,1024]{1,0:T(8,128)(2,1)} %refs_0_.1), channel_id=1, source_target_pairs={{0,2},{1,3},{2,4},{3,5},{4,6},{5,7},{6,0},{7,1},{8,10},{9,11},{10,... | collective-permute-start | bytes 393224 | tf_op jit(solution)/shard_map/ppermute | solution.py:45
  5.2 8.4 %collective-permute-start.3 = (bf16[64,1024]{1,0:T(8,128)(2,1)}, bf16[64,1024]{1,0:T(8,128)(2,1)S(1)}, u32[]{:S(2)}, u32[]{:S(2)}) collective-permute-start(bf16[64,1024]{1,0:T(8,128)(2,1)} %refs_0_.1), channel_id=1, source_target_pairs={{0,6},{1,7},{2,0},{3,1},{4,2},{5,3},{6,4},{7,5},{8,14},{9,15},{10,... | collective-permute-start | bytes 393224 | tf_op jit(solution)/shard_map/ppermute | solution.py:45
  7.3 9.1 %collective-permute-start.1 = (bf16[64,1024]{1,0:T(8,128)(2,1)}, bf16[64,1024]{1,0:T(8,128)(2,1)S(1)}, u32[]{:S(2)}, u32[]{:S(2)}) collective-permute-start(bf16[64,1024]{1,0:T(8,128)(2,1)} %refs_0_.1), channel_id=1, source_target_pairs={{0,7},{1,0},{2,1},{3,2},{4,3},{5,4},{6,5},{7,6},{8,15},{9,8},{10,9... | collective-permute-start | bytes 393224 | tf_op jit(solution)/shard_map/ppermute | solution.py:45
  11.3 34.9 %collective-permute-start.11 = (bf16[128,4096]{1,0:T(8,128)(2,1)S(1)}, bf16[128,4096]{1,0:T(8,128)(2,1)}, u32[]{:S(2)}, u32[]{:S(2)}) collective-permute-start(bf16[128,4096]{1,0:T(8,128)(2,1)S(1)} %norm.1.own_ref), channel_id=1, source_target_pairs={{0,128},{128,0},{1,129},{129,1},{2,130},{130,2},{3,131},{131,3},{4... | collective-permute-start | bytes 3145736 | tf_op jit(solution)/shard_map/ppermute | solution.py:49
  14.2 8.1 %collective-permute-start.12 = (bf16[64,1024]{1,0:T(8,128)(2,1)S(1)}, bf16[64,1024]{1,0:T(8,128)(2,1)S(1)}, u32[]{:S(2)}, u32[]{:S(2)}) collective-permute-start(bf16[64,1024]{1,0:T(8,128)(2,1)S(1)} %get-tuple-element.36.refs_0_), channel_id=1, source_target_pairs={{0,7},{1,0},{2,1},{3,2},{4,3},{5,4},{6,5},{7,6},{8,15},{9,8},{10,9... | collective-permute-start | bytes 393224 | tf_op jit(solution)/shard_map/ppermute | solution.py:45
  16.4 23.1 %collective-permute-start.5 = (bf16[256,1024]{1,0:T(8,128)(2,1)S(1)}, bf16[256,1024]{1,0:T(8,128)(2,1)S(1)}, u32[]{:S(2)}, u32[]{:S(2)}) collective-permute-start(bf16[256,1024]{1,0:T(8,128)(2,1)S(1)} %stack.2.refs_0_), channel_id=1, source_target_pairs={{0,16},{1,17},{2,18},{3,19},{4,20},{5,21},{6,22},{7,23},{8,24},{9,... | collective-permute-start | bytes 1572872 | tf_op jit(solution)/shard_map/ppermute | solution.py:45
  18.1 21.5 %collective-permute-start.7 = (bf16[256,1024]{1,0:T(8,128)(2,1)S(1)}, bf16[256,1024]{1,0:T(8,128)(2,1)S(1)}, u32[]{:S(2)}, u32[]{:S(2)}) collective-permute-start(bf16[256,1024]{1,0:T(8,128)(2,1)S(1)} %stack.2.refs_0_), channel_id=1, source_target_pairs={{0,48},{1,49},{2,50},{3,51},{4,52},{5,53},{6,54},{7,55},{8,56},{9,... | collective-permute-start | bytes 1572872 | tf_op jit(solution)/shard_map/ppermute | solution.py:45
  29.7 11.9 %collective-permute-start.15 = (bf16[256,1024]{1,0:T(8,128)(2,1)S(1)}, bf16[256,1024]{1,0:T(8,128)(2,1)S(1)}, u32[]{:S(2)}, u32[]{:S(2)}) collective-permute-start(bf16[256,1024]{1,0:T(8,128)(2,1)S(1)} %stack.3.refs_0_), channel_id=1, source_target_pairs={{0,16},{1,17},{2,18},{3,19},{4,20},{5,21},{6,22},{7,23},{8,24},{9,... | collective-permute-start | bytes 1572872 | tf_op jit(solution)/shard_map/ppermute | solution.py:45
  30.2 12.9 %collective-permute-start.16 = (bf16[256,1024]{1,0:T(8,128)(2,1)S(1)}, bf16[256,1024]{1,0:T(8,128)(2,1)S(1)}, u32[]{:S(2)}, u32[]{:S(2)}) collective-permute-start(bf16[256,1024]{1,0:T(8,128)(2,1)S(1)} %stack.3.refs_0_), channel_id=1, source_target_pairs={{0,48},{1,49},{2,50},{3,51},{4,52},{5,53},{6,54},{7,55},{8,56},{9,... | collective-permute-start | bytes 1572872 | tf_op jit(solution)/shard_map/ppermute | solution.py:45
  39.5 23.5 %collective-permute-start.10 = (bf16[128,4096]{1,0:T(8,128)(2,1)S(1)}, bf16[128,4096]{1,0:T(8,128)(2,1)S(1)}, u32[]{:S(2)}, u32[]{:S(2)}) collective-permute-start(bf16[128,4096]{1,0:T(8,128)(2,1)S(1)} %norm.1.own_ref), channel_id=1, source_target_pairs={{0,64},{64,0},{1,65},{65,1},{2,66},{66,2},{3,67},{67,3},{4,68},{68... | collective-permute-start | bytes 3145736 | tf_op jit(solution)/shard_map/ppermute | solution.py:49
  39.6 12.5 %collective-permute-start.4 = (bf16[128,896]{1,0:T(8,128)(2,1)S(1)}, bf16[128,896]{1,0:T(8,128)(2,1)S(1)}, u32[]{:S(2)}, u32[]{:S(2)}) collective-permute-start(bf16[128,896]{1,0:T(8,128)(2,1)S(1)} %dynamic-slice_bitcast_fusion), channel_id=1, source_target_pairs={{0,1},{1,2},{2,3},{3,4},{4,5},{5,6},{6,7},{7,8},{8,9},{9,10},{10,1... | collective-permute-start | bytes 688136 | tf_op jit(solution)/shard_map/ppermute | solution.py:387
  41.6 14.4 %collective-permute-start.6 = (bf16[256,1024]{1,0:T(8,128)(2,1)S(1)}, bf16[256,1024]{1,0:T(8,128)(2,1)S(1)}, u32[]{:S(2)}, u32[]{:S(2)}) collective-permute-start(bf16[256,1024]{1,0:T(8,128)(2,1)S(1)} %broadcast_select_fusion.3), channel_id=1, source_target_pairs={{0,8},{1,9},{2,10},{3,11},{4,12},{5,13},{6,14},{7,15},{8,0},{9,1},... | collective-permute-start | bytes 1572872 | tf_op jit(solution)/shard_map/ppermute | solution.py:45
  43.1 14.1 %collective-permute-start.8 = (bf16[256,1024]{1,0:T(8,128)(2,1)S(1)}, bf16[256,1024]{1,0:T(8,128)(2,1)S(1)}, u32[]{:S(2)}, u32[]{:S(2)}) collective-permute-start(bf16[256,1024]{1,0:T(8,128)(2,1)S(1)} %collective-permute-done.7.refs_2_), channel_id=1, source_target_pairs={{0,48},{1,49},{2,50},{3,51},{4,52},{5,53},{6,54},{7,55},{8,56},{9,... | collective-permute-start | bytes 1572872 | tf_op jit(solution)/shard_map/ppermute | solution.py:45
  46.3 18.6 %collective-permute-start.17 = (bf16[128,4096]{1,0:T(8,128)(2,1)}, bf16[128,4096]{1,0:T(8,128)(2,1)S(1)}, u32[]{:S(2)}, u32[]{:S(2)}) collective-permute-start(bf16[128,4096]{1,0:T(8,128)(2,1)} %collective-permute-done.11.far_ref), channel_id=1, source_target_pairs={{0,64},{64,0},{1,65},{65,1},{2,66},{66,2},{3,67},{67,3},{4,68},{68... | collective-permute-start | bytes 3145736 | tf_op jit(solution)/shard_map/ppermute | solution.py:49
  52.1 7.8 %collective-permute-start.9 = (bf16[128,896]{1,0:T(8,128)(2,1)S(1)}, bf16[128,896]{1,0:T(8,128)(2,1)S(1)}, u32[]{:S(2)}, u32[]{:S(2)}) collective-permute-start(bf16[128,896]{1,0:T(8,128)(2,1)S(1)} %collective-permute-done.4.mine_ref), channel_id=1, source_target_pairs={{0,64},{64,0},{1,65},{65,1},{2,66},{66,2},{3,67},{67,3},{4,68},{68... | collective-permute-start | bytes 688136 | tf_op jit(solution)/shard_map/ppermute | solution.py:49
  56.0 11.6 %collective-permute-start.18 = (bf16[256,1024]{1,0:T(8,128)(2,1)S(1)}, bf16[256,1024]{1,0:T(8,128)(2,1)S(1)}, u32[]{:S(2)}, u32[]{:S(2)}) collective-permute-start(bf16[256,1024]{1,0:T(8,128)(2,1)S(1)} %broadcast_select_fusion.2), channel_id=1, source_target_pairs={{0,8},{1,9},{2,10},{3,11},{4,12},{5,13},{6,14},{7,15},{8,0},{9,1},... | collective-permute-start | bytes 1572872 | tf_op jit(solution)/shard_map/ppermute | solution.py:45
  57.2 10.3 %collective-permute-start.20 = (bf16[256,1024]{1,0:T(8,128)(2,1)S(1)}, bf16[256,1024]{1,0:T(8,128)(2,1)S(1)}, u32[]{:S(2)}, u32[]{:S(2)}) collective-permute-start(bf16[256,1024]{1,0:T(8,128)(2,1)S(1)} %collective-permute-done.16.refs_2_), channel_id=1, source_target_pairs={{0,48},{1,49},{2,50},{3,51},{4,52},{5,53},{6,54},{7,55},{8,56},{9,... | collective-permute-start | bytes 1572872 | tf_op jit(solution)/shard_map/ppermute | solution.py:45
  61.1 11.4 %collective-permute-start.22 = (bf16[256,1024]{1,0:T(8,128)(2,1)S(1)}, bf16[256,1024]{1,0:T(8,128)(2,1)S(1)}, u32[]{:S(2)}, u32[]{:S(2)}) collective-permute-start(bf16[256,1024]{1,0:T(8,128)(2,1)S(1)} %collective-permute-done.6.refs_3_), channel_id=1, source_target_pairs={{0,16},{1,17},{2,18},{3,19},{4,20},{5,21},{6,22},{7,23},{8,24},{9,... | collective-permute-start | bytes 1572872 | tf_op jit(solution)/shard_map/ppermute | solution.py:45
  63.0 9.5 %collective-permute-start.23 = (bf16[256,1024]{1,0:T(8,128)(2,1)S(1)}, bf16[256,1024]{1,0:T(8,128)(2,1)S(1)}, u32[]{:S(2)}, u32[]{:S(2)}) collective-permute-start(bf16[256,1024]{1,0:T(8,128)(2,1)S(1)} %broadcast_select_fusion), channel_id=1, source_target_pairs={{0,48},{1,49},{2,50},{3,51},{4,52},{5,53},{6,54},{7,55},{8,56},{9,... | collective-permute-start | bytes 1572872 | tf_op jit(solution)/shard_map/ppermute | solution.py:45
  67.6 10.5 %collective-permute-start.21 = (bf16[256,1024]{1,0:T(8,128)(2,1)S(1)}, bf16[256,1024]{1,0:T(8,128)(2,1)S(1)}, u32[]{:S(2)}, u32[]{:S(2)}) collective-permute-start(bf16[256,1024]{1,0:T(8,128)(2,1)S(1)} %broadcast_select_fusion.1), channel_id=1, source_target_pairs={{0,48},{1,49},{2,50},{3,51},{4,52},{5,53},{6,54},{7,55},{8,56},{9,... | collective-permute-start | bytes 1572872 | tf_op jit(solution)/shard_map/ppermute | solution.py:45
  68.0 13.3 %collective-permute-start.19 = (bf16[256,1024]{1,0:T(8,128)(2,1)S(1)}, bf16[256,1024]{1,0:T(8,128)(2,1)S(1)}, u32[]{:S(2)}, u32[]{:S(2)}) collective-permute-start(bf16[256,1024]{1,0:T(8,128)(2,1)S(1)} %collective-permute-done.18.refs_0_), channel_id=1, source_target_pairs={{0,16},{1,17},{2,18},{3,19},{4,20},{5,21},{6,22},{7,23},{8,24},{9,... | collective-permute-start | bytes 1572872 | tf_op jit(solution)/shard_map/ppermute | solution.py:45
  73.5 10.0 %collective-permute-start.25 = (bf16[128,1024]{1,0:T(8,128)(2,1)S(1)}, bf16[128,1024]{1,0:T(8,128)(2,1)S(1)}, u32[]{:S(2)}, u32[]{:S(2)}) collective-permute-start(bf16[128,1024]{1,0:T(8,128)(2,1)S(1)} %slice.17), channel_id=1, source_target_pairs={{0,48},{1,49},{2,50},{3,51},{4,52},{5,53},{6,54},{7,55},{8,56},{9,... | collective-permute-start | bytes 786440 | tf_op jit(solution)/shard_map/ppermute | solution.py:45
  81.3 7.9 %collective-permute-start.26 = (bf16[128,1024]{1,0:T(8,128)(2,1)S(1)}, bf16[128,1024]{1,0:T(8,128)(2,1)S(1)}, u32[]{:S(2)}, u32[]{:S(2)}) collective-permute-start(bf16[128,1024]{1,0:T(8,128)(2,1)S(1)} %slice.18), channel_id=1, source_target_pairs={{0,16},{1,17},{2,18},{3,19},{4,20},{5,21},{6,22},{7,23},{8,24},{9,... | collective-permute-start | bytes 786440 | tf_op jit(solution)/shard_map/ppermute | solution.py:45
  (13 other events, 83.4 us)

commit v5 on v4

--- a/solution.py
+++ b/solution.py
@@ -370,7 +370,7 @@
         send(w_query, (-2, "z"), (2, 0)),
     ]
     normed = normalize(hidden, norm_gain[None])
-    near = hop(normed, "core")
+    near = hop(after(normed, *round_one), "core")
     far = hop(normed, "xh")
     column_a = stacked([w_query, *round_one], ((3, 1, 0, 2), (0, 3, 4, 2)))
     head = after(pick(round_one[3], round_one[0]), normed)
@@ -384,25 +384,25 @@
     a = [column_a, *outer_first(column_a)]
     half = nbr_states.shape[1] // 2
     prev = lax.dynamic_slice_in_dim(nbr_states[-1], core * half, half, 0)
-    prev = lax.ppermute(after(prev, column_a), ("y", "xl", "z"), [(i, i + 1) for i in range(63)])
-    keys_a = projected(0, 0, column_a)
-    b = [column_b, *outer_first(column_b)]
-    a += outer_second(*a, keys_a)
-    values_a = projected(1, 0, *a[1:3])
-    b += outer_second(*b, values_a, prev)
-    prev_near = hop(prev, "core")
+    prev = lax.ppermute(after(prev, column_b), ("y", "xl", "z"), [(i, i + 1) for i in range(63)])
+    keys_a = projected(0, 0, column_b, *a[1:3])
+    b = [column_b, *outer_first(after(column_b, near))]
+    a += outer_second(*a)
+    values_a = projected(1, 0, keys_a, *a[1:3])
+    b += outer_second(*b, values_a)
     keys_b = projected(0, 1, *b[1:3])
     far_near = hop(after(far, keys_b), "core")
     a += outer_third(*a[3:5], keys_b)
     values_b = projected(1, 1, *a[3:5])
-    prev = project_prev(after(prev, values_b), prev_near, w_keyval)
-    whole = gather_rows([after(normed, prev), near, far, far_near])
+    whole = gather_rows([after(normed, values_b), near, far, far_near])
     b += outer_third(*b[3:5], whole)
     total = partial_product(after(whole, *b[3:5]), [(0, [0, 1, 2], a[:3])])
     a += outer_last(*a[5:7], total)
     total = partial_product(
         after(whole, *a[5:7]), [(256, [0, 1, 2], b[:3]), (0, [3, 4], a[3:5])], total
     )
+    prev_near = hop(after(prev, total), "core")
+    prev = project_prev(prev, prev_near, w_keyval)
     b += outer_last(*b[5:7], total)
     total = partial_product(
         after(whole, *b[5:7]),

time: 97 us -> 112 us (1.15); the launches traced: 95.4 us -> 112 us
  waiting for transfers between devices: 20.3 us -> 28.6 us
  local copies, waits for them, and re-layouts: 6.13 us -> 10.9 us
  other arithmetic: 0.91 us -> 3.03 us
  Pallas kernels: 25.3 us -> 27.3 us
    ppermute x23, waiting for transfers between devices: 15.7 us -> 24.5 us  [send(): return lax.ppermute(x, PLANE, pairs)]
    unnamed x16 -> x44, local copies, waits for them, and re-layouts: 6.04 us -> 10.8 us
    pallas_call x3, Pallas kernels: 4.31 us -> 6.85 us  [partial_product(): pl.pallas_call(body, out_shape=jax.ShapeDtypeStruct((rows, columns), jnp....]
    select_n x5, other arithmetic: 0.91 us -> 3.03 us  [pick(): return jnp.where(core == 0, zero, one)]
    ppermute x1, starting transfers between devices: 1.92 us -> 3.8 us  [local(): lax.ppermute(after(prev, column_b), ('y', 'xl', 'z'), [(i, i + 1) for i i...]
    ppermute x4, starting transfers between devices: 3.52 us -> 2.22 us  [hop(): return lax.ppermute(x, axis, [(0, 1), (1, 0)])]
    ppermute x23, starting transfers between devices: 37 us -> 35.7 us  [send(): return lax.ppermute(x, PLANE, pairs)]
  transfers between devices with their start and end apart: 28 -> 28, of which waited for: 9 -> 10; matrix products, arithmetic and copies ran while one was open for 1% -> 3% of each run, Pallas kernels for 20% -> 19%
where the time goes in v5:
time: 112 us
  starting transfers between devices  41.8 us (37%)
  waiting for transfers between devices  28.6 us (26%)
  Pallas kernels  27.3 us (24%)
  local copies, waits for them, and re-layouts  10.9 us (10%)
  other arithmetic  3.03 us (3%)
    ppermute x23, starting transfers between devices, send(): return lax.ppermute(x, PLANE, pairs)  35.7 us
    ppermute x23, waiting for transfers between devices, send(): return lax.ppermute(x, PLANE, pairs)  24.5 us
    unnamed x44, local copies, waits for them, and re-layouts  10.8 us
    pallas_call x4, Pallas kernels, project(): pl.pallas_call(project_kernel, grid=(1,), out_shape=jax.ShapeDtypeStruct(...  9.32 us
    pallas_call x3, Pallas kernels, partial_product(): pl.pallas_call(body, out_shape=jax.ShapeDtypeStruct((rows, columns), jnp....  6.85 us
    pallas_call x1, Pallas kernels, attend(): pl.pallas_call(body, out_shape=jax.ShapeDtypeStruct((rows, columns), jnp....  6.1 us
    ppermute x1, waiting for transfers between devices, local(): lax.ppermute(after(prev, column_b), ('y', 'xl', 'z'), [(i, i + 1) for i i...  4.08 us
    ppermute x1, starting transfers between devices, local(): lax.ppermute(after(prev, column_b), ('y', 'xl', 'z'), [(i, i + 1) for i i...  3.8 us
  transfers between devices with their start and end apart: 28, of which 10 were waited for; matrix products, arithmetic and copies ran while one was open for 3% of the time, Pallas kernels for 19%

profile of v5, /device:TPU:2, one launch (start us, length us, event | category | flops | bytes accessed | tf_op | source)
XLA Modules:
  0.0 111.9 jit_solution(11604861991175805429)
XLA Ops:
  1.9 3.3 %collective-permute-start.2 = (bf16[64,1024]{1,0:T(8,128)(2,1)}, bf16[64,1024]{1,0:T(8,128)(2,1)S(1)}, u32[]{:S(2)}, u32[]{:S(2)}) collective-permute-start(bf16[64,1024]{1,0:T(8,128)(2,1)} %refs_0_.1), channel_id=1, source_target_pairs={{0,2},{1,3},{2,4},{3,5},{4,6},{5,7},{6,0},{7,1},{8,10},{9,11},{10,... | collective-permute-start | bytes 393224 | tf_op jit(solution)/shard_map/ppermute | solution.py:45
  5.2 2.1 %collective-permute-start.3 = (bf16[64,1024]{1,0:T(8,128)(2,1)}, bf16[64,1024]{1,0:T(8,128)(2,1)S(1)}, u32[]{:S(2)}, u32[]{:S(2)}) collective-permute-start(bf16[64,1024]{1,0:T(8,128)(2,1)} %refs_0_.1), channel_id=1, source_target_pairs={{0,6},{1,7},{2,0},{3,1},{4,2},{5,3},{6,4},{7,5},{8,14},{9,15},{10,... | collective-permute-start | bytes 393224 | tf_op jit(solution)/shard_map/ppermute | solution.py:45
  14.3 2.3 %collective-permute-start.10 = (bf16[64,1024]{1,0:T(8,128)(2,1)S(1)}, bf16[64,1024]{1,0:T(8,128)(2,1)S(1)}, u32[]{:S(2)}, u32[]{:S(2)}) collective-permute-start(bf16[64,1024]{1,0:T(8,128)(2,1)S(1)} %get-tuple-element.32.refs_0_), channel_id=1, source_target_pairs={{0,7},{1,0},{2,1},{3,2},{4,3},{5,4},{6,5},{7,6},{8,15},{9,8},{10,9... | collective-permute-start | bytes 393224 | tf_op jit(solution)/shard_map/ppermute | solution.py:45
  16.6 2.1 %collective-permute-start.9 = (bf16[128,4096]{1,0:T(8,128)(2,1)S(1)}, bf16[128,4096]{1,0:T(8,128)(2,1)}, u32[]{:S(2)}, u32[]{:S(2)}) collective-permute-start(bf16[128,4096]{1,0:T(8,128)(2,1)S(1)} %norm.1.own_ref), channel_id=1, source_target_pairs={{0,128},{128,0},{1,129},{129,1},{2,130},{130,2},{3,131},{131,3},{4... | collective-permute-start | bytes 3145736 | tf_op jit(solution)/shard_map/ppermute | solution.py:49
  23.6 7.2 %collective-permute-done.11.refs_2_ = bf16[64,1024]{1,0:T(8,128)(2,1)S(1)} collective-permute-done((bf16[64,1024]{1,0:T(8,128)(2,1)S(1)}, bf16[64,1024]{1,0:T(8,128)(2,1)S(1)}, u32[]{:S(2)}, u32[]{:S(2)}) %collective-permute-start.11) | collective-permute-done | bytes 131104 | tf_op jit(solution)/shard_map/ppermute | solution.py:45
  30.9 6.1 %collective-permute-done.12.refs_3_ = bf16[64,1024]{1,0:T(8,128)(2,1)S(1)} collective-permute-done((bf16[64,1024]{1,0:T(8,128)(2,1)S(1)}, bf16[64,1024]{1,0:T(8,128)(2,1)S(1)}, u32[]{:S(2)}, u32[]{:S(2)}) %collective-permute-start.12) | collective-permute-done | bytes 131104 | tf_op jit(solution)/shard_map/ppermute | solution.py:45
  41.4 3.2 %collective-permute-start.7 = (bf16[256,1024]{1,0:T(8,128)(2,1)}, bf16[256,1024]{1,0:T(8,128)(2,1)}, u32[]{:S(2)}, u32[]{:S(2)}) collective-permute-start(bf16[256,1024]{1,0:T(8,128)(2,1)} %collective-permute-done.6.refs_2_), channel_id=1, source_target_pairs={{0,48},{1,49},{2,50},{3,51},{4,52},{5,53},{6,54},{7,55},{8,56},{9,... | collective-permute-start | bytes 1572872 | tf_op jit(solution)/shard_map/ppermute | solution.py:45
  46.4 2.6 %collective-permute-done.13.refs_1_ = bf16[256,1024]{1,0:T(8,128)(2,1)S(1)} collective-permute-done((bf16[256,1024]{1,0:T(8,128)(2,1)S(1)}, bf16[256,1024]{1,0:T(8,128)(2,1)S(1)}, u32[]{:S(2)}, u32[]{:S(2)}) %collective-permute-start.13) | collective-permute-done | bytes 524320 | tf_op jit(solution)/shard_map/ppermute | solution.py:45
  49.0 2.0 %copy-done.3 = bf16[8,256,896]{2,1,0:T(8,128)(2,1)S(1)} copy-done((bf16[8,256,896]{2,1,0:T(8,128)(2,1)S(1)}, bf16[8,256,896]{2,1,0:T(8,128)(2,1)}, u32[]{:S(2)}) %copy-start.3) | copy-done | bytes 3670040
  51.1 2.3 %project.5.refs_6_ = bf16[8,256,512]{2,1,0:T(8,128)(2,1)S(1)} custom-call(bf16[8,256,896]{2,1,0:T(8,128)(2,1)S(1)} %copy-done.3, bf16[2,896,1024]{2,1,0:T(8,128)(2,1)S(1)} %copy-done), custom_call_target="tpu_custom_call" | custom-call | flops 1879048192 | bytes 6291456 | tf_op jit(solution)/shard_map/project/pallas_call | solution.py:181
  53.6 2.3 %project.6.refs_5_ = bf16[8,256,512]{2,1,0:T(8,128)(2,1)S(1)} custom-call(bf16[8,256,896]{2,1,0:T(8,128)(2,1)S(1)} %copy-done.3, bf16[2,896,1024]{2,1,0:T(8,128)(2,1)S(1)} %copy-done), custom_call_target="tpu_custom_call" | custom-call | flops 1879048192 | bytes 6291456 | tf_op jit(solution)/shard_map/project/pallas_call | solution.py:181
  57.2 2.3 %project.7.refs_7_ = bf16[8,256,512]{2,1,0:T(8,128)(2,1)S(1)} custom-call(bf16[8,256,896]{2,1,0:T(8,128)(2,1)S(1)} %copy-done.3, bf16[2,896,1024]{2,1,0:T(8,128)(2,1)S(1)} %copy-done), custom_call_target="tpu_custom_call" | custom-call | flops 1879048192 | bytes 6291456 | tf_op jit(solution)/shard_map/project/pallas_call | solution.py:181
  68.2 2.0 %copy-done.1 = bf16[2,896,1024]{2,1,0:T(8,128)(2,1)S(1)} copy-done((bf16[2,896,1024]{2,1,0:T(8,128)(2,1)S(1)}, bf16[2,896,1024]{2,1,0:T(8,128)(2,1)}, u32[]{:S(2)}) %copy-start.1) | copy-done | bytes 3670040
  70.2 2.0 %copy-done.4 = bf16[8,256,896]{2,1,0:T(8,128)(2,1)S(1)} copy-done((bf16[8,256,896]{2,1,0:T(8,128)(2,1)S(1)}, bf16[8,256,896]{2,1,0:T(8,128)(2,1)}, u32[]{:S(2)}) %copy-start.4) | copy-done | bytes 3670040
  72.2 2.3 %project.4.refs_8_ = bf16[8,256,512]{2,1,0:T(8,128)(2,1)S(1)} custom-call(bf16[8,256,896]{2,1,0:T(8,128)(2,1)S(1)} %copy-done.4, bf16[2,896,1024]{2,1,0:T(8,128)(2,1)S(1)} %copy-done.1), custom_call_target="tpu_custom_call" | custom-call | flops 1879048192 | bytes 6291456 | tf_op jit(solution)/shard_map/project/pallas_call | solution.py:181
  74.6 3.1 %rows.1.n_ref = bf16[512,4096]{1,0:T(8,128)(2,1)S(1)} custom-call(bf16[128,4096]{1,0:T(8,128)(2,1)S(1)} %norm.1.own_ref, bf16[128,4096]{1,0:T(8,128)(2,1)S(1)} %copy-done.17, bf16[128,4096]{1,0:T(8,128)(2,1)} %collective-permute-done.9.far_ref, bf16[128,4096]{1,0:T(8,128)(2,1)} %collective-permute-done.15.far_near_ref), custom_call_target="tpu_custom_call" | custom-call | bytes 8388608 | tf_op jit(solution)/shard_map/rows/pallas_call | solution.py:159
  78.6 2.8 %collective-permute-start.19 = (bf16[256,1024]{1,0:T(8,128)(2,1)S(1)}, bf16[256,1024]{1,0:T(8,128)(2,1)S(1)}, u32[]{:S(2)}, u32[]{:S(2)}) collective-permute-start(bf16[256,1024]{1,0:T(8,128)(2,1)S(1)} %broadcast_select_fusion.1), channel_id=1, source_target_pairs={{0,48},{1,49},{2,50},{3,51},{4,52},{5,53},{6,54},{7,55},{8,56},{9,... | collective-permute-start | bytes 1572872 | tf_op jit(solution)/shard_map/ppermute | solution.py:45
  81.4 3.8 %collective-permute-start.26 = (bf16[128,896]{1,0:T(8,128)(2,1)S(1)}, bf16[128,896]{1,0:T(8,128)(2,1)S(1)}, u32[]{:S(2)}, u32[]{:S(2)}) collective-permute-start(bf16[128,896]{1,0:T(8,128)(2,1)S(1)} %dynamic-slice_bitcast_fusion), channel_id=1, source_target_pairs={{0,1},{1,2},{2,3},{3,4},{4,5},{5,6},{6,7},{7,8},{8,9},{9,10},{10,1... | collective-permute-start | bytes 688136 | tf_op jit(solution)/shard_map/ppermute | solution.py:387
  85.3 2.0 %partial.3.refs_5_ = f32[512,1024]{1,0:T(8,128)S(1)} custom-call(bf16[512,4096]{1,0:T(8,128)(2,1)S(1)} %rows.1.n_ref, bf16[256,1024]{1,0:T(8,128)(2,1)S(1)} %stack.2.refs_0_, bf16[256,1024]{1,0:T(8,128)(2,1)S(1)} %copy-done.12, bf16[256,1024]{1,0:T(8,128)(2,1)} %collective-permute-done.6.refs_2_), custom_call_target="tpu_custom_call" | custom-call | flops 805306368 | bytes 2359296 | tf_op jit(solution)/shard_map/partial/pallas_call | solution.py:241
  87.3 3.0 %partial.4.refs_6_ = f32[512,1024]{1,0:T(8,128)S(1)} custom-call(bf16[512,4096]{1,0:T(8,128)(2,1)S(1)} %rows.1.n_ref, bf16[256,1024]{1,0:T(8,128)(2,1)S(1)} %stack.3.refs_0_, bf16[256,1024]{1,0:T(8,128)(2,1)S(1)} %copy-done.14, bf16[256,1024]{1,0:T(8,128)(2,1)} %collective-permute-done.14.refs_2_, bf16[256,1024]{1,0:T(8,128)(2,1)} %collective-permute-done.5.refs_3_, ...), custom_call_target="tpu_custom_call" | custom-call | flops 1342177280 | bytes 3932160 | tf_op jit(solution)/shard_map/partial/pallas_call | solution.py:241
  90.4 4.1 %collective-permute-done.26.mine_ref = bf16[128,896]{1,0:T(8,128)(2,1)S(1)} collective-permute-done((bf16[128,896]{1,0:T(8,128)(2,1)S(1)}, bf16[128,896]{1,0:T(8,128)(2,1)S(1)}, u32[]{:S(2)}, u32[]{:S(2)}) %collective-permute-start.26) | collective-permute-done | bytes 229408 | tf_op jit(solution)/shard_map/ppermute | solution.py:387
  94.7 2.0 %collective-permute-start.22 = (bf16[128,1024]{1,0:T(8,128)(2,1)S(1)}, bf16[128,1024]{1,0:T(8,128)(2,1)S(1)}, u32[]{:S(2)}, u32[]{:S(2)}) collective-permute-start(bf16[128,1024]{1,0:T(8,128)(2,1)S(1)} %slice.15), channel_id=1, source_target_pairs={{0,16},{1,17},{2,18},{3,19},{4,20},{5,21},{6,22},{7,23},{8,24},{9,... | collective-permute-start | bytes 786440 | tf_op jit(solution)/shard_map/ppermute | solution.py:45
  103.7 2.1 %collective-permute-done.24.refs_2_ = bf16[128,1024]{1,0:T(8,128)(2,1)S(1)} collective-permute-done((bf16[128,1024]{1,0:T(8,128)(2,1)S(1)}, bf16[128,1024]{1,0:T(8,128)(2,1)S(1)}, u32[]{:S(2)}, u32[]{:S(2)}) %collective-permute-start.24) | collective-permute-done | bytes 262176 | tf_op jit(solution)/shard_map/ppermute | solution.py:45
  105.8 6.1 %attend.1 = bf16[512,1024]{1,0:T(8,128)(2,1)} custom-call(s32[2,512]{1,0:T(2,128)S(1)} %bitcast.7, s32[256,128]{1,0:T(8,128)S(1)} %bitcast.6, f32[512,1024]{1,0:T(8,128)S(1)} %partial.5.total_ref, bf16[512,4096]{1,0:T(8,128)(2,1)S(1)} %rows.1.n_ref, bf16[128,1024]{1,0:T(8,128)(2,1)S(1)} %collective-permute-done.22.refs_0_, ...), custom_call_target="tpu_custom_call" | custom-call | flops 6291456000 | bytes 16777216 | tf_op jit(solution)/shard_map/attend/pallas_call | solution.py:320
  (101 shorter events, 38.2 us)
Async XLA Ops:
  0.0 11.3 %collective-permute-start = (bf16[64,1024]{1,0:T(8,128)(2,1)}, bf16[64,1024]{1,0:T(8,128)(2,1)S(1)}, u32[]{:S(2)}, u32[]{:S(2)}) collective-permute-start(bf16[64,1024]{1,0:T(8,128)(2,1)} %refs_0_.1), channel_id=1, source_target_pairs={{0,1},{1,2},{2,3},{3,4},{4,5},{5,6},{6,7},{7,0},{8,9},{9,10},{10,1... | collective-permute-start | bytes 393224 | tf_op jit(solution)/shard_map/ppermute | solution.py:45
  1.9 10.6 %collective-permute-start.2 = (bf16[64,1024]{1,0:T(8,128)(2,1)}, bf16[64,1024]{1,0:T(8,128)(2,1)S(1)}, u32[]{:S(2)}, u32[]{:S(2)}) collective-permute-start(bf16[64,1024]{1,0:T(8,128)(2,1)} %refs_0_.1), channel_id=1, source_target_pairs={{0,2},{1,3},{2,4},{3,5},{4,6},{5,7},{6,0},{7,1},{8,10},{9,11},{10,... | collective-permute-start | bytes 393224 | tf_op jit(solution)/shard_map/ppermute | solution.py:45
  5.2 7.3 %collective-permute-start.3 = (bf16[64,1024]{1,0:T(8,128)(2,1)}, bf16[64,1024]{1,0:T(8,128)(2,1)S(1)}, u32[]{:S(2)}, u32[]{:S(2)}) collective-permute-start(bf16[64,1024]{1,0:T(8,128)(2,1)} %refs_0_.1), channel_id=1, source_target_pairs={{0,6},{1,7},{2,0},{3,1},{4,2},{5,3},{6,4},{7,5},{8,14},{9,15},{10,... | collective-permute-start | bytes 393224 | tf_op jit(solution)/shard_map/ppermute | solution.py:45
  14.3 22.7 %collective-permute-start.8 = (bf16[128,4096]{1,0:T(8,128)(2,1)S(1)}, bf16[128,4096]{1,0:T(8,128)(2,1)S(1)}, u32[]{:S(2)}, u32[]{:S(2)}) collective-permute-start(bf16[128,4096]{1,0:T(8,128)(2,1)S(1)} %norm.1.own_ref), channel_id=1, source_target_pairs={{0,64},{64,0},{1,65},{65,1},{2,66},{66,2},{3,67},{67,3},{4,68},{68... | collective-permute-start | bytes 3145736 | tf_op jit(solution)/shard_map/ppermute | solution.py:49
  14.3 7.8 %collective-permute-start.10 = (bf16[64,1024]{1,0:T(8,128)(2,1)S(1)}, bf16[64,1024]{1,0:T(8,128)(2,1)S(1)}, u32[]{:S(2)}, u32[]{:S(2)}) collective-permute-start(bf16[64,1024]{1,0:T(8,128)(2,1)S(1)} %get-tuple-element.32.refs_0_), channel_id=1, source_target_pairs={{0,7},{1,0},{2,1},{3,2},{4,3},{5,4},{6,5},{7,6},{8,15},{9,8},{10,9... | collective-permute-start | bytes 393224 | tf_op jit(solution)/shard_map/ppermute | solution.py:45
  16.6 36.8 %collective-permute-start.9 = (bf16[128,4096]{1,0:T(8,128)(2,1)S(1)}, bf16[128,4096]{1,0:T(8,128)(2,1)}, u32[]{:S(2)}, u32[]{:S(2)}) collective-permute-start(bf16[128,4096]{1,0:T(8,128)(2,1)S(1)} %norm.1.own_ref), channel_id=1, source_target_pairs={{0,128},{128,0},{1,129},{129,1},{2,130},{130,2},{3,131},{131,3},{4... | collective-permute-start | bytes 3145736 | tf_op jit(solution)/shard_map/ppermute | solution.py:49
  18.8 20.4 %collective-permute-start.4 = (bf16[256,1024]{1,0:T(8,128)(2,1)S(1)}, bf16[256,1024]{1,0:T(8,128)(2,1)S(1)}, u32[]{:S(2)}, u32[]{:S(2)}) collective-permute-start(bf16[256,1024]{1,0:T(8,128)(2,1)S(1)} %stack.2.refs_0_), channel_id=1, source_target_pairs={{0,16},{1,17},{2,18},{3,19},{4,20},{5,21},{6,22},{7,23},{8,24},{9,... | collective-permute-start | bytes 1572872 | tf_op jit(solution)/shard_map/ppermute | solution.py:45
  20.5 18.7 %collective-permute-start.6 = (bf16[256,1024]{1,0:T(8,128)(2,1)S(1)}, bf16[256,1024]{1,0:T(8,128)(2,1)}, u32[]{:S(2)}, u32[]{:S(2)}) collective-permute-start(bf16[256,1024]{1,0:T(8,128)(2,1)S(1)} %stack.2.refs_0_), channel_id=1, source_target_pairs={{0,48},{1,49},{2,50},{3,51},{4,52},{5,53},{6,54},{7,55},{8,56},{9,... | collective-permute-start | bytes 1572872 | tf_op jit(solution)/shard_map/ppermute | solution.py:45
  22.1 8.7 %collective-permute-start.11 = (bf16[64,1024]{1,0:T(8,128)(2,1)S(1)}, bf16[64,1024]{1,0:T(8,128)(2,1)S(1)}, u32[]{:S(2)}, u32[]{:S(2)}) collective-permute-start(bf16[64,1024]{1,0:T(8,128)(2,1)S(1)} %get-tuple-element.32.refs_0_), channel_id=1, source_target_pairs={{0,6},{1,7},{2,0},{3,1},{4,2},{5,3},{6,4},{7,5},{8,14},{9,15},{10,... | collective-permute-start | bytes 393224 | tf_op jit(solution)/shard_map/ppermute | solution.py:45
  37.1 9.4 %collective-permute-start.14 = (bf16[256,1024]{1,0:T(8,128)(2,1)S(1)}, bf16[256,1024]{1,0:T(8,128)(2,1)}, u32[]{:S(2)}, u32[]{:S(2)}) collective-permute-start(bf16[256,1024]{1,0:T(8,128)(2,1)S(1)} %stack.3.refs_0_), channel_id=1, source_target_pairs={{0,48},{1,49},{2,50},{3,51},{4,52},{5,53},{6,54},{7,55},{8,56},{9,... | collective-permute-start | bytes 1572872 | tf_op jit(solution)/shard_map/ppermute | solution.py:45
  38.7 10.4 %collective-permute-start.13 = (bf16[256,1024]{1,0:T(8,128)(2,1)S(1)}, bf16[256,1024]{1,0:T(8,128)(2,1)S(1)}, u32[]{:S(2)}, u32[]{:S(2)}) collective-permute-start(bf16[256,1024]{1,0:T(8,128)(2,1)S(1)} %stack.3.refs_0_), channel_id=1, source_target_pairs={{0,16},{1,17},{2,18},{3,19},{4,20},{5,21},{6,22},{7,23},{8,24},{9,... | collective-permute-start | bytes 1572872 | tf_op jit(solution)/shard_map/ppermute | solution.py:45
  40.1 23.6 %collective-permute-start.5 = (bf16[256,1024]{1,0:T(8,128)(2,1)}, bf16[256,1024]{1,0:T(8,128)(2,1)}, u32[]{:S(2)}, u32[]{:S(2)}) collective-permute-start(bf16[256,1024]{1,0:T(8,128)(2,1)} %broadcast_select_fusion.3), channel_id=1, source_target_pairs={{0,8},{1,9},{2,10},{3,11},{4,12},{5,13},{6,14},{7,15},{8,0},{9,1},... | collective-permute-start | bytes 1572872 | tf_op jit(solution)/shard_map/ppermute | solution.py:45
  41.4 22.4 %collective-permute-start.7 = (bf16[256,1024]{1,0:T(8,128)(2,1)}, bf16[256,1024]{1,0:T(8,128)(2,1)}, u32[]{:S(2)}, u32[]{:S(2)}) collective-permute-start(bf16[256,1024]{1,0:T(8,128)(2,1)} %collective-permute-done.6.refs_2_), channel_id=1, source_target_pairs={{0,48},{1,49},{2,50},{3,51},{4,52},{5,53},{6,54},{7,55},{8,56},{9,... | collective-permute-start | bytes 1572872 | tf_op jit(solution)/shard_map/ppermute | solution.py:45
  53.5 21.1 %collective-permute-start.15 = (bf16[128,4096]{1,0:T(8,128)(2,1)}, bf16[128,4096]{1,0:T(8,128)(2,1)}, u32[]{:S(2)}, u32[]{:S(2)}) collective-permute-start(bf16[128,4096]{1,0:T(8,128)(2,1)} %collective-permute-done.9.far_ref), channel_id=1, source_target_pairs={{0,64},{64,0},{1,65},{65,1},{2,66},{66,2},{3,67},{67,3},{4,68},{68... | collective-permute-start | bytes 3145736 | tf_op jit(solution)/shard_map/ppermute | solution.py:49
  60.9 16.8 %collective-permute-start.18 = (bf16[256,1024]{1,0:T(8,128)(2,1)}, bf16[256,1024]{1,0:T(8,128)(2,1)S(1)}, u32[]{:S(2)}, u32[]{:S(2)}) collective-permute-start(bf16[256,1024]{1,0:T(8,128)(2,1)} %collective-permute-done.14.refs_2_), channel_id=1, source_target_pairs={{0,48},{1,49},{2,50},{3,51},{4,52},{5,53},{6,54},{7,55},{8,56},{9,... | collective-permute-start | bytes 1572872 | tf_op jit(solution)/shard_map/ppermute | solution.py:45
  62.0 15.8 %collective-permute-start.16 = (bf16[256,1024]{1,0:T(8,128)(2,1)}, bf16[256,1024]{1,0:T(8,128)(2,1)S(1)}, u32[]{:S(2)}, u32[]{:S(2)}) collective-permute-start(bf16[256,1024]{1,0:T(8,128)(2,1)} %broadcast_select_fusion.2), channel_id=1, source_target_pairs={{0,8},{1,9},{2,10},{3,11},{4,12},{5,13},{6,14},{7,15},{8,0},{9,1},... | collective-permute-start | bytes 1572872 | tf_op jit(solution)/shard_map/ppermute | solution.py:45
  63.7 21.5 %collective-permute-start.20 = (bf16[256,1024]{1,0:T(8,128)(2,1)}, bf16[256,1024]{1,0:T(8,128)(2,1)S(1)}, u32[]{:S(2)}, u32[]{:S(2)}) collective-permute-start(bf16[256,1024]{1,0:T(8,128)(2,1)} %collective-permute-done.5.refs_3_), channel_id=1, source_target_pairs={{0,16},{1,17},{2,18},{3,19},{4,20},{5,21},{6,22},{7,23},{8,24},{9,... | collective-permute-start | bytes 1572872 | tf_op jit(solution)/shard_map/ppermute | solution.py:45
  66.8 18.5 %collective-permute-start.21 = (bf16[256,1024]{1,0:T(8,128)(2,1)S(1)}, bf16[256,1024]{1,0:T(8,128)(2,1)S(1)}, u32[]{:S(2)}, u32[]{:S(2)}) collective-permute-start(bf16[256,1024]{1,0:T(8,128)(2,1)S(1)} %broadcast_select_fusion), channel_id=1, source_target_pairs={{0,48},{1,49},{2,50},{3,51},{4,52},{5,53},{6,54},{7,55},{8,56},{9,... | collective-permute-start | bytes 1572872 | tf_op jit(solution)/shard_map/ppermute | solution.py:45
  77.7 20.4 %collective-permute-start.17 = (bf16[256,1024]{1,0:T(8,128)(2,1)S(1)}, bf16[256,1024]{1,0:T(8,128)(2,1)S(1)}, u32[]{:S(2)}, u32[]{:S(2)}) collective-permute-start(bf16[256,1024]{1,0:T(8,128)(2,1)S(1)} %collective-permute-done.16.refs_0_), channel_id=1, source_target_pairs={{0,16},{1,17},{2,18},{3,19},{4,20},{5,21},{6,22},{7,23},{8,24},{9,... | collective-permute-start | bytes 1572872 | tf_op jit(solution)/shard_map/ppermute | solution.py:45
  78.6 18.1 %collective-permute-start.19 = (bf16[256,1024]{1,0:T(8,128)(2,1)S(1)}, bf16[256,1024]{1,0:T(8,128)(2,1)S(1)}, u32[]{:S(2)}, u32[]{:S(2)}) collective-permute-start(bf16[256,1024]{1,0:T(8,128)(2,1)S(1)} %broadcast_select_fusion.1), channel_id=1, source_target_pairs={{0,48},{1,49},{2,50},{3,51},{4,52},{5,53},{6,54},{7,55},{8,56},{9,... | collective-permute-start | bytes 1572872 | tf_op jit(solution)/shard_map/ppermute | solution.py:45
  81.4 13.0 %collective-permute-start.26 = (bf16[128,896]{1,0:T(8,128)(2,1)S(1)}, bf16[128,896]{1,0:T(8,128)(2,1)S(1)}, u32[]{:S(2)}, u32[]{:S(2)}) collective-permute-start(bf16[128,896]{1,0:T(8,128)(2,1)S(1)} %dynamic-slice_bitcast_fusion), channel_id=1, source_target_pairs={{0,1},{1,2},{2,3},{3,4},{4,5},{5,6},{6,7},{7,8},{8,9},{9,10},{10,1... | collective-permute-start | bytes 688136 | tf_op jit(solution)/shard_map/ppermute | solution.py:387
  94.5 7.6 %collective-permute-start.23 = (bf16[128,1024]{1,0:T(8,128)(2,1)S(1)}, bf16[128,1024]{1,0:T(8,128)(2,1)S(1)}, u32[]{:S(2)}, u32[]{:S(2)}) collective-permute-start(bf16[128,1024]{1,0:T(8,128)(2,1)S(1)} %slice.16), channel_id=1, source_target_pairs={{0,48},{1,49},{2,50},{3,51},{4,52},{5,53},{6,54},{7,55},{8,56},{9,... | collective-permute-start | bytes 786440 | tf_op jit(solution)/shard_map/ppermute | solution.py:45
  94.7 7.7 %collective-permute-start.22 = (bf16[128,1024]{1,0:T(8,128)(2,1)S(1)}, bf16[128,1024]{1,0:T(8,128)(2,1)S(1)}, u32[]{:S(2)}, u32[]{:S(2)}) collective-permute-start(bf16[128,1024]{1,0:T(8,128)(2,1)S(1)} %slice.15), channel_id=1, source_target_pairs={{0,16},{1,17},{2,18},{3,19},{4,20},{5,21},{6,22},{7,23},{8,24},{9,... | collective-permute-start | bytes 786440 | tf_op jit(solution)/shard_map/ppermute | solution.py:45
  98.1 7.7 %collective-permute-start.24 = (bf16[128,1024]{1,0:T(8,128)(2,1)S(1)}, bf16[128,1024]{1,0:T(8,128)(2,1)S(1)}, u32[]{:S(2)}, u32[]{:S(2)}) collective-permute-start(bf16[128,1024]{1,0:T(8,128)(2,1)S(1)} %slice.17), channel_id=1, source_target_pairs={{0,16},{1,17},{2,18},{3,19},{4,20},{5,21},{6,22},{7,23},{8,24},{9,... | collective-permute-start | bytes 786440 | tf_op jit(solution)/shard_map/ppermute | solution.py:45
  (27 other events, 176.4 us)

commit v6 on v4

--- a/solution.py
+++ b/solution.py
@@ -256,11 +256,11 @@
     half = columns // 2
 
     def body(lens_ref, seg_ref, total_ref, n_ref, *refs):
-        piece_refs, prev_ref, k_refs, v_refs = refs[:4], refs[4], refs[5:7], refs[7:9]
-        out_ref, q_scr, c_scr, s_scr, w_scr = refs[9:]
+        piece_refs, prev_ref, k_refs, v_refs = refs[:3], refs[3], refs[4:6], refs[6:8]
+        out_ref, q_scr, c_scr, s_scr, w_scr = refs[8:]
         seq = (lax.axis_index("y") * 2 + lax.axis_index("xl")) * 8 + lax.axis_index("z")
         (slot,) = outer_slots([7])
-        places = [slot * 512 + i * 128 for i in range(4)]
+        places = [slot * 512 + i for i in (0, 256, 384)]
         acc = total_ref[...] + products(n_ref, piece_refs, places)
         acc = acc * HEAD_DIM ** (-0.5)
         acc = jnp.concatenate([acc, jnp.zeros((SPAN, columns), jnp.float32)], axis=0)
@@ -320,7 +320,7 @@
     return pl.pallas_call(
         body,
         out_shape=jax.ShapeDtypeStruct((rows, columns), jnp.bfloat16),
-        in_specs=[SMEM] + [VMEM] * 12,
+        in_specs=[SMEM] + [VMEM] * 11,
         out_specs=VMEM,
         scratch_shapes=[
             pltpu.VMEM((blocks * SPAN, columns), jnp.bfloat16),
@@ -399,7 +399,7 @@
     whole = gather_rows([after(normed, prev), near, far, far_near])
     b += outer_third(*b[3:5], whole)
     total = partial_product(after(whole, *b[3:5]), [(0, [0, 1, 2], a[:3])])
-    a += outer_last(*a[5:7], total)
+    a.append(send(after(a[5], total), (1, 0), (1, "z")))
     total = partial_product(
         after(whole, *a[5:7]), [(256, [0, 1, 2], b[:3]), (0, [3, 4], a[3:5])], total
     )

time: 97 us -> 96.1 us (level)
  starting transfers between devices: 42.5 us -> 39.5 us
  waiting for transfers between devices: 20.3 us -> 22.7 us
    ppermute x23 -> x22, starting transfers between devices: 37 us -> 34 us  [send(): return lax.ppermute(x, PLANE, pairs)]
    ppermute x23 -> x22, waiting for transfers between devices: 15.7 us -> 18.1 us  [send(): return lax.ppermute(x, PLANE, pairs)]
  transfers between devices with their start and end apart: 28 -> 27, of which waited for: 9 -> 10; matrix products, arithmetic and copies ran while one was open for 1% -> 1% of each run, Pallas kernels for 20% -> 20%
where the time goes in v6:
time: 96.1 us; the launch traced here: 94.5 us
  starting transfers between devices  39.5 us (41%)
  Pallas kernels  25 us (26%)
  waiting for transfers between devices  22.7 us (24%)
  local copies, waits for them, and re-layouts  6.1 us (6%)
    ppermute x22, starting transfers between devices, send(): return lax.ppermute(x, PLANE, pairs)  34 us
    ppermute x22, waiting for transfers between devices, send(): return lax.ppermute(x, PLANE, pairs)  18.1 us
    pallas_call x4, Pallas kernels, project(): pl.pallas_call(project_kernel, grid=(1,), out_shape=jax.ShapeDtypeStruct(...  9.32 us
    unnamed x16, local copies, waits for them, and re-layouts  6.04 us
    pallas_call x1, Pallas kernels, attend(): pl.pallas_call(body, out_shape=jax.ShapeDtypeStruct((rows, columns), jnp....  5.83 us
    ppermute x1, waiting for transfers between devices, local(): lax.ppermute(after(prev, column_a), ('y', 'xl', 'z'), [(i, i + 1) for i i...  4.6 us
    pallas_call x3, Pallas kernels, partial_product(): pl.pallas_call(body, out_shape=jax.ShapeDtypeStruct((rows, columns), jnp....  4.3 us
    ppermute x4, starting transfers between devices, hop(): return lax.ppermute(x, axis, [(0, 1), (1, 0)])  3.52 us
  transfers between devices with their start and end apart: 27, of which 10 were waited for; matrix products, arithmetic and copies ran while one was open for 1% of the time, Pallas kernels for 20%

profile of v6, /device:TPU:2, one launch (start us, length us, event | category | flops | bytes accessed | tf_op | source)
XLA Modules:
  0.0 94.5 jit_solution(4033253791038101877)
XLA Ops:
  0.0 1.9 %collective-permute-start = (bf16[64,1024]{1,0:T(8,128)(2,1)}, bf16[64,1024]{1,0:T(8,128)(2,1)S(1)}, u32[]{:S(2)}, u32[]{:S(2)}) collective-permute-start(bf16[64,1024]{1,0:T(8,128)(2,1)} %refs_0_.1), channel_id=1, source_target_pairs={{0,1},{1,2},{2,3},{3,4},{4,5},{5,6},{6,7},{7,0},{8,9},{9,10},{10,1... | collective-permute-start | bytes 393224 | tf_op jit(solution)/shard_map/ppermute | solution.py:45
  1.9 3.3 %collective-permute-start.2 = (bf16[64,1024]{1,0:T(8,128)(2,1)}, bf16[64,1024]{1,0:T(8,128)(2,1)S(1)}, u32[]{:S(2)}, u32[]{:S(2)}) collective-permute-start(bf16[64,1024]{1,0:T(8,128)(2,1)} %refs_0_.1), channel_id=1, source_target_pairs={{0,2},{1,3},{2,4},{3,5},{4,6},{5,7},{6,0},{7,1},{8,10},{9,11},{10,... | collective-permute-start | bytes 393224 | tf_op jit(solution)/shard_map/ppermute | solution.py:45
  5.2 2.1 %collective-permute-start.3 = (bf16[64,1024]{1,0:T(8,128)(2,1)}, bf16[64,1024]{1,0:T(8,128)(2,1)S(1)}, u32[]{:S(2)}, u32[]{:S(2)}) collective-permute-start(bf16[64,1024]{1,0:T(8,128)(2,1)} %refs_0_.1), channel_id=1, source_target_pairs={{0,6},{1,7},{2,0},{3,1},{4,2},{5,3},{6,4},{7,5},{8,14},{9,15},{10,... | collective-permute-start | bytes 393224 | tf_op jit(solution)/shard_map/ppermute | solution.py:45
  11.3 2.2 %collective-permute-start.11 = (bf16[128,4096]{1,0:T(8,128)(2,1)S(1)}, bf16[128,4096]{1,0:T(8,128)(2,1)}, u32[]{:S(2)}, u32[]{:S(2)}) collective-permute-start(bf16[128,4096]{1,0:T(8,128)(2,1)S(1)} %norm.1.own_ref), channel_id=1, source_target_pairs={{0,128},{128,0},{1,129},{129,1},{2,130},{130,2},{3,131},{131,3},{4... | collective-permute-start | bytes 3145736 | tf_op jit(solution)/shard_map/ppermute | solution.py:49
  14.2 2.1 %collective-permute-start.12 = (bf16[64,1024]{1,0:T(8,128)(2,1)S(1)}, bf16[64,1024]{1,0:T(8,128)(2,1)S(1)}, u32[]{:S(2)}, u32[]{:S(2)}) collective-permute-start(bf16[64,1024]{1,0:T(8,128)(2,1)S(1)} %get-tuple-element.35.refs_0_), channel_id=1, source_target_pairs={{0,7},{1,0},{2,1},{3,2},{4,3},{5,4},{6,5},{7,6},{8,15},{9,8},{10,9... | collective-permute-start | bytes 393224 | tf_op jit(solution)/shard_map/ppermute | solution.py:45
  19.7 2.6 %collective-permute-start.13 = (bf16[64,1024]{1,0:T(8,128)(2,1)S(1)}, bf16[64,1024]{1,0:T(8,128)(2,1)S(1)}, u32[]{:S(2)}, u32[]{:S(2)}) collective-permute-start(bf16[64,1024]{1,0:T(8,128)(2,1)S(1)} %get-tuple-element.35.refs_0_), channel_id=1, source_target_pairs={{0,6},{1,7},{2,0},{3,1},{4,2},{5,3},{6,4},{7,5},{8,14},{9,15},{10,... | collective-permute-start | bytes 393224 | tf_op jit(solution)/shard_map/ppermute | solution.py:45
  23.3 4.0 %collective-permute-done.13.refs_2_ = bf16[64,1024]{1,0:T(8,128)(2,1)S(1)} collective-permute-done((bf16[64,1024]{1,0:T(8,128)(2,1)S(1)}, bf16[64,1024]{1,0:T(8,128)(2,1)S(1)}, u32[]{:S(2)}, u32[]{:S(2)}) %collective-permute-start.13) | collective-permute-done | bytes 131104 | tf_op jit(solution)/shard_map/ppermute | solution.py:45
  30.2 2.9 %collective-permute-start.16 = (bf16[256,1024]{1,0:T(8,128)(2,1)S(1)}, bf16[256,1024]{1,0:T(8,128)(2,1)S(1)}, u32[]{:S(2)}, u32[]{:S(2)}) collective-permute-start(bf16[256,1024]{1,0:T(8,128)(2,1)S(1)} %stack.3.refs_0_), channel_id=1, source_target_pairs={{0,48},{1,49},{2,50},{3,51},{4,52},{5,53},{6,54},{7,55},{8,56},{9,... | collective-permute-start | bytes 1572872 | tf_op jit(solution)/shard_map/ppermute | solution.py:45
  33.1 2.0 %copy-done = bf16[2,896,1024]{2,1,0:T(8,128)(2,1)S(1)} copy-done((bf16[2,896,1024]{2,1,0:T(8,128)(2,1)S(1)}, bf16[2,896,1024]{2,1,0:T(8,128)(2,1)}, u32[]{:S(2)}) %copy-start) | copy-done | bytes 3670040
  35.1 2.0 %copy-done.2 = bf16[8,256,896]{2,1,0:T(8,128)(2,1)S(1)} copy-done((bf16[8,256,896]{2,1,0:T(8,128)(2,1)S(1)}, bf16[8,256,896]{2,1,0:T(8,128)(2,1)}, u32[]{:S(2)}) %copy-start.2) | copy-done | bytes 3670040
  37.2 2.3 %project.4.refs_4_ = bf16[8,256,512]{2,1,0:T(8,128)(2,1)S(1)} custom-call(bf16[8,256,896]{2,1,0:T(8,128)(2,1)S(1)} %copy-done.2, bf16[2,896,1024]{2,1,0:T(8,128)(2,1)S(1)} %copy-done), custom_call_target="tpu_custom_call" | custom-call | flops 1879048192 | bytes 6291456 | tf_op jit(solution)/shard_map/project/pallas_call | solution.py:181
  39.6 1.9 %collective-permute-start.4 = (bf16[128,896]{1,0:T(8,128)(2,1)S(1)}, bf16[128,896]{1,0:T(8,128)(2,1)S(1)}, u32[]{:S(2)}, u32[]{:S(2)}) collective-permute-start(bf16[128,896]{1,0:T(8,128)(2,1)S(1)} %dynamic-slice_bitcast_fusion), channel_id=1, source_target_pairs={{0,1},{1,2},{2,3},{3,4},{4,5},{5,6},{6,7},{7,8},{8,9},{9,10},{10,1... | collective-permute-start | bytes 688136 | tf_op jit(solution)/shard_map/ppermute | solution.py:387
  43.9 2.3 %project.6.refs_5_ = bf16[8,256,512]{2,1,0:T(8,128)(2,1)S(1)} custom-call(bf16[8,256,896]{2,1,0:T(8,128)(2,1)S(1)} %copy-done.2, bf16[2,896,1024]{2,1,0:T(8,128)(2,1)S(1)} %copy-done), custom_call_target="tpu_custom_call" | custom-call | flops 1879048192 | bytes 6291456 | tf_op jit(solution)/shard_map/project/pallas_call | solution.py:181
  47.5 4.6 %collective-permute-done.4.mine_ref = bf16[128,896]{1,0:T(8,128)(2,1)S(1)} collective-permute-done((bf16[128,896]{1,0:T(8,128)(2,1)S(1)}, bf16[128,896]{1,0:T(8,128)(2,1)S(1)}, u32[]{:S(2)}, u32[]{:S(2)}) %collective-permute-start.4) | collective-permute-done | bytes 229408 | tf_op jit(solution)/shard_map/ppermute | solution.py:387
  52.1 2.3 %project.7.refs_6_ = bf16[8,256,512]{2,1,0:T(8,128)(2,1)S(1)} custom-call(bf16[8,256,896]{2,1,0:T(8,128)(2,1)S(1)} %copy-done.2, bf16[2,896,1024]{2,1,0:T(8,128)(2,1)S(1)} %copy-done), custom_call_target="tpu_custom_call" | custom-call | flops 1879048192 | bytes 6291456 | tf_op jit(solution)/shard_map/project/pallas_call | solution.py:181
  57.5 2.3 %project.5.refs_7_ = bf16[8,256,512]{2,1,0:T(8,128)(2,1)S(1)} custom-call(bf16[8,256,896]{2,1,0:T(8,128)(2,1)S(1)} %copy-done.2, bf16[2,896,1024]{2,1,0:T(8,128)(2,1)S(1)} %copy-done), custom_call_target="tpu_custom_call" | custom-call | flops 1879048192 | bytes 6291456 | tf_op jit(solution)/shard_map/project/pallas_call | solution.py:181
  61.1 1.8 %collective-permute-start.22 = (bf16[256,1024]{1,0:T(8,128)(2,1)S(1)}, bf16[256,1024]{1,0:T(8,128)(2,1)S(1)}, u32[]{:S(2)}, u32[]{:S(2)}) collective-permute-start(bf16[256,1024]{1,0:T(8,128)(2,1)S(1)} %collective-permute-done.6.refs_3_), channel_id=1, source_target_pairs={{0,16},{1,17},{2,18},{3,19},{4,20},{5,21},{6,22},{7,23},{8,24},{9,... | collective-permute-start | bytes 1572872 | tf_op jit(solution)/shard_map/ppermute | solution.py:45
  63.0 1.8 %collective-permute-start.23 = (bf16[256,1024]{1,0:T(8,128)(2,1)S(1)}, bf16[256,1024]{1,0:T(8,128)(2,1)S(1)}, u32[]{:S(2)}, u32[]{:S(2)}) collective-permute-start(bf16[256,1024]{1,0:T(8,128)(2,1)S(1)} %broadcast_select_fusion), channel_id=1, source_target_pairs={{0,48},{1,49},{2,50},{3,51},{4,52},{5,53},{6,54},{7,55},{8,56},{9,... | collective-permute-start | bytes 1572872 | tf_op jit(solution)/shard_map/ppermute | solution.py:45
  64.8 2.7 %rows.1.n_ref = bf16[512,4096]{1,0:T(8,128)(2,1)S(1)} custom-call(bf16[128,4096]{1,0:T(8,128)(2,1)S(1)} %norm.1.own_ref, bf16[128,4096]{1,0:T(8,128)(2,1)S(1)} %collective-permute-done.10.near_ref, bf16[128,4096]{1,0:T(8,128)(2,1)} %collective-permute-done.11.far_ref, bf16[128,4096]{1,0:T(8,128)(2,1)S(1)} %collective-permute-done.17.far_near_ref), custom_call_target="tpu_custom_call" | custom-call | bytes 8388608 | tf_op jit(solution)/shard_map/rows/pallas_call | solution.py:159
  74.0 4.1 %collective-permute-done.21.refs_5_ = bf16[256,1024]{1,0:T(8,128)(2,1)S(1)} collective-permute-done((bf16[256,1024]{1,0:T(8,128)(2,1)S(1)}, bf16[256,1024]{1,0:T(8,128)(2,1)S(1)}, u32[]{:S(2)}, u32[]{:S(2)}) %collective-permute-start.21) | collective-permute-done | bytes 524320 | tf_op jit(solution)/shard_map/ppermute | solution.py:45
  78.1 2.8 %collective-permute-start.26 = (bf16[128,1024]{1,0:T(8,128)(2,1)S(1)}, bf16[128,1024]{1,0:T(8,128)(2,1)S(1)}, u32[]{:S(2)}, u32[]{:S(2)}) collective-permute-start(bf16[128,1024]{1,0:T(8,128)(2,1)S(1)} %slice.11), channel_id=1, source_target_pairs={{0,48},{1,49},{2,50},{3,51},{4,52},{5,53},{6,54},{7,55},{8,56},{9,... | collective-permute-start | bytes 786440 | tf_op jit(solution)/shard_map/ppermute | solution.py:45
  81.1 1.8 %partial.5.total_ref = f32[512,1024]{1,0:T(8,128)S(1)} custom-call(bf16[512,4096]{1,0:T(8,128)(2,1)S(1)} %rows.1.n_ref, bf16[256,1024]{1,0:T(8,128)(2,1)S(1)} %collective-permute-done.18.refs_0_, bf16[256,1024]{1,0:T(8,128)(2,1)S(1)} %collective-permute-done.20.refs_1_, bf16[256,1024]{1,0:T(8,128)(2,1)S(1)} %collective-permute-done.22.refs_2_, ...), custom_call_target="tpu_custom_call" | custom-call | flops 1610612736 | bytes 4718592 | tf_op jit(solution)/shard_map/partial/pallas_call | solution.py:241
  84.8 3.8 %collective-permute-done.25.refs_1_ = bf16[128,1024]{1,0:T(8,128)(2,1)S(1)} collective-permute-done((bf16[128,1024]{1,0:T(8,128)(2,1)S(1)}, bf16[128,1024]{1,0:T(8,128)(2,1)S(1)}, u32[]{:S(2)}, u32[]{:S(2)}) %collective-permute-start.25) | collective-permute-done | bytes 262176 | tf_op jit(solution)/shard_map/ppermute | solution.py:45
  88.7 5.8 %attend.1 = bf16[512,1024]{1,0:T(8,128)(2,1)} custom-call(s32[2,512]{1,0:T(2,128)S(1)} %bitcast.7, s32[256,128]{1,0:T(8,128)S(1)} %bitcast.6, f32[512,1024]{1,0:T(8,128)S(1)} %partial.5.total_ref, bf16[512,4096]{1,0:T(8,128)(2,1)S(1)} %rows.1.n_ref, bf16[256,1024]{1,0:T(8,128)(2,1)S(1)} %collective-permute-done.24.refs_0_, ...), custom_call_target="tpu_custom_call" | custom-call | flops 6291456000 | bytes 16777216 | tf_op jit(solution)/shard_map/attend/pallas_call | solution.py:320
  (69 shorter events, 28.6 us)
Async XLA Ops:
  0.0 13.5 %collective-permute-start = (bf16[64,1024]{1,0:T(8,128)(2,1)}, bf16[64,1024]{1,0:T(8,128)(2,1)S(1)}, u32[]{:S(2)}, u32[]{:S(2)}) collective-permute-start(bf16[64,1024]{1,0:T(8,128)(2,1)} %refs_0_.1), channel_id=1, source_target_pairs={{0,1},{1,2},{2,3},{3,4},{4,5},{5,6},{6,7},{7,0},{8,9},{9,10},{10,1... | collective-permute-start | bytes 393224 | tf_op jit(solution)/shard_map/ppermute | solution.py:45
  1.9 11.6 %collective-permute-start.2 = (bf16[64,1024]{1,0:T(8,128)(2,1)}, bf16[64,1024]{1,0:T(8,128)(2,1)S(1)}, u32[]{:S(2)}, u32[]{:S(2)}) collective-permute-start(bf16[64,1024]{1,0:T(8,128)(2,1)} %refs_0_.1), channel_id=1, source_target_pairs={{0,2},{1,3},{2,4},{3,5},{4,6},{5,7},{6,0},{7,1},{8,10},{9,11},{10,... | collective-permute-start | bytes 393224 | tf_op jit(solution)/shard_map/ppermute | solution.py:45
  5.2 8.4 %collective-permute-start.3 = (bf16[64,1024]{1,0:T(8,128)(2,1)}, bf16[64,1024]{1,0:T(8,128)(2,1)S(1)}, u32[]{:S(2)}, u32[]{:S(2)}) collective-permute-start(bf16[64,1024]{1,0:T(8,128)(2,1)} %refs_0_.1), channel_id=1, source_target_pairs={{0,6},{1,7},{2,0},{3,1},{4,2},{5,3},{6,4},{7,5},{8,14},{9,15},{10,... | collective-permute-start | bytes 393224 | tf_op jit(solution)/shard_map/ppermute | solution.py:45
  7.3 9.1 %collective-permute-start.1 = (bf16[64,1024]{1,0:T(8,128)(2,1)}, bf16[64,1024]{1,0:T(8,128)(2,1)S(1)}, u32[]{:S(2)}, u32[]{:S(2)}) collective-permute-start(bf16[64,1024]{1,0:T(8,128)(2,1)} %refs_0_.1), channel_id=1, source_target_pairs={{0,7},{1,0},{2,1},{3,2},{4,3},{5,4},{6,5},{7,6},{8,15},{9,8},{10,9... | collective-permute-start | bytes 393224 | tf_op jit(solution)/shard_map/ppermute | solution.py:45
  11.3 34.9 %collective-permute-start.11 = (bf16[128,4096]{1,0:T(8,128)(2,1)S(1)}, bf16[128,4096]{1,0:T(8,128)(2,1)}, u32[]{:S(2)}, u32[]{:S(2)}) collective-permute-start(bf16[128,4096]{1,0:T(8,128)(2,1)S(1)} %norm.1.own_ref), channel_id=1, source_target_pairs={{0,128},{128,0},{1,129},{129,1},{2,130},{130,2},{3,131},{131,3},{4... | collective-permute-start | bytes 3145736 | tf_op jit(solution)/shard_map/ppermute | solution.py:49
  14.2 8.1 %collective-permute-start.12 = (bf16[64,1024]{1,0:T(8,128)(2,1)S(1)}, bf16[64,1024]{1,0:T(8,128)(2,1)S(1)}, u32[]{:S(2)}, u32[]{:S(2)}) collective-permute-start(bf16[64,1024]{1,0:T(8,128)(2,1)S(1)} %get-tuple-element.35.refs_0_), channel_id=1, source_target_pairs={{0,7},{1,0},{2,1},{3,2},{4,3},{5,4},{6,5},{7,6},{8,15},{9,8},{10,9... | collective-permute-start | bytes 393224 | tf_op jit(solution)/shard_map/ppermute | solution.py:45
  16.4 23.1 %collective-permute-start.5 = (bf16[256,1024]{1,0:T(8,128)(2,1)S(1)}, bf16[256,1024]{1,0:T(8,128)(2,1)S(1)}, u32[]{:S(2)}, u32[]{:S(2)}) collective-permute-start(bf16[256,1024]{1,0:T(8,128)(2,1)S(1)} %stack.2.refs_0_), channel_id=1, source_target_pairs={{0,16},{1,17},{2,18},{3,19},{4,20},{5,21},{6,22},{7,23},{8,24},{9,... | collective-permute-start | bytes 1572872 | tf_op jit(solution)/shard_map/ppermute | solution.py:45
  18.1 21.5 %collective-permute-start.7 = (bf16[256,1024]{1,0:T(8,128)(2,1)S(1)}, bf16[256,1024]{1,0:T(8,128)(2,1)S(1)}, u32[]{:S(2)}, u32[]{:S(2)}) collective-permute-start(bf16[256,1024]{1,0:T(8,128)(2,1)S(1)} %stack.2.refs_0_), channel_id=1, source_target_pairs={{0,48},{1,49},{2,50},{3,51},{4,52},{5,53},{6,54},{7,55},{8,56},{9,... | collective-permute-start | bytes 1572872 | tf_op jit(solution)/shard_map/ppermute | solution.py:45
  29.7 11.9 %collective-permute-start.15 = (bf16[256,1024]{1,0:T(8,128)(2,1)S(1)}, bf16[256,1024]{1,0:T(8,128)(2,1)S(1)}, u32[]{:S(2)}, u32[]{:S(2)}) collective-permute-start(bf16[256,1024]{1,0:T(8,128)(2,1)S(1)} %stack.3.refs_0_), channel_id=1, source_target_pairs={{0,16},{1,17},{2,18},{3,19},{4,20},{5,21},{6,22},{7,23},{8,24},{9,... | collective-permute-start | bytes 1572872 | tf_op jit(solution)/shard_map/ppermute | solution.py:45
  30.2 12.9 %collective-permute-start.16 = (bf16[256,1024]{1,0:T(8,128)(2,1)S(1)}, bf16[256,1024]{1,0:T(8,128)(2,1)S(1)}, u32[]{:S(2)}, u32[]{:S(2)}) collective-permute-start(bf16[256,1024]{1,0:T(8,128)(2,1)S(1)} %stack.3.refs_0_), channel_id=1, source_target_pairs={{0,48},{1,49},{2,50},{3,51},{4,52},{5,53},{6,54},{7,55},{8,56},{9,... | collective-permute-start | bytes 1572872 | tf_op jit(solution)/shard_map/ppermute | solution.py:45
  39.5 23.5 %collective-permute-start.10 = (bf16[128,4096]{1,0:T(8,128)(2,1)S(1)}, bf16[128,4096]{1,0:T(8,128)(2,1)S(1)}, u32[]{:S(2)}, u32[]{:S(2)}) collective-permute-start(bf16[128,4096]{1,0:T(8,128)(2,1)S(1)} %norm.1.own_ref), channel_id=1, source_target_pairs={{0,64},{64,0},{1,65},{65,1},{2,66},{66,2},{3,67},{67,3},{4,68},{68... | collective-permute-start | bytes 3145736 | tf_op jit(solution)/shard_map/ppermute | solution.py:49
  39.6 12.5 %collective-permute-start.4 = (bf16[128,896]{1,0:T(8,128)(2,1)S(1)}, bf16[128,896]{1,0:T(8,128)(2,1)S(1)}, u32[]{:S(2)}, u32[]{:S(2)}) collective-permute-start(bf16[128,896]{1,0:T(8,128)(2,1)S(1)} %dynamic-slice_bitcast_fusion), channel_id=1, source_target_pairs={{0,1},{1,2},{2,3},{3,4},{4,5},{5,6},{6,7},{7,8},{8,9},{9,10},{10,1... | collective-permute-start | bytes 688136 | tf_op jit(solution)/shard_map/ppermute | solution.py:387
  41.6 14.4 %collective-permute-start.6 = (bf16[256,1024]{1,0:T(8,128)(2,1)S(1)}, bf16[256,1024]{1,0:T(8,128)(2,1)S(1)}, u32[]{:S(2)}, u32[]{:S(2)}) collective-permute-start(bf16[256,1024]{1,0:T(8,128)(2,1)S(1)} %broadcast_select_fusion.3), channel_id=1, source_target_pairs={{0,8},{1,9},{2,10},{3,11},{4,12},{5,13},{6,14},{7,15},{8,0},{9,1},... | collective-permute-start | bytes 1572872 | tf_op jit(solution)/shard_map/ppermute | solution.py:45
  43.1 14.1 %collective-permute-start.8 = (bf16[256,1024]{1,0:T(8,128)(2,1)S(1)}, bf16[256,1024]{1,0:T(8,128)(2,1)S(1)}, u32[]{:S(2)}, u32[]{:S(2)}) collective-permute-start(bf16[256,1024]{1,0:T(8,128)(2,1)S(1)} %collective-permute-done.7.refs_2_), channel_id=1, source_target_pairs={{0,48},{1,49},{2,50},{3,51},{4,52},{5,53},{6,54},{7,55},{8,56},{9,... | collective-permute-start | bytes 1572872 | tf_op jit(solution)/shard_map/ppermute | solution.py:45
  46.3 18.6 %collective-permute-start.17 = (bf16[128,4096]{1,0:T(8,128)(2,1)}, bf16[128,4096]{1,0:T(8,128)(2,1)S(1)}, u32[]{:S(2)}, u32[]{:S(2)}) collective-permute-start(bf16[128,4096]{1,0:T(8,128)(2,1)} %collective-permute-done.11.far_ref), channel_id=1, source_target_pairs={{0,64},{64,0},{1,65},{65,1},{2,66},{66,2},{3,67},{67,3},{4,68},{68... | collective-permute-start | bytes 3145736 | tf_op jit(solution)/shard_map/ppermute | solution.py:49
  52.1 7.8 %collective-permute-start.9 = (bf16[128,896]{1,0:T(8,128)(2,1)S(1)}, bf16[128,896]{1,0:T(8,128)(2,1)S(1)}, u32[]{:S(2)}, u32[]{:S(2)}) collective-permute-start(bf16[128,896]{1,0:T(8,128)(2,1)S(1)} %collective-permute-done.4.mine_ref), channel_id=1, source_target_pairs={{0,64},{64,0},{1,65},{65,1},{2,66},{66,2},{3,67},{67,3},{4,68},{68... | collective-permute-start | bytes 688136 | tf_op jit(solution)/shard_map/ppermute | solution.py:49
  56.0 11.6 %collective-permute-start.18 = (bf16[256,1024]{1,0:T(8,128)(2,1)S(1)}, bf16[256,1024]{1,0:T(8,128)(2,1)S(1)}, u32[]{:S(2)}, u32[]{:S(2)}) collective-permute-start(bf16[256,1024]{1,0:T(8,128)(2,1)S(1)} %broadcast_select_fusion.2), channel_id=1, source_target_pairs={{0,8},{1,9},{2,10},{3,11},{4,12},{5,13},{6,14},{7,15},{8,0},{9,1},... | collective-permute-start | bytes 1572872 | tf_op jit(solution)/shard_map/ppermute | solution.py:45
  57.2 10.3 %collective-permute-start.20 = (bf16[256,1024]{1,0:T(8,128)(2,1)S(1)}, bf16[256,1024]{1,0:T(8,128)(2,1)S(1)}, u32[]{:S(2)}, u32[]{:S(2)}) collective-permute-start(bf16[256,1024]{1,0:T(8,128)(2,1)S(1)} %collective-permute-done.16.refs_2_), channel_id=1, source_target_pairs={{0,48},{1,49},{2,50},{3,51},{4,52},{5,53},{6,54},{7,55},{8,56},{9,... | collective-permute-start | bytes 1572872 | tf_op jit(solution)/shard_map/ppermute | solution.py:45
  61.1 10.5 %collective-permute-start.22 = (bf16[256,1024]{1,0:T(8,128)(2,1)S(1)}, bf16[256,1024]{1,0:T(8,128)(2,1)S(1)}, u32[]{:S(2)}, u32[]{:S(2)}) collective-permute-start(bf16[256,1024]{1,0:T(8,128)(2,1)S(1)} %collective-permute-done.6.refs_3_), channel_id=1, source_target_pairs={{0,16},{1,17},{2,18},{3,19},{4,20},{5,21},{6,22},{7,23},{8,24},{9,... | collective-permute-start | bytes 1572872 | tf_op jit(solution)/shard_map/ppermute | solution.py:45
  63.0 9.5 %collective-permute-start.23 = (bf16[256,1024]{1,0:T(8,128)(2,1)S(1)}, bf16[256,1024]{1,0:T(8,128)(2,1)S(1)}, u32[]{:S(2)}, u32[]{:S(2)}) collective-permute-start(bf16[256,1024]{1,0:T(8,128)(2,1)S(1)} %broadcast_select_fusion), channel_id=1, source_target_pairs={{0,48},{1,49},{2,50},{3,51},{4,52},{5,53},{6,54},{7,55},{8,56},{9,... | collective-permute-start | bytes 1572872 | tf_op jit(solution)/shard_map/ppermute | solution.py:45
  67.6 10.5 %collective-permute-start.21 = (bf16[256,1024]{1,0:T(8,128)(2,1)S(1)}, bf16[256,1024]{1,0:T(8,128)(2,1)S(1)}, u32[]{:S(2)}, u32[]{:S(2)}) collective-permute-start(bf16[256,1024]{1,0:T(8,128)(2,1)S(1)} %broadcast_select_fusion.1), channel_id=1, source_target_pairs={{0,48},{1,49},{2,50},{3,51},{4,52},{5,53},{6,54},{7,55},{8,56},{9,... | collective-permute-start | bytes 1572872 | tf_op jit(solution)/shard_map/ppermute | solution.py:45
  68.0 12.9 %collective-permute-start.19 = (bf16[256,1024]{1,0:T(8,128)(2,1)S(1)}, bf16[256,1024]{1,0:T(8,128)(2,1)S(1)}, u32[]{:S(2)}, u32[]{:S(2)}) collective-permute-start(bf16[256,1024]{1,0:T(8,128)(2,1)S(1)} %collective-permute-done.18.refs_0_), channel_id=1, source_target_pairs={{0,16},{1,17},{2,18},{3,19},{4,20},{5,21},{6,22},{7,23},{8,24},{9,... | collective-permute-start | bytes 1572872 | tf_op jit(solution)/shard_map/ppermute | solution.py:45
  71.6 12.4 %collective-permute-start.24 = (bf16[256,1024]{1,0:T(8,128)(2,1)S(1)}, bf16[256,1024]{1,0:T(8,128)(2,1)S(1)}, u32[]{:S(2)}, u32[]{:S(2)}) collective-permute-start(bf16[256,1024]{1,0:T(8,128)(2,1)S(1)} %collective-permute-done.22.refs_2_), channel_id=1, source_target_pairs={{0,16},{1,17},{2,18},{3,19},{4,20},{5,21},{6,22},{7,23},{8,24},{9,... | collective-permute-start | bytes 1572872 | tf_op jit(solution)/shard_map/ppermute | solution.py:45
  81.0 7.7 %collective-permute-start.25 = (bf16[128,1024]{1,0:T(8,128)(2,1)S(1)}, bf16[128,1024]{1,0:T(8,128)(2,1)S(1)}, u32[]{:S(2)}, u32[]{:S(2)}) collective-permute-start(bf16[128,1024]{1,0:T(8,128)(2,1)S(1)} %slice.10), channel_id=1, source_target_pairs={{0,16},{1,17},{2,18},{3,19},{4,20},{5,21},{6,22},{7,23},{8,24},{9,... | collective-permute-start | bytes 786440 | tf_op jit(solution)/shard_map/ppermute | solution.py:45
  (12 other events, 74.9 us)

commit v7 on v6

--- a/solution.py
+++ b/solution.py
@@ -397,7 +397,7 @@
     values_b = projected(1, 1, *a[3:5])
     prev = project_prev(after(prev, values_b), prev_near, w_keyval)
     whole = gather_rows([after(normed, prev), near, far, far_near])
-    b += outer_third(*b[3:5], whole)
+    b += outer_third(*b[3:5], prev)
     total = partial_product(after(whole, *b[3:5]), [(0, [0, 1, 2], a[:3])])
     a.append(send(after(a[5], total), (1, 0), (1, "z")))
     total = partial_product(

time: 96.1 us -> 102 us (1.061)
  waiting for transfers between devices: 22.7 us -> 28.7 us
    ppermute x1, waiting for transfers between devices: 4.6 us -> 8.85 us  [local(): lax.ppermute(after(prev, column_a), ('y', 'xl', 'z'), [(i, i + 1) for i i...]
    ppermute x22, waiting for transfers between devices: 18.1 us -> 19.8 us  [send(): return lax.ppermute(x, PLANE, pairs)]
  transfers between devices with their start and end apart: 27 -> 27, of which waited for: 10 -> 10; matrix products, arithmetic and copies ran while one was open for 1% -> 0% of each run, Pallas kernels for 20% -> 18%
where the time goes in v7:
time: 102 us; the launch traced here: 99.9 us
  starting transfers between devices  40.5 us (40%)
  waiting for transfers between devices  28.7 us (28%)
  Pallas kernels  24.1 us (24%)
  local copies, waits for them, and re-layouts  6.1 us (6%)
    ppermute x22, starting transfers between devices, send(): return lax.ppermute(x, PLANE, pairs)  35.1 us
    ppermute x22, waiting for transfers between devices, send(): return lax.ppermute(x, PLANE, pairs)  19.8 us
    pallas_call x4, Pallas kernels, project(): pl.pallas_call(project_kernel, grid=(1,), out_shape=jax.ShapeDtypeStruct(...  9.32 us
    ppermute x1, waiting for transfers between devices, local(): lax.ppermute(after(prev, column_a), ('y', 'xl', 'z'), [(i, i + 1) for i i...  8.85 us
    unnamed x16, local copies, waits for them, and re-layouts  6.04 us
    pallas_call x1, Pallas kernels, attend(): pl.pallas_call(body, out_shape=jax.ShapeDtypeStruct((rows, columns), jnp....  5.83 us
    pallas_call x3, Pallas kernels, partial_product(): pl.pallas_call(body, out_shape=jax.ShapeDtypeStruct((rows, columns), jnp....  4.3 us
    ppermute x4, starting transfers between devices, hop(): return lax.ppermute(x, axis, [(0, 1), (1, 0)])  2.99 us
  transfers between devices with their start and end apart: 27, of which 10 were waited for; matrix products, arithmetic and copies ran while one was open for 0% of the time, Pallas kernels for 18%

profile of v7, /device:TPU:2, one launch (start us, length us, event | category | flops | bytes accessed | tf_op | source)
XLA Modules:
  0.0 99.9 jit_solution(14045953242593959657)
XLA Ops:
  0.0 1.9 %collective-permute-start = (bf16[64,1024]{1,0:T(8,128)(2,1)}, bf16[64,1024]{1,0:T(8,128)(2,1)S(1)}, u32[]{:S(2)}, u32[]{:S(2)}) collective-permute-start(bf16[64,1024]{1,0:T(8,128)(2,1)} %refs_0_.1), channel_id=1, source_target_pairs={{0,1},{1,2},{2,3},{3,4},{4,5},{5,6},{6,7},{7,0},{8,9},{9,10},{10,1... | collective-permute-start | bytes 393224 | tf_op jit(solution)/shard_map/ppermute | solution.py:45
  1.9 3.3 %collective-permute-start.2 = (bf16[64,1024]{1,0:T(8,128)(2,1)}, bf16[64,1024]{1,0:T(8,128)(2,1)S(1)}, u32[]{:S(2)}, u32[]{:S(2)}) collective-permute-start(bf16[64,1024]{1,0:T(8,128)(2,1)} %refs_0_.1), channel_id=1, source_target_pairs={{0,2},{1,3},{2,4},{3,5},{4,6},{5,7},{6,0},{7,1},{8,10},{9,11},{10,... | collective-permute-start | bytes 393224 | tf_op jit(solution)/shard_map/ppermute | solution.py:45
  5.2 2.1 %collective-permute-start.3 = (bf16[64,1024]{1,0:T(8,128)(2,1)}, bf16[64,1024]{1,0:T(8,128)(2,1)S(1)}, u32[]{:S(2)}, u32[]{:S(2)}) collective-permute-start(bf16[64,1024]{1,0:T(8,128)(2,1)} %refs_0_.1), channel_id=1, source_target_pairs={{0,6},{1,7},{2,0},{3,1},{4,2},{5,3},{6,4},{7,5},{8,14},{9,15},{10,... | collective-permute-start | bytes 393224 | tf_op jit(solution)/shard_map/ppermute | solution.py:45
  11.3 2.2 %collective-permute-start.11 = (bf16[128,4096]{1,0:T(8,128)(2,1)S(1)}, bf16[128,4096]{1,0:T(8,128)(2,1)}, u32[]{:S(2)}, u32[]{:S(2)}) collective-permute-start(bf16[128,4096]{1,0:T(8,128)(2,1)S(1)} %norm.1.own_ref), channel_id=1, source_target_pairs={{0,128},{128,0},{1,129},{129,1},{2,130},{130,2},{3,131},{131,3},{4... | collective-permute-start | bytes 3145736 | tf_op jit(solution)/shard_map/ppermute | solution.py:49
  16.0 2.3 %collective-permute-start.12 = (bf16[64,1024]{1,0:T(8,128)(2,1)S(1)}, bf16[64,1024]{1,0:T(8,128)(2,1)S(1)}, u32[]{:S(2)}, u32[]{:S(2)}) collective-permute-start(bf16[64,1024]{1,0:T(8,128)(2,1)S(1)} %get-tuple-element.35.refs_0_), channel_id=1, source_target_pairs={{0,7},{1,0},{2,1},{3,2},{4,3},{5,4},{6,5},{7,6},{8,15},{9,8},{10,9... | collective-permute-start | bytes 393224 | tf_op jit(solution)/shard_map/ppermute | solution.py:45
  24.1 3.4 %collective-permute-done.13.refs_2_ = bf16[64,1024]{1,0:T(8,128)(2,1)S(1)} collective-permute-done((bf16[64,1024]{1,0:T(8,128)(2,1)S(1)}, bf16[64,1024]{1,0:T(8,128)(2,1)S(1)}, u32[]{:S(2)}, u32[]{:S(2)}) %collective-permute-start.13) | collective-permute-done | bytes 131104 | tf_op jit(solution)/shard_map/ppermute | solution.py:45
  30.9 2.0 %copy-done = bf16[2,896,1024]{2,1,0:T(8,128)(2,1)S(1)} copy-done((bf16[2,896,1024]{2,1,0:T(8,128)(2,1)S(1)}, bf16[2,896,1024]{2,1,0:T(8,128)(2,1)}, u32[]{:S(2)}) %copy-start) | copy-done | bytes 3670040
  33.0 2.0 %copy-done.2 = bf16[8,256,896]{2,1,0:T(8,128)(2,1)S(1)} copy-done((bf16[8,256,896]{2,1,0:T(8,128)(2,1)S(1)}, bf16[8,256,896]{2,1,0:T(8,128)(2,1)}, u32[]{:S(2)}) %copy-start.2) | copy-done | bytes 3670040
  35.0 2.3 %project.4.refs_4_ = bf16[8,256,512]{2,1,0:T(8,128)(2,1)S(1)} custom-call(bf16[8,256,896]{2,1,0:T(8,128)(2,1)S(1)} %copy-done.2, bf16[2,896,1024]{2,1,0:T(8,128)(2,1)S(1)} %copy-done), custom_call_target="tpu_custom_call" | custom-call | flops 1879048192 | bytes 6291456 | tf_op jit(solution)/shard_map/project/pallas_call | solution.py:181
  37.4 2.5 %collective-permute-start.4 = (bf16[128,896]{1,0:T(8,128)(2,1)S(1)}, bf16[128,896]{1,0:T(8,128)(2,1)S(1)}, u32[]{:S(2)}, u32[]{:S(2)}) collective-permute-start(bf16[128,896]{1,0:T(8,128)(2,1)S(1)} %dynamic-slice_bitcast_fusion), channel_id=1, source_target_pairs={{0,1},{1,2},{2,3},{3,4},{4,5},{5,6},{6,7},{7,8},{8,9},{9,10},{10,1... | collective-permute-start | bytes 688136 | tf_op jit(solution)/shard_map/ppermute | solution.py:387
  40.0 8.8 %collective-permute-done.4.mine_ref = bf16[128,896]{1,0:T(8,128)(2,1)S(1)} collective-permute-done((bf16[128,896]{1,0:T(8,128)(2,1)S(1)}, bf16[128,896]{1,0:T(8,128)(2,1)S(1)}, u32[]{:S(2)}, u32[]{:S(2)}) %collective-permute-start.4) | collective-permute-done | bytes 229408 | tf_op jit(solution)/shard_map/ppermute | solution.py:387
  49.4 2.3 %project.7.refs_6_ = bf16[8,256,512]{2,1,0:T(8,128)(2,1)S(1)} custom-call(bf16[8,256,896]{2,1,0:T(8,128)(2,1)S(1)} %copy-done.2, bf16[2,896,1024]{2,1,0:T(8,128)(2,1)S(1)} %copy-done), custom_call_target="tpu_custom_call" | custom-call | flops 1879048192 | bytes 6291456 | tf_op jit(solution)/shard_map/project/pallas_call | solution.py:181
  52.4 2.3 %project.6.refs_5_ = bf16[8,256,512]{2,1,0:T(8,128)(2,1)S(1)} custom-call(bf16[8,256,896]{2,1,0:T(8,128)(2,1)S(1)} %copy-done.2, bf16[2,896,1024]{2,1,0:T(8,128)(2,1)S(1)} %copy-done), custom_call_target="tpu_custom_call" | custom-call | flops 1879048192 | bytes 6291456 | tf_op jit(solution)/shard_map/project/pallas_call | solution.py:181
  55.0 2.8 %collective-permute-start.18 = (bf16[256,1024]{1,0:T(8,128)(2,1)S(1)}, bf16[256,1024]{1,0:T(8,128)(2,1)S(1)}, u32[]{:S(2)}, u32[]{:S(2)}) collective-permute-start(bf16[256,1024]{1,0:T(8,128)(2,1)S(1)} %broadcast_select_fusion.2), channel_id=1, source_target_pairs={{0,8},{1,9},{2,10},{3,11},{4,12},{5,13},{6,14},{7,15},{8,0},{9,1},... | collective-permute-start | bytes 1572872 | tf_op jit(solution)/shard_map/ppermute | solution.py:45
  59.8 2.3 %project.5.refs_7_ = bf16[8,256,512]{2,1,0:T(8,128)(2,1)S(1)} custom-call(bf16[8,256,896]{2,1,0:T(8,128)(2,1)S(1)} %copy-done.2, bf16[2,896,1024]{2,1,0:T(8,128)(2,1)S(1)} %copy-done), custom_call_target="tpu_custom_call" | custom-call | flops 1879048192 | bytes 6291456 | tf_op jit(solution)/shard_map/project/pallas_call | solution.py:181
  63.8 3.4 %collective-permute-done.20.refs_1_ = bf16[256,1024]{1,0:T(8,128)(2,1)S(1)} collective-permute-done((bf16[256,1024]{1,0:T(8,128)(2,1)S(1)}, bf16[256,1024]{1,0:T(8,128)(2,1)S(1)}, u32[]{:S(2)}, u32[]{:S(2)}) %collective-permute-start.20) | collective-permute-done | bytes 524320 | tf_op jit(solution)/shard_map/ppermute | solution.py:45
  67.2 3.0 %collective-permute-start.23 = (bf16[256,1024]{1,0:T(8,128)(2,1)S(1)}, bf16[256,1024]{1,0:T(8,128)(2,1)S(1)}, u32[]{:S(2)}, u32[]{:S(2)}) collective-permute-start(bf16[256,1024]{1,0:T(8,128)(2,1)S(1)} %broadcast_select_fusion), channel_id=1, source_target_pairs={{0,48},{1,49},{2,50},{3,51},{4,52},{5,53},{6,54},{7,55},{8,56},{9,... | collective-permute-start | bytes 1572872 | tf_op jit(solution)/shard_map/ppermute | solution.py:45
  70.4 2.0 %collective-permute-start.19 = (bf16[256,1024]{1,0:T(8,128)(2,1)S(1)}, bf16[256,1024]{1,0:T(8,128)(2,1)S(1)}, u32[]{:S(2)}, u32[]{:S(2)}) collective-permute-start(bf16[256,1024]{1,0:T(8,128)(2,1)S(1)} %collective-permute-done.18.refs_0_), channel_id=1, source_target_pairs={{0,16},{1,17},{2,18},{3,19},{4,20},{5,21},{6,22},{7,23},{8,24},{9,... | collective-permute-start | bytes 1572872 | tf_op jit(solution)/shard_map/ppermute | solution.py:45
  72.4 2.7 %rows.1.n_ref = bf16[512,4096]{1,0:T(8,128)(2,1)S(1)} custom-call(bf16[128,4096]{1,0:T(8,128)(2,1)S(1)} %norm.1.own_ref, bf16[128,4096]{1,0:T(8,128)(2,1)S(1)} %collective-permute-done.10.near_ref, bf16[128,4096]{1,0:T(8,128)(2,1)} %collective-permute-done.11.far_ref, bf16[128,4096]{1,0:T(8,128)(2,1)S(1)} %collective-permute-done.17.far_near_ref), custom_call_target="tpu_custom_call" | custom-call | bytes 8388608 | tf_op jit(solution)/shard_map/rows/pallas_call | solution.py:159
  78.5 4.1 %collective-permute-done.21.refs_5_ = bf16[256,1024]{1,0:T(8,128)(2,1)S(1)} collective-permute-done((bf16[256,1024]{1,0:T(8,128)(2,1)S(1)}, bf16[256,1024]{1,0:T(8,128)(2,1)S(1)}, u32[]{:S(2)}, u32[]{:S(2)}) %collective-permute-start.21) | collective-permute-done | bytes 524320 | tf_op jit(solution)/shard_map/ppermute | solution.py:45
  82.6 3.8 %collective-permute-start.26 = (bf16[128,1024]{1,0:T(8,128)(2,1)S(1)}, bf16[128,1024]{1,0:T(8,128)(2,1)S(1)}, u32[]{:S(2)}, u32[]{:S(2)}) collective-permute-start(bf16[128,1024]{1,0:T(8,128)(2,1)S(1)} %slice.11), channel_id=1, source_target_pairs={{0,48},{1,49},{2,50},{3,51},{4,52},{5,53},{6,54},{7,55},{8,56},{9,... | collective-permute-start | bytes 786440 | tf_op jit(solution)/shard_map/ppermute | solution.py:45
  88.3 2.0 %collective-permute-done.26.refs_2_ = bf16[128,1024]{1,0:T(8,128)(2,1)S(1)} collective-permute-done((bf16[128,1024]{1,0:T(8,128)(2,1)S(1)}, bf16[128,1024]{1,0:T(8,128)(2,1)S(1)}, u32[]{:S(2)}, u32[]{:S(2)}) %collective-permute-start.26) | collective-permute-done | bytes 262176 | tf_op jit(solution)/shard_map/ppermute | solution.py:45
  90.2 3.8 %collective-permute-done.25.refs_1_ = bf16[128,1024]{1,0:T(8,128)(2,1)S(1)} collective-permute-done((bf16[128,1024]{1,0:T(8,128)(2,1)S(1)}, bf16[128,1024]{1,0:T(8,128)(2,1)S(1)}, u32[]{:S(2)}, u32[]{:S(2)}) %collective-permute-start.25) | collective-permute-done | bytes 262176 | tf_op jit(solution)/shard_map/ppermute | solution.py:45
  94.1 5.8 %attend.1 = bf16[512,1024]{1,0:T(8,128)(2,1)} custom-call(s32[2,512]{1,0:T(2,128)S(1)} %bitcast.7, s32[256,128]{1,0:T(8,128)S(1)} %bitcast.6, f32[512,1024]{1,0:T(8,128)S(1)} %partial.5.total_ref, bf16[512,4096]{1,0:T(8,128)(2,1)S(1)} %rows.1.n_ref, bf16[256,1024]{1,0:T(8,128)(2,1)S(1)} %collective-permute-done.24.refs_0_, ...), custom_call_target="tpu_custom_call" | custom-call | flops 6291456000 | bytes 16777216 | tf_op jit(solution)/shard_map/attend/pallas_call | solution.py:320
  (69 shorter events, 26.3 us)
Async XLA Ops:
  0.0 13.5 %collective-permute-start = (bf16[64,1024]{1,0:T(8,128)(2,1)}, bf16[64,1024]{1,0:T(8,128)(2,1)S(1)}, u32[]{:S(2)}, u32[]{:S(2)}) collective-permute-start(bf16[64,1024]{1,0:T(8,128)(2,1)} %refs_0_.1), channel_id=1, source_target_pairs={{0,1},{1,2},{2,3},{3,4},{4,5},{5,6},{6,7},{7,0},{8,9},{9,10},{10,1... | collective-permute-start | bytes 393224 | tf_op jit(solution)/shard_map/ppermute | solution.py:45
  1.9 11.6 %collective-permute-start.2 = (bf16[64,1024]{1,0:T(8,128)(2,1)}, bf16[64,1024]{1,0:T(8,128)(2,1)S(1)}, u32[]{:S(2)}, u32[]{:S(2)}) collective-permute-start(bf16[64,1024]{1,0:T(8,128)(2,1)} %refs_0_.1), channel_id=1, source_target_pairs={{0,2},{1,3},{2,4},{3,5},{4,6},{5,7},{6,0},{7,1},{8,10},{9,11},{10,... | collective-permute-start | bytes 393224 | tf_op jit(solution)/shard_map/ppermute | solution.py:45
  5.2 8.4 %collective-permute-start.3 = (bf16[64,1024]{1,0:T(8,128)(2,1)}, bf16[64,1024]{1,0:T(8,128)(2,1)S(1)}, u32[]{:S(2)}, u32[]{:S(2)}) collective-permute-start(bf16[64,1024]{1,0:T(8,128)(2,1)} %refs_0_.1), channel_id=1, source_target_pairs={{0,6},{1,7},{2,0},{3,1},{4,2},{5,3},{6,4},{7,5},{8,14},{9,15},{10,... | collective-permute-start | bytes 393224 | tf_op jit(solution)/shard_map/ppermute | solution.py:45
  11.3 43.4 %collective-permute-start.11 = (bf16[128,4096]{1,0:T(8,128)(2,1)S(1)}, bf16[128,4096]{1,0:T(8,128)(2,1)}, u32[]{:S(2)}, u32[]{:S(2)}) collective-permute-start(bf16[128,4096]{1,0:T(8,128)(2,1)S(1)} %norm.1.own_ref), channel_id=1, source_target_pairs={{0,128},{128,0},{1,129},{129,1},{2,130},{130,2},{3,131},{131,3},{4... | collective-permute-start | bytes 3145736 | tf_op jit(solution)/shard_map/ppermute | solution.py:49
  14.4 23.0 %collective-permute-start.5 = (bf16[256,1024]{1,0:T(8,128)(2,1)S(1)}, bf16[256,1024]{1,0:T(8,128)(2,1)S(1)}, u32[]{:S(2)}, u32[]{:S(2)}) collective-permute-start(bf16[256,1024]{1,0:T(8,128)(2,1)S(1)} %stack.2.refs_0_), channel_id=1, source_target_pairs={{0,16},{1,17},{2,18},{3,19},{4,20},{5,21},{6,22},{7,23},{8,24},{9,... | collective-permute-start | bytes 1572872 | tf_op jit(solution)/shard_map/ppermute | solution.py:45
  18.3 9.2 %collective-permute-start.13 = (bf16[64,1024]{1,0:T(8,128)(2,1)S(1)}, bf16[64,1024]{1,0:T(8,128)(2,1)S(1)}, u32[]{:S(2)}, u32[]{:S(2)}) collective-permute-start(bf16[64,1024]{1,0:T(8,128)(2,1)S(1)} %get-tuple-element.35.refs_0_), channel_id=1, source_target_pairs={{0,6},{1,7},{2,0},{3,1},{4,2},{5,3},{6,4},{7,5},{8,14},{9,15},{10,... | collective-permute-start | bytes 393224 | tf_op jit(solution)/shard_map/ppermute | solution.py:45
  22.5 17.4 %collective-permute-start.7 = (bf16[256,1024]{1,0:T(8,128)(2,1)S(1)}, bf16[256,1024]{1,0:T(8,128)(2,1)S(1)}, u32[]{:S(2)}, u32[]{:S(2)}) collective-permute-start(bf16[256,1024]{1,0:T(8,128)(2,1)S(1)} %stack.2.refs_0_), channel_id=1, source_target_pairs={{0,48},{1,49},{2,50},{3,51},{4,52},{5,53},{6,54},{7,55},{8,56},{9,... | collective-permute-start | bytes 1572872 | tf_op jit(solution)/shard_map/ppermute | solution.py:45
  27.6 24.2 %collective-permute-start.15 = (bf16[256,1024]{1,0:T(8,128)(2,1)S(1)}, bf16[256,1024]{1,0:T(8,128)(2,1)S(1)}, u32[]{:S(2)}, u32[]{:S(2)}) collective-permute-start(bf16[256,1024]{1,0:T(8,128)(2,1)S(1)} %stack.3.refs_0_), channel_id=1, source_target_pairs={{0,16},{1,17},{2,18},{3,19},{4,20},{5,21},{6,22},{7,23},{8,24},{9,... | collective-permute-start | bytes 1572872 | tf_op jit(solution)/shard_map/ppermute | solution.py:45
  29.3 22.6 %collective-permute-start.16 = (bf16[256,1024]{1,0:T(8,128)(2,1)S(1)}, bf16[256,1024]{1,0:T(8,128)(2,1)S(1)}, u32[]{:S(2)}, u32[]{:S(2)}) collective-permute-start(bf16[256,1024]{1,0:T(8,128)(2,1)S(1)} %stack.3.refs_0_), channel_id=1, source_target_pairs={{0,48},{1,49},{2,50},{3,51},{4,52},{5,53},{6,54},{7,55},{8,56},{9,... | collective-permute-start | bytes 1572872 | tf_op jit(solution)/shard_map/ppermute | solution.py:45
  37.4 11.5 %collective-permute-start.4 = (bf16[128,896]{1,0:T(8,128)(2,1)S(1)}, bf16[128,896]{1,0:T(8,128)(2,1)S(1)}, u32[]{:S(2)}, u32[]{:S(2)}) collective-permute-start(bf16[128,896]{1,0:T(8,128)(2,1)S(1)} %dynamic-slice_bitcast_fusion), channel_id=1, source_target_pairs={{0,1},{1,2},{2,3},{3,4},{4,5},{5,6},{6,7},{7,8},{8,9},{9,10},{10,1... | collective-permute-start | bytes 688136 | tf_op jit(solution)/shard_map/ppermute | solution.py:387
  39.9 15.1 %collective-permute-start.6 = (bf16[256,1024]{1,0:T(8,128)(2,1)S(1)}, bf16[256,1024]{1,0:T(8,128)(2,1)S(1)}, u32[]{:S(2)}, u32[]{:S(2)}) collective-permute-start(bf16[256,1024]{1,0:T(8,128)(2,1)S(1)} %broadcast_select_fusion.3), channel_id=1, source_target_pairs={{0,8},{1,9},{2,10},{3,11},{4,12},{5,13},{6,14},{7,15},{8,0},{9,1},... | collective-permute-start | bytes 1572872 | tf_op jit(solution)/shard_map/ppermute | solution.py:45
  48.8 9.2 %collective-permute-start.8 = (bf16[256,1024]{1,0:T(8,128)(2,1)S(1)}, bf16[256,1024]{1,0:T(8,128)(2,1)S(1)}, u32[]{:S(2)}, u32[]{:S(2)}) collective-permute-start(bf16[256,1024]{1,0:T(8,128)(2,1)S(1)} %collective-permute-done.7.refs_2_), channel_id=1, source_target_pairs={{0,48},{1,49},{2,50},{3,51},{4,52},{5,53},{6,54},{7,55},{8,56},{9,... | collective-permute-start | bytes 1572872 | tf_op jit(solution)/shard_map/ppermute | solution.py:45
  51.8 18.6 %collective-permute-start.10 = (bf16[128,4096]{1,0:T(8,128)(2,1)S(1)}, bf16[128,4096]{1,0:T(8,128)(2,1)S(1)}, u32[]{:S(2)}, u32[]{:S(2)}) collective-permute-start(bf16[128,4096]{1,0:T(8,128)(2,1)S(1)} %norm.1.own_ref), channel_id=1, source_target_pairs={{0,64},{64,0},{1,65},{65,1},{2,66},{66,2},{3,67},{67,3},{4,68},{68... | collective-permute-start | bytes 3145736 | tf_op jit(solution)/shard_map/ppermute | solution.py:49
  51.9 10.3 %collective-permute-start.9 = (bf16[128,896]{1,0:T(8,128)(2,1)S(1)}, bf16[128,896]{1,0:T(8,128)(2,1)S(1)}, u32[]{:S(2)}, u32[]{:S(2)}) collective-permute-start(bf16[128,896]{1,0:T(8,128)(2,1)S(1)} %collective-permute-done.4.mine_ref), channel_id=1, source_target_pairs={{0,64},{64,0},{1,65},{65,1},{2,66},{66,2},{3,67},{67,3},{4,68},{68... | collective-permute-start | bytes 688136 | tf_op jit(solution)/shard_map/ppermute | solution.py:49
  54.7 17.7 %collective-permute-start.17 = (bf16[128,4096]{1,0:T(8,128)(2,1)}, bf16[128,4096]{1,0:T(8,128)(2,1)S(1)}, u32[]{:S(2)}, u32[]{:S(2)}) collective-permute-start(bf16[128,4096]{1,0:T(8,128)(2,1)} %collective-permute-done.11.far_ref), channel_id=1, source_target_pairs={{0,64},{64,0},{1,65},{65,1},{2,66},{66,2},{3,67},{67,3},{4,68},{68... | collective-permute-start | bytes 3145736 | tf_op jit(solution)/shard_map/ppermute | solution.py:49
  55.0 15.2 %collective-permute-start.18 = (bf16[256,1024]{1,0:T(8,128)(2,1)S(1)}, bf16[256,1024]{1,0:T(8,128)(2,1)S(1)}, u32[]{:S(2)}, u32[]{:S(2)}) collective-permute-start(bf16[256,1024]{1,0:T(8,128)(2,1)S(1)} %broadcast_select_fusion.2), channel_id=1, source_target_pairs={{0,8},{1,9},{2,10},{3,11},{4,12},{5,13},{6,14},{7,15},{8,0},{9,1},... | collective-permute-start | bytes 1572872 | tf_op jit(solution)/shard_map/ppermute | solution.py:45
  58.0 9.2 %collective-permute-start.20 = (bf16[256,1024]{1,0:T(8,128)(2,1)S(1)}, bf16[256,1024]{1,0:T(8,128)(2,1)S(1)}, u32[]{:S(2)}, u32[]{:S(2)}) collective-permute-start(bf16[256,1024]{1,0:T(8,128)(2,1)S(1)} %collective-permute-done.16.refs_2_), channel_id=1, source_target_pairs={{0,48},{1,49},{2,50},{3,51},{4,52},{5,53},{6,54},{7,55},{8,56},{9,... | collective-permute-start | bytes 1572872 | tf_op jit(solution)/shard_map/ppermute | solution.py:45
  62.2 13.9 %collective-permute-start.22 = (bf16[256,1024]{1,0:T(8,128)(2,1)S(1)}, bf16[256,1024]{1,0:T(8,128)(2,1)S(1)}, u32[]{:S(2)}, u32[]{:S(2)}) collective-permute-start(bf16[256,1024]{1,0:T(8,128)(2,1)S(1)} %collective-permute-done.6.refs_3_), channel_id=1, source_target_pairs={{0,16},{1,17},{2,18},{3,19},{4,20},{5,21},{6,22},{7,23},{8,24},{9,... | collective-permute-start | bytes 1572872 | tf_op jit(solution)/shard_map/ppermute | solution.py:45
  67.2 9.7 %collective-permute-start.23 = (bf16[256,1024]{1,0:T(8,128)(2,1)S(1)}, bf16[256,1024]{1,0:T(8,128)(2,1)S(1)}, u32[]{:S(2)}, u32[]{:S(2)}) collective-permute-start(bf16[256,1024]{1,0:T(8,128)(2,1)S(1)} %broadcast_select_fusion), channel_id=1, source_target_pairs={{0,48},{1,49},{2,50},{3,51},{4,52},{5,53},{6,54},{7,55},{8,56},{9,... | collective-permute-start | bytes 1572872 | tf_op jit(solution)/shard_map/ppermute | solution.py:45
  70.3 12.3 %collective-permute-start.21 = (bf16[256,1024]{1,0:T(8,128)(2,1)S(1)}, bf16[256,1024]{1,0:T(8,128)(2,1)S(1)}, u32[]{:S(2)}, u32[]{:S(2)}) collective-permute-start(bf16[256,1024]{1,0:T(8,128)(2,1)S(1)} %broadcast_select_fusion.1), channel_id=1, source_target_pairs={{0,48},{1,49},{2,50},{3,51},{4,52},{5,53},{6,54},{7,55},{8,56},{9,... | collective-permute-start | bytes 1572872 | tf_op jit(solution)/shard_map/ppermute | solution.py:45
  70.4 15.9 %collective-permute-start.19 = (bf16[256,1024]{1,0:T(8,128)(2,1)S(1)}, bf16[256,1024]{1,0:T(8,128)(2,1)S(1)}, u32[]{:S(2)}, u32[]{:S(2)}) collective-permute-start(bf16[256,1024]{1,0:T(8,128)(2,1)S(1)} %collective-permute-done.18.refs_0_), channel_id=1, source_target_pairs={{0,16},{1,17},{2,18},{3,19},{4,20},{5,21},{6,22},{7,23},{8,24},{9,... | collective-permute-start | bytes 1572872 | tf_op jit(solution)/shard_map/ppermute | solution.py:45
  76.1 17.9 %collective-permute-start.24 = (bf16[256,1024]{1,0:T(8,128)(2,1)S(1)}, bf16[256,1024]{1,0:T(8,128)(2,1)S(1)}, u32[]{:S(2)}, u32[]{:S(2)}) collective-permute-start(bf16[256,1024]{1,0:T(8,128)(2,1)S(1)} %collective-permute-done.22.refs_2_), channel_id=1, source_target_pairs={{0,16},{1,17},{2,18},{3,19},{4,20},{5,21},{6,22},{7,23},{8,24},{9,... | collective-permute-start | bytes 1572872 | tf_op jit(solution)/shard_map/ppermute | solution.py:45
  82.6 7.7 %collective-permute-start.26 = (bf16[128,1024]{1,0:T(8,128)(2,1)S(1)}, bf16[128,1024]{1,0:T(8,128)(2,1)S(1)}, u32[]{:S(2)}, u32[]{:S(2)}) collective-permute-start(bf16[128,1024]{1,0:T(8,128)(2,1)S(1)} %slice.11), channel_id=1, source_target_pairs={{0,48},{1,49},{2,50},{3,51},{4,52},{5,53},{6,54},{7,55},{8,56},{9,... | collective-permute-start | bytes 786440 | tf_op jit(solution)/shard_map/ppermute | solution.py:45
  86.4 7.7 %collective-permute-start.25 = (bf16[128,1024]{1,0:T(8,128)(2,1)S(1)}, bf16[128,1024]{1,0:T(8,128)(2,1)S(1)}, u32[]{:S(2)}, u32[]{:S(2)}) collective-permute-start(bf16[128,1024]{1,0:T(8,128)(2,1)S(1)} %slice.10), channel_id=1, source_target_pairs={{0,16},{1,17},{2,18},{3,19},{4,20},{5,21},{6,22},{7,23},{8,24},{9,... | collective-permute-start | bytes 786440 | tf_op jit(solution)/shard_map/ppermute | solution.py:45
  (12 other events, 66.8 us)
